TPU v7x, 32 devices: a whole 2x2x4 slice. The times are simulated.
32 devices in a mesh: grp: 2 (over x), dev: 16 (over z, y, core).
Axes of the slice: x: 2, y: 2, z: 4, core: 2. Of those that a mesh axis runs over, the one named last changes fastest.
Arguments:
- populations: float32 [19, 128, 64, 256], P(None, 'dev', 'grp'), may hold values from 0 to 0.5, as said below
- heat_pops: float32 [7, 128, 64, 256], P(None, 'dev', 'grp'), may hold values from 0 to 0.75, as said below
- solid_temp: float32 [128, 64, 256], P('dev', 'grp'), may hold values from 0.2 to 2
- conductivity: float32 [128, 64, 256], P('dev', 'grp'), may hold values from 1 to 10
- pore_mask: int32 [128, 64, 256], P('dev', 'grp'), may hold values 0 or 1
Outputs:
- new_pops: float32 [19, 128, 64, 256], P(None, 'dev', 'grp')
- new_heat: float32 [7, 128, 64, 256], P(None, 'dev', 'grp')
- new_solid: float32 [128, 64, 256], P('dev', 'grp')
Inputs may be any that keep to these rules, and one draw needn't show every extreme that they name: `populations`: each flow population is its lattice weight times a factor of order one, so the density is positive. `heat_pops`: each thermal population is its lattice weight times a positive factor.
All inputs are finite; a program needn't handle non-finite values. No bound on the sum of `pore_mask` on one device may be relied on, other than what follows from the above.
Results may differ from a plain program's by a relative error of at most 0.00002.
Values sent between devices are 32-bit elements; how exact they have to be, the bound alone decides.
No kernel may reach another device: no remote copies, remote signals or barrier semaphores. Data moves between devices by JAX's collectives and lax.ppermute only.
A program may use at most 128 MiB of HBM per device.

v0:
```python
import jax
import jax.numpy as jnp
import numpy as np
from jax import lax
from jax.sharding import PartitionSpec as P

ITERS = 4


flow_dirs = np.array(
    [
        [0, 0, 0],
        [1, 0, 0],
        [-1, 0, 0],
        [0, 1, 0],
        [0, -1, 0],
        [0, 0, 1],
        [0, 0, -1],
        [1, 1, 0],
        [-1, -1, 0],
        [1, -1, 0],
        [-1, 1, 0],
        [1, 0, 1],
        [-1, 0, -1],
        [1, 0, -1],
        [-1, 0, 1],
        [0, 1, 1],
        [0, -1, -1],
        [0, 1, -1],
        [0, -1, 1],
    ]
)
flow_weights = [1.0 / 3.0] + [1.0 / 18.0] * 6 + [1.0 / 36.0] * 12
flow_opposite = [0, 2, 1, 4, 3, 6, 5, 8, 7, 10, 9, 12, 11, 14, 13, 16, 15, 18, 17]
heat_weights = [0.25] + [0.125] * 6
relax_flow = 0.8
relax_heat = 0.7
jump_ratio = 0.3
film_coeff = 0.5
cheb_theta = 61.0
cheb_delta = 60.0


def with_halo(block, sides, width):
    for axis, dim in sides:
        count = lax.axis_size(axis)
        forward = [(i, i + 1) for i in range(count - 1)]
        forward.append((count - 1, 0))
        backward = [(target, source) for source, target in forward]
        low = lax.ppermute(
            lax.slice_in_dim(block, block.shape[dim] - width, None, axis=dim), axis, forward
        )
        high = lax.ppermute(lax.slice_in_dim(block, 0, width, axis=dim), axis, backward)
        block = jnp.concatenate([low, block, high], axis=dim)
    return block


def shifted(padded, width, index, core_x, core_z):
    dirc = flow_dirs[index]
    rank_all = padded.ndim
    piece = lax.slice_in_dim(
        padded, width - int(dirc[0]), width - int(dirc[0]) + core_x, axis=rank_all - 3
    )
    piece = lax.slice_in_dim(
        piece, width - int(dirc[2]), width - int(dirc[2]) + core_z, axis=rank_all - 2
    )
    return jnp.roll(piece, int(dirc[1]), axis=rank_all - 1)


def chebyshev(start, source, operate):
    sigma = cheb_theta / cheb_delta
    iterate = start
    resid = source - operate(iterate)
    ratio = 1.0 / sigma
    step = resid / cheb_theta
    for sweep in range(ITERS):
        iterate = iterate + step
        if sweep + 1 < ITERS:
            resid = resid - operate(step)
            ratio_next = 1.0 / (2.0 * sigma - ratio)
            step = ratio_next * ratio * step + 2.0 * ratio_next / cheb_delta * resid
            ratio = ratio_next
    return iterate


def per_device(populations, heat_pops, solid_temp, conductivity, pore_mask):
    core_x, core_z, core_y = solid_temp.shape
    pore = pore_mask.astype(jnp.float32)
    solid = 1.0 - pore
    density = jnp.sum(populations, axis=0)
    vel = [
        jnp.sum(
            populations * jnp.asarray(flow_dirs[:, a], jnp.float32)[:, None, None, None], axis=0
        )
        / density
        for a in range(3)
    ]
    fluid_temp = jnp.sum(heat_pops, axis=0)
    usq = vel[0] * vel[0] + vel[1] * vel[1] + vel[2] * vel[2]
    flow_star = []
    heat_star = []
    for index in range(19):
        dirc = flow_dirs[index]
        cdot = float(dirc[0]) * vel[0] + float(dirc[1]) * vel[1] + float(dirc[2]) * vel[2]
        equil = flow_weights[index] * density * (1.0 + 3.0 * cdot + 4.5 * cdot * cdot - 1.5 * usq)
        flow_star.append(populations[index] - (populations[index] - equil) / relax_flow)
        if index < 7:
            hequil = heat_weights[index] * fluid_temp * (1.0 + 4.0 * cdot)
            heat_star.append(heat_pops[index] - (heat_pops[index] - hequil) / relax_heat)
    fields = flow_star + heat_star + [solid_temp, pore]
    padded = with_halo(jnp.stack(fields, axis=0), (("dev", 1), ("grp", 2)), 1)
    views = [padded[slot] for slot in range(28)]
    new_flow = []
    new_hot = []
    for index in range(19):
        near_pore = shifted(views[27], 1, index, core_x, core_z)
        moved = (
            near_pore * shifted(views[index], 1, index, core_x, core_z)
            + (1.0 - near_pore) * flow_star[flow_opposite[index]]
        )
        new_flow.append(pore * moved + solid * populations[index])
        if index < 7:
            near_solid = shifted(views[26], 1, index, core_x, core_z)
            wall_temp = near_solid + jump_ratio * (fluid_temp - near_solid)
            hmoved = near_pore * shifted(views[19 + index], 1, index, core_x, core_z) + (
                1.0 - near_pore
            ) * (-heat_star[flow_opposite[index]] + 2.0 * heat_weights[index] * wall_temp)
            new_hot.append(pore * hmoved + solid * heat_pops[index])
    new_pops = jnp.stack(new_flow, axis=0)
    new_heat = jnp.stack(new_hot, axis=0)
    temp_new = pore * jnp.sum(new_heat, axis=0)
    temp_pad = with_halo(temp_new, (("dev", 0), ("grp", 1)), 1)
    inflow = jnp.zeros_like(solid_temp)
    for index in range(1, 7):
        inflow = inflow + shifted(views[27], 1, index, core_x, core_z) * film_coeff * (
            shifted(temp_pad, 1, index, core_x, core_z) - solid_temp
        )
    source = solid_temp + solid * inflow
    coef_pad = with_halo(jnp.stack([conductivity, solid], axis=0), (("dev", 1), ("grp", 2)), 1)
    faces = []
    for index in range(1, 7):
        knear = shifted(coef_pad[0], 1, index, core_x, core_z)
        faces.append(
            solid
            * shifted(coef_pad[1], 1, index, core_x, core_z)
            * 2.0
            * conductivity
            * knear
            / (conductivity + knear)
        )

    def operate(field):
        field_pad = with_halo(field, (("dev", 0), ("grp", 1)), 1)
        total = field
        for index in range(1, 7):
            total = total + faces[index - 1] * (
                field - shifted(field_pad, 1, index, core_x, core_z)
            )
        return total

    iterate = chebyshev(solid_temp, source, operate)
    new_solid = solid * iterate + pore * solid_temp
    return (new_pops, new_heat, new_solid)


def solution(mesh):
    in_specs = (
        P(None, "dev", "grp", None),
        P(None, "dev", "grp", None),
        P("dev", "grp", None),
        P("dev", "grp", None),
        P("dev", "grp", None),
    )
    out_specs = (P(None, "dev", "grp", None), P(None, "dev", "grp", None), P("dev", "grp", None))
    return jax.shard_map(
        per_device, mesh=mesh, in_specs=in_specs, out_specs=out_specs, check_vma=False
    )
```

profile of v0, /device:TPU:0, one launch (start us, length us, event | category | flops | bytes accessed | tf_op | source)
XLA Modules:
  0.0 152.4 jit_solution(3331372486005497726)
XLA Ops:
  0.6 4.0 %multiply_reduce_fusion.2 = (f32[8,32,256]{2,1,0:T(8,128)S(1)}, f32[8,32,256]{2,1,0:T(8,128)S(1)}, f32[8,32,256]{2,1,0:T(8,128)S(1)}, f32[8,32,256]{2,1,0:T(8,128)S(1)}) fusion(f32[19,8,32,256]{3,2,1,0:T(8,128)} %param.8, f32[19]{0:T(128)} %constant.83.clone, f32[19]{0:T(128)} %constant.85.clone, f32[19]{0:T(128)} %constant.84.clone), kind=kLoop, calls=%fused_computation.2 | loop fusion | flops 8454144 | bytes 6029540 | tf_op jit(solution)/shard_map/reduce_sum | solution.py:92
  21.6 1.8 %fusion.528 = f32[28,8,32,256]{3,2,1,0:T(8,128)} fusion(f32[28,8,32,256]{3,2,1,0:T(8,128)} %fusion.552, f32[7,8,32,256]{3,2,1,0:T(8,128)S(1)} %copy-done.2, f32[8,32,256]{2,1,0:T(8,128)S(1)} %reduce_sum.71, f32[1,8,32,256]{3,2,1,0:T(8,128)} %copy-done.5, f32[8,32,256]{2,1,0:T(8,128)S(1)} %get-tuple-element.47), kind=kLoop, calls=%fused_computation.761 | loop fusion | flops 589824 | bytes 1310720
  23.4 1.7 %fusion.532 = f32[28,8,32,256]{3,2,1,0:T(8,128)} fusion(f32[28,8,32,256]{3,2,1,0:T(8,128)} %fusion.528, f32[7,8,32,256]{3,2,1,0:T(8,128)S(1)} %copy-done.2, f32[8,32,256]{2,1,0:T(8,128)S(1)} %reduce_sum.71, f32[1,8,32,256]{3,2,1,0:T(8,128)} %copy-done.6, f32[8,32,256]{2,1,0:T(8,128)S(1)} %get-tuple-element.47), kind=kLoop, calls=%fused_computation.765 | loop fusion | flops 589824 | bytes 1310720
  25.1 1.8 %fusion.536 = f32[28,8,32,256]{3,2,1,0:T(8,128)} fusion(f32[28,8,32,256]{3,2,1,0:T(8,128)} %fusion.532, f32[7,8,32,256]{3,2,1,0:T(8,128)S(1)} %copy-done.2, f32[8,32,256]{2,1,0:T(8,128)S(1)} %reduce_sum.71, f32[1,8,32,256]{3,2,1,0:T(8,128)} %copy-done.7, f32[8,32,256]{2,1,0:T(8,128)S(1)} %get-tuple-element.47), kind=kLoop, calls=%fused_computation.769 | loop fusion | flops 589824 | bytes 1310720
  30.8 1.6 %fusion.589 = (f32[28,1,32,256]{3,2,1,0:T(8,128)S(1)}, f32[28,1,32,256]{3,2,1,0:T(8,128)S(1)}) fusion(f32[28,8,32,256]{3,2,1,0:T(8,128)} %bitcast_dynamic-update-slice_fusion.7), kind=kLoop, calls=%fused_computation.863 | loop fusion | bytes 3670016 | tf_op jit(solution)/shard_map/slice | solution.py:51
  32.9 5.1 %collective-permute-start.1 = (f32[28,1,32,256]{3,2,1,0:T(8,128)S(1)}, f32[28,1,32,256]{3,2,1,0:T(8,128)S(1)}, u32[]{:S(2)}, u32[]{:S(2)}) collective-permute-start(f32[28,1,32,256]{3,2,1,0:T(8,128)S(1)} %get-tuple-element.83), channel_id=1, source_target_pairs={{1,0},{2,1},{3,2},{4,3},{5,4},{6,5},{7,6},{8,7},{9,8},{10,9},{11,1... | collective-permute-start | bytes 2752520 | tf_op jit(solution)/shard_map/ppermute | solution.py:53
  38.1 4.4 %collective-permute-start.9 = (f32[2,1,32,256]{3,2,1,0:T(8,128)S(1)}, f32[2,1,32,256]{3,2,1,0:T(8,128)S(1)}, u32[]{:S(2)}, u32[]{:S(2)}) collective-permute-start(f32[2,1,32,256]{3,2,1,0:T(8,128)S(1)} %get-tuple-element.93), channel_id=1, source_target_pairs={{1,0},{2,1},{3,2},{4,3},{5,4},{6,5},{7,6},{8,7},{9,8},{10,9},{11,1... | collective-permute-start | bytes 196616 | tf_op jit(solution)/shard_map/ppermute | solution.py:53
  42.8 7.4 %collective-permute-done.12 = f32[1,32,256]{2,1,0:T(8,128)S(1)} collective-permute-done((f32[1,32,256]{2,1,0:T(8,128)S(1)}, f32[1,32,256]{2,1,0:T(8,128)S(1)}, u32[]{:S(2)}, u32[]{:S(2)}) %collective-permute-start.12) | collective-permute-done | bytes 32800 | tf_op jit(solution)/shard_map/ppermute | solution.py:50
  50.2 8.3 %collective-permute-done.13 = f32[1,32,256]{2,1,0:T(8,128)S(1)} collective-permute-done((f32[1,32,256]{2,1,0:T(8,128)S(1)}, f32[1,32,256]{2,1,0:T(8,128)S(1)}, u32[]{:S(2)}, u32[]{:S(2)}) %collective-permute-start.13) | collective-permute-done | bytes 32800 | tf_op jit(solution)/shard_map/ppermute | solution.py:53
  58.6 1.6 %collective-permute-start.10 = (f32[2,10,1,256]{3,2,1,0:T(1,128)S(1)}, f32[2,10,1,256]{3,2,1,0:T(1,128)S(1)}, u32[]{:S(2)}, u32[]{:S(2)}) collective-permute-start(f32[2,10,1,256]{3,2,1,0:T(1,128)S(1)} %get-tuple-element.90), channel_id=1, source_target_pairs={{0,16},{16,0},{1,17},{17,1},{2,18},{18,2},{3,19},{19,3},{4,20},{20... | collective-permute-start | bytes 61448 | tf_op jit(solution)/shard_map/ppermute | solution.py:50
  60.7 1.6 %collective-permute-start.14 = (f32[10,1,256]{2,1,0:T(1,128)S(1)}, f32[10,1,256]{2,1,0:T(1,128)S(1)}, u32[]{:S(2)}, u32[]{:S(2)}) collective-permute-start(f32[10,1,256]{2,1,0:T(1,128)S(1)} %get-tuple-element.110), channel_id=1, source_target_pairs={{0,16},{16,0},{1,17},{17,1},{2,18},{18,2},{3,19},{19,3},{4,20},{20... | collective-permute-start | bytes 30728 | tf_op jit(solution)/shard_map/ppermute | solution.py:50
  62.4 1.5 collective-permute-start.15
  64.2 2.5 %pad_maximum_fusion.7 = (f32[28,10,1,256]{3,2,1,0:T(1,128)S(1)}, f32[28,10,1,256]{3,2,1,0:T(1,128)S(1)}) fusion(f32[28,1,32,256]{3,2,1,0:T(8,128)S(1)} %collective-permute-done.1, f32[28,8,32,256]{3,2,1,0:T(8,128)} %bitcast_dynamic-update-slice_fusion.7, f32[28,1,32,256]{3,2,1,0:T(8,128)S(1)} %collective-permute-done), kind=kLoop, calls=%fused_computation.86 | loop fusion | flops 286720 | bytes 9748480 | tf_op jit(solution)/shard_map/slice | solution.py:51
  67.3 1.5 collective-permute-start.3
  69.2 5.9 %collective-permute-done.2 = f32[28,10,1,256]{3,2,1,0:T(1,128)S(1)} collective-permute-done((f32[28,10,1,256]{3,2,1,0:T(1,128)S(1)}, f32[28,10,1,256]{3,2,1,0:T(1,128)S(1)}, u32[]{:S(2)}, u32[]{:S(2)}) %collective-permute-start.2) | collective-permute-done | bytes 286752 | tf_op jit(solution)/shard_map/ppermute | solution.py:50
  75.1 6.1 %collective-permute-done.3 = f32[28,10,1,256]{3,2,1,0:T(1,128)S(1)} collective-permute-done((f32[28,10,1,256]{3,2,1,0:T(1,128)S(1)}, f32[28,10,1,256]{3,2,1,0:T(1,128)S(1)}, u32[]{:S(2)}, u32[]{:S(2)}) %collective-permute-start.3) | collective-permute-done | bytes 286752 | tf_op jit(solution)/shard_map/ppermute | solution.py:53
  92.2 2.0 %add_multiply_fusion = (f32[8,32,256]{2,1,0:T(8,128)S(1)}, f32[8,32,256]{2,1,0:T(8,128)S(1)}, f32[8,32,256]{2,1,0:T(8,128)S(1)}, f32[8,32,256]{2,1,0:T(8,128)S(1...) fusion(s32[8,32,256]{2,1,0:T(8,128)S(1)} %copy-done, ...), kind=kLoop, calls=%fused_computation.814 | loop fusion | flops 11010048 | bytes 12058624 | tf_op jit(solution)/shard_map/mul | solution.py:131
  97.3 1.4 maximum_bitcast_fusion.21
  101.6 3.3 %collective-permute-start.5 = (f32[1,32,256]{2,1,0:T(8,128)S(1)}, f32[1,32,256]{2,1,0:T(8,128)S(1)}, u32[]{:S(2)}, u32[]{:S(2)}) collective-permute-start(f32[1,32,256]{2,1,0:T(8,128)S(1)} %get-tuple-element.159), channel_id=1, source_target_pairs={{1,0},{2,1},{3,2},{4,3},{5,4},{6,5},{7,6},{8,7},{9,8},{10,9},{11,1... | collective-permute-start | bytes 98312 | tf_op jit(solution)/shard_map/ppermute | solution.py:53
  113.1 1.5 %collective-permute-done.6 = f32[10,1,256]{2,1,0:T(1,128)S(1)} collective-permute-done((f32[10,1,256]{2,1,0:T(1,128)S(1)}, f32[10,1,256]{2,1,0:T(1,128)S(1)}, u32[]{:S(2)}, u32[]{:S(2)}) %collective-permute-start.6) | collective-permute-done | bytes 10272 | tf_op jit(solution)/shard_map/ppermute | solution.py:50
  115.4 2.1 %broadcast_multiply_fusion = (f32[8,32,256]{2,1,0:T(8,128)S(1)}, f32[8,32,256]{2,1,0:T(8,128)S(1)}, f32[8,32,256]{2,1,0:T(8,128)S(1)}, f32[8,32,256]{2,1,0:T(8,1...) fusion(f32[8,32,256]{2,1,0:T(8,128)S(1)} %copy-done.3, ...), kind=kLoop, calls=%fused_computation.838 | loop fusion | flops 6881280 | bytes 9412608 | tf_op jit(solution)/shard_map/div | solution.py:75
  117.6 4.4 %collective-permute-start.17 = (f32[1,32,256]{2,1,0:T(8,128)S(1)}, f32[1,32,256]{2,1,0:T(8,128)S(1)}, u32[]{:S(2)}, u32[]{:S(2)}) collective-permute-start(f32[1,32,256]{2,1,0:T(8,128)S(1)} %get-tuple-element.153), channel_id=1, source_target_pairs={{1,0},{2,1},{3,2},{4,3},{5,4},{6,5},{7,6},{8,7},{9,8},{10,9},{11,1... | collective-permute-start | bytes 98312 | tf_op jit(solution)/shard_map/ppermute | solution.py:53
  122.2 1.5 collective-permute-done.16
  123.7 1.3 collective-permute-start.18
  125.8 1.5 %collective-permute-done.18 = f32[10,1,256]{2,1,0:T(1,128)S(1)} collective-permute-done((f32[10,1,256]{2,1,0:T(1,128)S(1)}, f32[10,1,256]{2,1,0:T(1,128)S(1)}, u32[]{:S(2)}, u32[]{:S(2)}) %collective-permute-start.18) | collective-permute-done | bytes 10272 | tf_op jit(solution)/shard_map/ppermute | solution.py:50
  129.1 4.4 %collective-permute-start.21 = (f32[1,32,256]{2,1,0:T(8,128)S(1)}, f32[1,32,256]{2,1,0:T(8,128)S(1)}, u32[]{:S(2)}, u32[]{:S(2)}) collective-permute-start(f32[1,32,256]{2,1,0:T(8,128)S(1)} %get-tuple-element.147), channel_id=1, source_target_pairs={{1,0},{2,1},{3,2},{4,3},{5,4},{6,5},{7,6},{8,7},{9,8},{10,9},{11,1... | collective-permute-start | bytes 98312 | tf_op jit(solution)/shard_map/ppermute | solution.py:53
  133.7 1.5 collective-permute-done.20
  137.3 1.5 %collective-permute-done.22 = f32[10,1,256]{2,1,0:T(1,128)S(1)} collective-permute-done((f32[10,1,256]{2,1,0:T(1,128)S(1)}, f32[10,1,256]{2,1,0:T(1,128)S(1)}, u32[]{:S(2)}, u32[]{:S(2)}) %collective-permute-start.22) | collective-permute-done | bytes 10272 | tf_op jit(solution)/shard_map/ppermute | solution.py:50
  140.1 4.4 %collective-permute-start.25 = (f32[1,32,256]{2,1,0:T(8,128)S(1)}, f32[1,32,256]{2,1,0:T(8,128)S(1)}, u32[]{:S(2)}, u32[]{:S(2)}) collective-permute-start(f32[1,32,256]{2,1,0:T(8,128)S(1)} %get-tuple-element.141), channel_id=1, source_target_pairs={{1,0},{2,1},{3,2},{4,3},{5,4},{6,5},{7,6},{8,7},{9,8},{10,9},{11,1... | collective-permute-start | bytes 98312 | tf_op jit(solution)/shard_map/ppermute | solution.py:53
  144.7 1.5 collective-permute-done.24
  146.2 1.3 collective-permute-start.26
  148.4 1.5 %collective-permute-done.26 = f32[10,1,256]{2,1,0:T(1,128)S(1)} collective-permute-done((f32[10,1,256]{2,1,0:T(1,128)S(1)}, f32[10,1,256]{2,1,0:T(1,128)S(1)}, u32[]{:S(2)}, u32[]{:S(2)}) %collective-permute-start.26) | collective-permute-done | bytes 10272 | tf_op jit(solution)/shard_map/ppermute | solution.py:50
  (189 shorter events, 59.0 us)
Async XLA Ops:
  6.5 13.4 %copy-start.5 = (f32[1,8,32,256]{3,2,1,0:T(8,128)}, f32[1,8,32,256]{3,2,1,0:T(8,128)S(1)}, u32[]{:S(2)}) copy-start(f32[1,8,32,256]{3,2,1,0:T(8,128)S(1)} %get-tuple-element.41) | copy-start | bytes 786436
  7.3 12.5 %copy-start.6 = (f32[1,8,32,256]{3,2,1,0:T(8,128)}, f32[1,8,32,256]{3,2,1,0:T(8,128)S(1)}, u32[]{:S(2)}) copy-start(f32[1,8,32,256]{3,2,1,0:T(8,128)S(1)} %get-tuple-element.39) | copy-start | bytes 786436
  8.2 11.7 %copy-start.7 = (f32[1,8,32,256]{3,2,1,0:T(8,128)}, f32[1,8,32,256]{3,2,1,0:T(8,128)S(1)}, u32[]{:S(2)}) copy-start(f32[1,8,32,256]{3,2,1,0:T(8,128)S(1)} %get-tuple-element.37) | copy-start | bytes 786436
  25.1 12.8 %copy-start.4 = (f32[8,32,256]{2,1,0:T(8,128)S(1)}, f32[8,32,256]{2,1,0:T(8,128)}, u32[]{:S(2)}) copy-start(f32[8,32,256]{2,1,0:T(8,128)} %param.11) | copy-start | bytes 786436
  32.4 31.8 %collective-permute-start = (f32[28,1,32,256]{3,2,1,0:T(8,128)S(1)}, f32[28,1,32,256]{3,2,1,0:T(8,128)S(1)}, u32[]{:S(2)}, u32[]{:S(2)}) collective-permute-start(f32[28,1,32,256]{3,2,1,0:T(8,128)S(1)} %get-tuple-element.82), channel_id=1, source_target_pairs={{0,1},{1,2},{2,3},{3,4},{4,5},{5,6},{6,7},{7,8},{8,9},{9,10},{10,1... | collective-permute-start | bytes 2752520 | tf_op jit(solution)/shard_map/ppermute | solution.py:50
  32.9 31.3 %collective-permute-start.1 = (f32[28,1,32,256]{3,2,1,0:T(8,128)S(1)}, f32[28,1,32,256]{3,2,1,0:T(8,128)S(1)}, u32[]{:S(2)}, u32[]{:S(2)}) collective-permute-start(f32[28,1,32,256]{3,2,1,0:T(8,128)S(1)} %get-tuple-element.83), channel_id=1, source_target_pairs={{1,0},{2,1},{3,2},{4,3},{5,4},{6,5},{7,6},{8,7},{9,8},{10,9},{11,1... | collective-permute-start | bytes 2752520 | tf_op jit(solution)/shard_map/ppermute | solution.py:53
  38.0 20.5 %collective-permute-start.8 = (f32[2,1,32,256]{3,2,1,0:T(8,128)S(1)}, f32[2,1,32,256]{3,2,1,0:T(8,128)S(1)}, u32[]{:S(2)}, u32[]{:S(2)}) collective-permute-start(f32[2,1,32,256]{3,2,1,0:T(8,128)S(1)} %get-tuple-element.92), channel_id=1, source_target_pairs={{0,1},{1,2},{2,3},{3,4},{4,5},{5,6},{6,7},{7,8},{8,9},{9,10},{10,1... | collective-permute-start | bytes 196616 | tf_op jit(solution)/shard_map/ppermute | solution.py:50
  38.1 20.4 %collective-permute-start.9 = (f32[2,1,32,256]{3,2,1,0:T(8,128)S(1)}, f32[2,1,32,256]{3,2,1,0:T(8,128)S(1)}, u32[]{:S(2)}, u32[]{:S(2)}) collective-permute-start(f32[2,1,32,256]{3,2,1,0:T(8,128)S(1)} %get-tuple-element.93), channel_id=1, source_target_pairs={{1,0},{2,1},{3,2},{4,3},{5,4},{6,5},{7,6},{8,7},{9,8},{10,9},{11,1... | collective-permute-start | bytes 196616 | tf_op jit(solution)/shard_map/ppermute | solution.py:53
  42.5 7.6 %collective-permute-start.12 = (f32[1,32,256]{2,1,0:T(8,128)S(1)}, f32[1,32,256]{2,1,0:T(8,128)S(1)}, u32[]{:S(2)}, u32[]{:S(2)}) collective-permute-start(f32[1,32,256]{2,1,0:T(8,128)S(1)} %get-tuple-element.165), channel_id=1, source_target_pairs={{0,1},{1,2},{2,3},{3,4},{4,5},{5,6},{6,7},{7,8},{8,9},{9,10},{10,1... | collective-permute-start | bytes 98312 | tf_op jit(solution)/shard_map/ppermute | solution.py:50
  50.1 8.4 %collective-permute-start.13 = (f32[1,32,256]{2,1,0:T(8,128)S(1)}, f32[1,32,256]{2,1,0:T(8,128)S(1)}, u32[]{:S(2)}, u32[]{:S(2)}) collective-permute-start(f32[1,32,256]{2,1,0:T(8,128)S(1)} %get-tuple-element.164), channel_id=1, source_target_pairs={{1,0},{2,1},{3,2},{4,3},{5,4},{6,5},{7,6},{8,7},{9,8},{10,9},{11,1... | collective-permute-start | bytes 98312 | tf_op jit(solution)/shard_map/ppermute | solution.py:53
  58.6 3.8 %collective-permute-start.10 = (f32[2,10,1,256]{3,2,1,0:T(1,128)S(1)}, f32[2,10,1,256]{3,2,1,0:T(1,128)S(1)}, u32[]{:S(2)}, u32[]{:S(2)}) collective-permute-start(f32[2,10,1,256]{3,2,1,0:T(1,128)S(1)} %get-tuple-element.90), channel_id=1, source_target_pairs={{0,16},{16,0},{1,17},{17,1},{2,18},{18,2},{3,19},{19,3},{4,20},{20... | collective-permute-start | bytes 61448 | tf_op jit(solution)/shard_map/ppermute | solution.py:50
  60.1 3.8 %collective-permute-start.11 = (f32[2,10,1,256]{3,2,1,0:T(1,128)S(1)}, f32[2,10,1,256]{3,2,1,0:T(1,128)S(1)}, u32[]{:S(2)}, u32[]{:S(2)}) collective-permute-start(f32[2,10,1,256]{3,2,1,0:T(1,128)S(1)} %get-tuple-element.91), channel_id=1, source_target_pairs={{16,0},{0,16},{17,1},{1,17},{18,2},{2,18},{19,3},{3,19},{20,4},{4,... | collective-permute-start | bytes 61448 | tf_op jit(solution)/shard_map/ppermute | solution.py:53
  60.7 52.4 %collective-permute-start.14 = (f32[10,1,256]{2,1,0:T(1,128)S(1)}, f32[10,1,256]{2,1,0:T(1,128)S(1)}, u32[]{:S(2)}, u32[]{:S(2)}) collective-permute-start(f32[10,1,256]{2,1,0:T(1,128)S(1)} %get-tuple-element.110), channel_id=1, source_target_pairs={{0,16},{16,0},{1,17},{17,1},{2,18},{18,2},{3,19},{19,3},{4,20},{20... | collective-permute-start | bytes 30728 | tf_op jit(solution)/shard_map/ppermute | solution.py:50
  62.4 50.7 %collective-permute-start.15 = (f32[10,1,256]{2,1,0:T(1,128)S(1)}, f32[10,1,256]{2,1,0:T(1,128)S(1)}, u32[]{:S(2)}, u32[]{:S(2)}) collective-permute-start(f32[10,1,256]{2,1,0:T(1,128)S(1)} %get-tuple-element.111), channel_id=1, source_target_pairs={{16,0},{0,16},{17,1},{1,17},{18,2},{2,18},{19,3},{3,19},{20,4},{4,... | collective-permute-start | bytes 30728 | tf_op jit(solution)/shard_map/ppermute | solution.py:53
  66.7 8.4 %collective-permute-start.2 = (f32[28,10,1,256]{3,2,1,0:T(1,128)S(1)}, f32[28,10,1,256]{3,2,1,0:T(1,128)S(1)}, u32[]{:S(2)}, u32[]{:S(2)}) collective-permute-start(f32[28,10,1,256]{3,2,1,0:T(1,128)S(1)} %get-tuple-element.80), channel_id=1, source_target_pairs={{0,16},{16,0},{1,17},{17,1},{2,18},{18,2},{3,19},{19,3},{4,20},{20... | collective-permute-start | bytes 860168 | tf_op jit(solution)/shard_map/ppermute | solution.py:50
  67.3 14.0 %collective-permute-start.3 = (f32[28,10,1,256]{3,2,1,0:T(1,128)S(1)}, f32[28,10,1,256]{3,2,1,0:T(1,128)S(1)}, u32[]{:S(2)}, u32[]{:S(2)}) collective-permute-start(f32[28,10,1,256]{3,2,1,0:T(1,128)S(1)} %get-tuple-element.81), channel_id=1, source_target_pairs={{16,0},{0,16},{17,1},{1,17},{18,2},{2,18},{19,3},{3,19},{20,4},{4,... | collective-permute-start | bytes 860168 | tf_op jit(solution)/shard_map/ppermute | solution.py:53
  100.4 10.5 %collective-permute-start.4 = (f32[1,32,256]{2,1,0:T(8,128)S(1)}, f32[1,32,256]{2,1,0:T(8,128)S(1)}, u32[]{:S(2)}, u32[]{:S(2)}) collective-permute-start(f32[1,32,256]{2,1,0:T(8,128)S(1)} %get-tuple-element.158), channel_id=1, source_target_pairs={{0,1},{1,2},{2,3},{3,4},{4,5},{5,6},{6,7},{7,8},{8,9},{9,10},{10,1... | collective-permute-start | bytes 98312 | tf_op jit(solution)/shard_map/ppermute | solution.py:50
  101.6 9.2 %collective-permute-start.5 = (f32[1,32,256]{2,1,0:T(8,128)S(1)}, f32[1,32,256]{2,1,0:T(8,128)S(1)}, u32[]{:S(2)}, u32[]{:S(2)}) collective-permute-start(f32[1,32,256]{2,1,0:T(8,128)S(1)} %get-tuple-element.159), channel_id=1, source_target_pairs={{1,0},{2,1},{3,2},{4,3},{5,4},{6,5},{7,6},{8,7},{9,8},{10,9},{11,1... | collective-permute-start | bytes 98312 | tf_op jit(solution)/shard_map/ppermute | solution.py:53
  110.9 3.7 %collective-permute-start.6 = (f32[10,1,256]{2,1,0:T(1,128)S(1)}, f32[10,1,256]{2,1,0:T(1,128)S(1)}, u32[]{:S(2)}, u32[]{:S(2)}) collective-permute-start(f32[10,1,256]{2,1,0:T(1,128)S(1)} %get-tuple-element.108), channel_id=1, source_target_pairs={{0,16},{16,0},{1,17},{17,1},{2,18},{18,2},{3,19},{19,3},{4,20},{20... | collective-permute-start | bytes 30728 | tf_op jit(solution)/shard_map/ppermute | solution.py:50
  111.7 3.7 %collective-permute-start.7 = (f32[10,1,256]{2,1,0:T(1,128)S(1)}, f32[10,1,256]{2,1,0:T(1,128)S(1)}, u32[]{:S(2)}, u32[]{:S(2)}) collective-permute-start(f32[10,1,256]{2,1,0:T(1,128)S(1)} %get-tuple-element.109), channel_id=1, source_target_pairs={{16,0},{0,16},{17,1},{1,17},{18,2},{2,18},{19,3},{3,19},{20,4},{4,... | collective-permute-start | bytes 30728 | tf_op jit(solution)/shard_map/ppermute | solution.py:53
  117.5 6.1 %collective-permute-start.16 = (f32[1,32,256]{2,1,0:T(8,128)S(1)}, f32[1,32,256]{2,1,0:T(8,128)S(1)}, u32[]{:S(2)}, u32[]{:S(2)}) collective-permute-start(f32[1,32,256]{2,1,0:T(8,128)S(1)} %get-tuple-element.152), channel_id=1, source_target_pairs={{0,1},{1,2},{2,3},{3,4},{4,5},{5,6},{6,7},{7,8},{8,9},{9,10},{10,1... | collective-permute-start | bytes 98312 | tf_op jit(solution)/shard_map/ppermute | solution.py:50
  117.6 6.0 %collective-permute-start.17 = (f32[1,32,256]{2,1,0:T(8,128)S(1)}, f32[1,32,256]{2,1,0:T(8,128)S(1)}, u32[]{:S(2)}, u32[]{:S(2)}) collective-permute-start(f32[1,32,256]{2,1,0:T(8,128)S(1)} %get-tuple-element.153), channel_id=1, source_target_pairs={{1,0},{2,1},{3,2},{4,3},{5,4},{6,5},{7,6},{8,7},{9,8},{10,9},{11,1... | collective-permute-start | bytes 98312 | tf_op jit(solution)/shard_map/ppermute | solution.py:53
  123.7 3.7 %collective-permute-start.18 = (f32[10,1,256]{2,1,0:T(1,128)S(1)}, f32[10,1,256]{2,1,0:T(1,128)S(1)}, u32[]{:S(2)}, u32[]{:S(2)}) collective-permute-start(f32[10,1,256]{2,1,0:T(1,128)S(1)} %get-tuple-element.98), channel_id=1, source_target_pairs={{0,16},{16,0},{1,17},{17,1},{2,18},{18,2},{3,19},{19,3},{4,20},{20... | collective-permute-start | bytes 30728 | tf_op jit(solution)/shard_map/ppermute | solution.py:50
  125.0 3.7 %collective-permute-start.19 = (f32[10,1,256]{2,1,0:T(1,128)S(1)}, f32[10,1,256]{2,1,0:T(1,128)S(1)}, u32[]{:S(2)}, u32[]{:S(2)}) collective-permute-start(f32[10,1,256]{2,1,0:T(1,128)S(1)} %get-tuple-element.99), channel_id=1, source_target_pairs={{16,0},{0,16},{17,1},{1,17},{18,2},{2,18},{19,3},{3,19},{20,4},{4,... | collective-permute-start | bytes 30728 | tf_op jit(solution)/shard_map/ppermute | solution.py:53
  129.0 6.1 %collective-permute-start.20 = (f32[1,32,256]{2,1,0:T(8,128)S(1)}, f32[1,32,256]{2,1,0:T(8,128)S(1)}, u32[]{:S(2)}, u32[]{:S(2)}) collective-permute-start(f32[1,32,256]{2,1,0:T(8,128)S(1)} %get-tuple-element.146), channel_id=1, source_target_pairs={{0,1},{1,2},{2,3},{3,4},{4,5},{5,6},{6,7},{7,8},{8,9},{9,10},{10,1... | collective-permute-start | bytes 98312 | tf_op jit(solution)/shard_map/ppermute | solution.py:50
  129.1 6.0 %collective-permute-start.21 = (f32[1,32,256]{2,1,0:T(8,128)S(1)}, f32[1,32,256]{2,1,0:T(8,128)S(1)}, u32[]{:S(2)}, u32[]{:S(2)}) collective-permute-start(f32[1,32,256]{2,1,0:T(8,128)S(1)} %get-tuple-element.147), channel_id=1, source_target_pairs={{1,0},{2,1},{3,2},{4,3},{5,4},{6,5},{7,6},{8,7},{9,8},{10,9},{11,1... | collective-permute-start | bytes 98312 | tf_op jit(solution)/shard_map/ppermute | solution.py:53
  135.1 3.7 %collective-permute-start.22 = (f32[10,1,256]{2,1,0:T(1,128)S(1)}, f32[10,1,256]{2,1,0:T(1,128)S(1)}, u32[]{:S(2)}, u32[]{:S(2)}) collective-permute-start(f32[10,1,256]{2,1,0:T(1,128)S(1)} %get-tuple-element.96), channel_id=1, source_target_pairs={{0,16},{16,0},{1,17},{17,1},{2,18},{18,2},{3,19},{19,3},{4,20},{20... | collective-permute-start | bytes 30728 | tf_op jit(solution)/shard_map/ppermute | solution.py:50
  136.0 3.7 %collective-permute-start.23 = (f32[10,1,256]{2,1,0:T(1,128)S(1)}, f32[10,1,256]{2,1,0:T(1,128)S(1)}, u32[]{:S(2)}, u32[]{:S(2)}) collective-permute-start(f32[10,1,256]{2,1,0:T(1,128)S(1)} %get-tuple-element.97), channel_id=1, source_target_pairs={{16,0},{0,16},{17,1},{1,17},{18,2},{2,18},{19,3},{3,19},{20,4},{4,... | collective-permute-start | bytes 30728 | tf_op jit(solution)/shard_map/ppermute | solution.py:53
  140.1 6.1 %collective-permute-start.24 = (f32[1,32,256]{2,1,0:T(8,128)S(1)}, f32[1,32,256]{2,1,0:T(8,128)S(1)}, u32[]{:S(2)}, u32[]{:S(2)}) collective-permute-start(f32[1,32,256]{2,1,0:T(8,128)S(1)} %get-tuple-element.140), channel_id=1, source_target_pairs={{0,1},{1,2},{2,3},{3,4},{4,5},{5,6},{6,7},{7,8},{8,9},{9,10},{10,1... | collective-permute-start | bytes 98312 | tf_op jit(solution)/shard_map/ppermute | solution.py:50
  140.1 6.0 %collective-permute-start.25 = (f32[1,32,256]{2,1,0:T(8,128)S(1)}, f32[1,32,256]{2,1,0:T(8,128)S(1)}, u32[]{:S(2)}, u32[]{:S(2)}) collective-permute-start(f32[1,32,256]{2,1,0:T(8,128)S(1)} %get-tuple-element.141), channel_id=1, source_target_pairs={{1,0},{2,1},{3,2},{4,3},{5,4},{6,5},{7,6},{8,7},{9,8},{10,9},{11,1... | collective-permute-start | bytes 98312 | tf_op jit(solution)/shard_map/ppermute | solution.py:53
  146.2 3.7 %collective-permute-start.26 = (f32[10,1,256]{2,1,0:T(1,128)S(1)}, f32[10,1,256]{2,1,0:T(1,128)S(1)}, u32[]{:S(2)}, u32[]{:S(2)}) collective-permute-start(f32[10,1,256]{2,1,0:T(1,128)S(1)} %get-tuple-element.94), channel_id=1, source_target_pairs={{0,16},{16,0},{1,17},{17,1},{2,18},{18,2},{3,19},{19,3},{4,20},{20... | collective-permute-start | bytes 30728 | tf_op jit(solution)/shard_map/ppermute | solution.py:50
  147.5 3.7 %collective-permute-start.27 = (f32[10,1,256]{2,1,0:T(1,128)S(1)}, f32[10,1,256]{2,1,0:T(1,128)S(1)}, u32[]{:S(2)}, u32[]{:S(2)}) collective-permute-start(f32[10,1,256]{2,1,0:T(1,128)S(1)} %get-tuple-element.95), channel_id=1, source_target_pairs={{16,0},{0,16},{17,1},{1,17},{18,2},{2,18},{19,3},{3,19},{20,4},{4,... | collective-permute-start | bytes 30728 | tf_op jit(solution)/shard_map/ppermute | solution.py:53
  (10 other events, 70.9 us)
where the time goes:
time: 153 us; the launch traced here: 152 us
  other arithmetic  57.6 us (38%)
  starting transfers between devices  43.6 us (28%)
  waiting for transfers between devices  42.6 us (28%)
  local copies, waits for them, and re-layouts  7.03 us (5%)
    ppermute x14, starting transfers between devices, with_halo(): lax.ppermute(lax.slice_in_dim(block, 0, width, axis=dim), axis, backward)  33.6 us
    unnamed x45, other arithmetic  29.8 us
    ppermute x14, waiting for transfers between devices, with_halo(): lax.ppermute(lax.slice_in_dim(block, block.shape[dim] - width, None, axis...  24.1 us
    ppermute x14, waiting for transfers between devices, with_halo(): lax.ppermute(lax.slice_in_dim(block, 0, width, axis=dim), axis, backward)  18.6 us
    slice x11, other arithmetic, shifted(): lax.slice_in_dim(padded, width - int(dirc[0]), width - int(dirc[0]) + cor...  13.8 us
    ppermute x14, starting transfers between devices, with_halo(): lax.ppermute(lax.slice_in_dim(block, block.shape[dim] - width, None, axis...  10 us
    slice x44, local copies, waits for them, and re-layouts, shifted(): return jnp.roll(piece, int(dirc[1]), axis=rank_all - 1)  4.23 us
    reduce_sum x1, other arithmetic, per_device(): jnp.sum(populations * jnp.asarray(flow_dirs[:, a], jnp.float32)[:, None,...  3.95 us
  transfers between devices with their start and end apart: 28, of which 16 were waited for; matrix products, arithmetic and copies ran while one was open for 19% of the time, Pallas kernels for 0%

commit v1 on v0

v1 whole, which is shorter than its diff:
```python
import functools

import jax
import jax.numpy as jnp
from jax import lax
from jax.experimental import pallas as pl
from jax.experimental.pallas import tpu as pltpu
from jax.sharding import PartitionSpec as P

ITERS = 4
DIRS = (
    (0, 0, 0),
    (1, 0, 0),
    (-1, 0, 0),
    (0, 1, 0),
    (0, -1, 0),
    (0, 0, 1),
    (0, 0, -1),
    (1, 1, 0),
    (-1, -1, 0),
    (1, -1, 0),
    (-1, 1, 0),
    (1, 0, 1),
    (-1, 0, -1),
    (1, 0, -1),
    (-1, 0, 1),
    (0, 1, 1),
    (0, -1, -1),
    (0, 1, -1),
    (0, -1, 1),
)
OPP = (0, 2, 1, 4, 3, 6, 5, 8, 7, 10, 9, 12, 11, 14, 13, 16, 15, 18, 17)
PAIRS = ((1, 2), (3, 4), (5, 6), (7, 8), (9, 10), (11, 12), (13, 14), (15, 16), (17, 18))
ZPAIRS = ((5, 6), (11, 12), (14, 13), (15, 16), (18, 17))
ZSLOT = {5: (1, 2), 6: (1, 2), 11: (1, 3), 12: (1, 3), 14: (2, 0), 13: (2, 0), 15: (2, 1), 16: (2, 1), 18: (2, 2), 17: (2, 2)}
XHIGH = (1, 7, 9, 11, 13)
XLOW = (2, 8, 10, 12, 14)
W0, W1, W2 = 1.0 / 3.0, 1.0 / 18.0, 1.0 / 36.0
RELAX_FLOW = 0.8
RELAX_HEAT = 0.7
JUMP = 0.3
FILM = 0.5
THETA = 61.0
DELTA = 60.0
WALL_OWN = 0.25 * JUMP
WALL_NEAR = 0.25 * (1.0 - JUMP)
DEEP = 4
TILE = 8

VM = pl.BlockSpec(memory_space=pltpu.VMEM)
ANY = pl.BlockSpec(memory_space=pl.ANY)


def call(body, outs, args, in_specs=None, out_specs=None, scratch=(), aliases=None, limit=4 << 20):
    return pl.pallas_call(
        body,
        out_shape=[jax.ShapeDtypeStruct(shape, jnp.float32) for shape in outs],
        in_specs=in_specs or [VM] * len(args),
        out_specs=out_specs or [VM] * len(outs),
        scratch_shapes=list(scratch),
        input_output_aliases=aliases or {},
        compiler_params=pltpu.CompilerParams(vmem_limit_bytes=limit),
    )(*args)


def rows8(shape):
    return lax.broadcasted_iota(jnp.int32, shape, 0)


def collide_body(pops, heat, ts, cond, pore, flow, hot, tsm, km):
    nx, nz = ts.shape[0], ts.shape[1] // TILE

    def step(i, carry):
        x = i // nz
        rows = pl.ds(pl.multiple_of((i % nz) * TILE, TILE), TILE)
        is_pore = pore[x, rows, :] != 0
        tsm[x, rows, :] = jnp.where(is_pore, 0.0, ts[x, rows, :])
        km[x, rows, :] = jnp.where(is_pore, 0.0, cond[x, rows, :])
        p = [pops[d, x, rows, :] for d in range(19)]
        diff = [p[a] - p[b] for a, b in PAIRS]
        rho = p[0]
        for a, b in PAIRS:
            rho = rho + (p[a] + p[b])
        inv = 1.0 / rho
        ux = (diff[0] + diff[3] + diff[4] + diff[5] + diff[6]) * inv
        uy = (diff[1] + diff[3] - diff[4] + diff[7] + diff[8]) * inv
        uz = (diff[2] + diff[5] - diff[6] + diff[7] - diff[8]) * inv
        base = 1.0 - 1.5 * (ux * ux + uy * uy + uz * uz)
        keep = 1.0 - 1.0 / RELAX_FLOW
        flow[0, x, rows, :] = jnp.where(is_pore, (W0 / RELAX_FLOW) * rho * base + keep * p[0], p[0])
        speeds = (ux, uy, uz, ux + uy, ux - uy, ux + uz, ux - uz, uy + uz, uy - uz)
        scaled1 = (W1 / RELAX_FLOW) * rho
        scaled2 = (W2 / RELAX_FLOW) * rho
        for n, (a, b) in enumerate(PAIRS):
            scaled = scaled1 if n < 3 else scaled2
            cu = speeds[n]
            even = scaled * (base + 4.5 * (cu * cu))
            odd = scaled * (3.0 * cu)
            flow[a, x, rows, :] = jnp.where(is_pore, (even + odd) + keep * p[a], p[a])
            flow[b, x, rows, :] = jnp.where(is_pore, (even - odd) + keep * p[b], p[b])
        h = [heat[d, x, rows, :] for d in range(7)]
        temp = h[0] + (h[1] + h[2]) + (h[3] + h[4]) + (h[5] + h[6])
        hkeep = 1.0 - 1.0 / RELAX_HEAT
        hot[0, x, rows, :] = jnp.where(is_pore, (0.25 / RELAX_HEAT) * temp + hkeep * h[0], h[0])
        even = (0.125 / RELAX_HEAT) * temp
        for n in range(3):
            a, b = PAIRS[n]
            odd = even * (4.0 * speeds[n])
            hot[a, x, rows, :] = jnp.where(is_pore, (even + odd) + hkeep * h[a], h[a])
            hot[b, x, rows, :] = jnp.where(is_pore, (even - odd) + hkeep * h[b], h[b])
        return carry

    lax.fori_loop(0, nx * nz, step, 0)


def edge_tile(low, high, row):
    return jnp.where(row < DEEP, low, high)


def pack_pairs(pairs, row):
    out = None
    for j, (low, high) in enumerate(pairs):
        if j:
            low, high = pltpu.roll(low, j, 0), pltpu.roll(high, TILE - j, 0)
        both = jnp.where(row < DEEP, low, high)
        out = both if out is None else jnp.where((row == j) | (row == TILE - 1 - j), both, out)
    return out


def heat_body(hot, flow, tsm, km, new_heat, temp, bounce, zmsg):
    nx, nz, ny = tsm.shape
    rowz = rows8((nz, ny))
    row = rows8((TILE, ny))
    first, last = slice(0, TILE), slice(nz - TILE, nz)
    for x in range(nx):
        t = tsm[x]
        is_pore = t == 0.0
        g = [hot[d, x] for d in range(7)]
        own = WALL_OWN * (g[0] + (g[1] + g[2]) + (g[3] + g[4]) + (g[5] + g[6]))
        new_heat[0, x] = g[0]
        total = g[0]

        def arrive(d, near, moved):
            return jnp.where(near == 0.0, moved, (own - g[OPP[d]]) + WALL_NEAR * near)

        for d in (1, 2):
            src = x - DIRS[d][0]
            if 0 <= src < nx:
                got = arrive(d, tsm[src], hot[d, src])
                total = total + got
                new_heat[d, x] = jnp.where(is_pore, got, g[d])
            else:
                new_heat[d, x] = g[d]
                bounce[0 if x == 0 else 1] = own - g[OPP[d]]
        for d in (3, 4):
            by = DIRS[d][1] % ny
            got = arrive(d, pltpu.roll(t, by, 1), pltpu.roll(g[d], by, 1))
            total = total + got
            new_heat[d, x] = jnp.where(is_pore, got, g[d])
        for d in (5, 6):
            by = DIRS[d][2] % nz
            got = arrive(d, pltpu.roll(t, by, 0), pltpu.roll(g[d], by, 0))
            inside = rowz != (0 if d == 5 else nz - 1)
            total = total + jnp.where(inside, got, 0.0)
            new_heat[d, x] = jnp.where(is_pore & inside, got, g[d])
        total = jnp.where(is_pore, total, 0.0)
        temp[x] = total
        zmsg[x] = edge_tile(total[first], total[last], row)
        pairs = [(g[6][first], g[5][last]), ((own - g[6])[first], (own - g[5])[last])]
        for up, down in ZPAIRS:
            pairs.append((flow[down, x, first, :], flow[up, x, last, :]))
        zmsg[nx + x] = pack_pairs(pairs[:4], row)
        zmsg[2 * nx + x] = pack_pairs(pairs[4:], row)
        zmsg[3 * nx + x] = edge_tile(t[first], t[last], row)
        zmsg[4 * nx + x] = edge_tile(km[x, first, :], km[x, last, :], row)
    ends = (hot[2, 0], hot[1, nx - 1], bounce[0], bounce[1])
    for n, v in enumerate(ends):
        zmsg[5 * nx + n] = edge_tile(v[first], v[last], row)


def zjoin_body(mine, theirs, temp, hot, tsm, km, bounce, flow, heat_in, heat_ends, low, high, flow_low, flow_high):
    nx, nz, ny = tsm.shape
    row = rows8((TILE, ny))
    edge = (row == 0) | (row == TILE - 1)
    first, last, halo = slice(0, TILE), slice(nz - TILE, nz), slice(nz, nz + TILE)
    half = nx // 2

    def swap(v):
        return jnp.where(row < DEEP, pltpu.roll(v, 1, 0), pltpu.roll(v, TILE - 1, 0))

    def slot1(v):
        return jnp.where(row < DEEP, pltpu.roll(v, TILE - 1, 0), pltpu.roll(v, 1, 0))

    for x in range(nx):
        my_t, their_t = mine[3 * nx + x], theirs[3 * nx + x]
        my_p, their_p = mine[nx + x], theirs[nx + x]
        near = swap(their_t)
        got = jnp.where(near == 0.0, swap(their_p), slot1(my_p) + WALL_NEAR * near)
        mine_in = edge & (my_t == 0.0)
        add = jnp.where(mine_in, got, 0.0)
        near = swap(my_t)
        back = jnp.where(near == 0.0, swap(my_p), slot1(their_p) + WALL_NEAR * near)
        back = jnp.where(edge & (their_t == 0.0), back, 0.0)
        heat_ends[0, x] = jnp.where(mine_in & (row == 0), got, heat_in[5, x, first, :])
        heat_ends[1, x] = jnp.where(mine_in & (row == TILE - 1), got, heat_in[6, x, last, :])
        out, n = (low, x) if x < half else (high, x - half)
        out[n, 0:nz, :] = temp[x]
        out[n, first, :] = temp[x, first, :] + jnp.where(row == 0, add, 0.0)
        out[n, last, :] = temp[x, last, :] + jnp.where(row == TILE - 1, add, 0.0)
        out[n, halo, :] = theirs[x] + back
        out[DEEP + 2 + n, 0:nz, :] = tsm[x]
        out[DEEP + 2 + n, halo, :] = their_t
        out[2 * DEEP + 2 + n, 0:nz, :] = km[x]
        out[2 * DEEP + 2 + n, halo, :] = theirs[4 * nx + x]
    for side, out in ((0, low), (1, high)):
        x = side * (nx - 1)
        out[DEEP, 0:nz, :] = hot[2 - side, x]
        out[DEEP, halo, :] = theirs[5 * nx + side]
        out[DEEP + 1, 0:nz, :] = bounce[side]
        out[DEEP + 1, halo, :] = theirs[5 * nx + 2 + side]
    for x, dirs, out in ((0, XLOW, flow_low), (nx - 1, XHIGH, flow_high)):
        for n, d in enumerate(dirs):
            out[n, 0:nz, :] = flow[d, x]
            if d in ZSLOT:
                block, j = ZSLOT[d]
                v = theirs[block * nx + x]
                by = j if DIRS[d][2] > 0 else TILE - j
                out[n, halo, :] = pltpu.roll(v, by % TILE, 0) if by % TILE else v
            else:
                out[n, halo, :] = jnp.zeros((TILE, ny), jnp.float32)


def conduct_body(low, high, from_low, from_high, hot, ts, heat_in, new_heat, new_solid, temp, fx, fy, fz, resid, step_a, step_b, ends, sems):
    nx, nz, ny = ts.shape
    ext = low.shape[1]
    planes = nx + 2 * DEEP

    def at(field, p):
        part, n = ((from_low, p), (low, p - DEEP), (high, p - 2 * DEEP), (from_high, p - 3 * DEEP))[p // DEEP]
        return part[{"temp": 0, "ts": DEEP + 2, "km": 2 * DEEP + 2}[field] + n]

    def join(below, above, p_low, p_high):
        t_low, t_high = at("ts", p_low), at("ts", p_high)
        up = jnp.where(t_low == 0.0, below[DEEP], above[DEEP + 1] + WALL_NEAR * t_low)
        down = jnp.where(t_high == 0.0, above[DEEP], below[DEEP + 1] + WALL_NEAR * t_high)
        temp[p_high] = jnp.where(t_high == 0.0, at("temp", p_high) + up, 0.0)
        temp[p_low] = jnp.where(t_low == 0.0, at("temp", p_low) + down, 0.0)
        return up, down

    for p in range(planes):
        if p not in (DEEP - 1, DEEP, DEEP + nx - 1, DEEP + nx):
            temp[p] = at("temp", p)
    up, _ = join(from_low, low, DEEP - 1, DEEP)
    _, down = join(high, from_high, DEEP + nx - 1, DEEP + nx)
    own = slice(0, nz)
    ends[0] = jnp.where(at("ts", DEEP)[own] == 0.0, up[own], hot[1, 0])
    ends[1] = jnp.where(at("ts", DEEP + nx - 1)[own] == 0.0, down[own], hot[2, nx - 1])
    copies = [
        pltpu.make_async_copy(ends.at[0], new_heat.at[1, 0], sems.at[0]),
        pltpu.make_async_copy(ends.at[1], new_heat.at[2, nx - 1], sems.at[1]),
    ]
    for copy in copies:
        copy.start()

    def face(a, b):
        return (2.0 * a) * b / jnp.maximum(a + b, 1.0)

    def net_of(p, v, below, prev, ahead):
        flux_y = fy[p] * (pltpu.roll(v, 1, 1) - v)
        flux_z = fz[p] * (pltpu.roll(v, 1, 0) - v)
        if below is None:
            below = fx[p] * (prev - v)
        above = fx[p + 1] * (v - ahead)
        net = below - above
        net = net + (flux_y - pltpu.roll(flux_y, ny - 1, 1))
        net = net + (flux_z - pltpu.roll(flux_z, ext - 1, 0))
        return net, above

    for p in range(1, planes):
        k, kp = at("km", p), at("km", p - 1)
        fx[p] = face(k, kp)
    below = None
    for p in range(1, planes - 1):
        k, t = at("km", p), at("ts", p)
        ky = pltpu.roll(k, 1, 1)
        kz = pltpu.roll(k, 1, 0)
        fy[p] = face(k, ky)
        fz[p] = face(k, kz)
        pore = jnp.where(k == 0.0, 1.0, 0.0)
        count = jnp.where(ky == 0.0, 1.0, 0.0) + jnp.where(kz == 0.0, 1.0, 0.0)
        count = count + pltpu.roll(pore, ny - 1, 1) + pltpu.roll(pore, ext - 1, 0)
        count = count + jnp.where(at("km", p - 1) == 0.0, 1.0, 0.0) + jnp.where(at("km", p + 1) == 0.0, 1.0, 0.0)
        mid = temp[p]
        near = (temp[p - 1] + temp[p + 1]) + (pltpu.roll(mid, 1, 1) + pltpu.roll(mid, ny - 1, 1))
        near = near + (pltpu.roll(mid, 1, 0) + pltpu.roll(mid, ext - 1, 0))
        net, below = net_of(p, t, below, at("ts", p - 1), at("ts", p + 1))
        r = jnp.where(k == 0.0, 0.0, FILM * (near - count * t)) + net
        resid[p] = r
        s = r / THETA
        step_a[p] = s
        if DEEP <= p < DEEP + nx:
            new_solid[p - DEEP] = ts[p - DEEP] + s[own]
    sigma = THETA / DELTA
    ratio = 1.0 / sigma
    now, later = step_a, step_b
    for sweep in range(1, ITERS):
        after = 1.0 / (2.0 * sigma - ratio)
        below = None
        for p in range(1 + sweep, planes - 1 - sweep):
            v = now[p]
            net, below = net_of(p, v, below, now[p - 1], now[p + 1])
            r = resid[p] - (v - net)
            s = (after * ratio) * v + (2.0 * after / DELTA) * r
            if sweep + 1 < ITERS:
                resid[p] = r
                later[p] = s
            if DEEP <= p < DEEP + nx:
                new_solid[p - DEEP] = new_solid[p - DEEP] + s[own]
        ratio = after
        now, later = later, now
    for copy in copies:
        copy.wait()


def flow_body(xs, ends, *refs):
    if ends:
        flow, theirs, low, high, from_low, from_high, flow_low, flow_high, held, out, buf, sems = refs
    else:
        flow, theirs, low, high, heat, heat_ends, out, heat_out, buf, sems, heat_sems = refs
    nx, nz, ny = flow.shape[1:]
    ext = low.shape[1]
    rowz = rows8((nz, ny))
    half = nx // 2
    own = slice(0, nz)
    if not ends:
        whole = pltpu.make_async_copy(heat, heat_out, heat_sems.at[0])
        whole.start()

    def tse(q):
        if q < 0:
            return from_low[2 * DEEP + 1]
        if q >= nx:
            return from_high[DEEP + 2]
        return low[DEEP + 2 + q] if q < half else high[DEEP + 2 + q - half]

    def source(d, q):
        if q < 0:
            return flow_low[XHIGH.index(d), own, :]
        if q >= nx:
            return flow_high[XLOW.index(d), own, :]
        return flow[d, q]

    def halo_row(d, q):
        up = DIRS[d][2] > 0
        if q < 0:
            n = ext - 1 if up else nz
            return flow_low[XHIGH.index(d), n : n + 1, :]
        if q >= nx:
            n = ext - 1 if up else nz
            return flow_high[XLOW.index(d), n : n + 1, :]
        block, j = ZSLOT[d]
        n = TILE - 1 - j if up else j
        return theirs[block * nx + q, n : n + 1, :]

    copies = []
    for n, x in enumerate(xs):
        slot = n % 2
        if n >= 2:
            copies[n - 2].wait()
        is_pore = tse(x)[own] == 0.0
        mids = {}
        for d in range(1, 19):
            cx, cy, cz = DIRS[d]
            q = x - cx
            t = tse(q)
            if cy:
                if (cx, cy) not in mids:
                    mids[cx, cy] = pltpu.roll(t, cy % ny, 1)
                t = mids[cx, cy]
            if cz:
                t = pltpu.roll(t, cz % ext, 0)
            both = is_pore & (t[own] == 0.0)
            v = source(d, q)
            if cz:
                v = jnp.where(rowz == (0 if cz > 0 else nz - 1), halo_row(d, q), pltpu.roll(v, cz % nz, 0))
            if cy:
                v = pltpu.roll(v, cy % ny, 1)
            still = jnp.where(is_pore, flow[OPP[d], x], flow[d, x])
            buf[slot, d] = jnp.where(both, v, still)
        buf[slot, 0] = flow[0, x]
        copy = pltpu.make_async_copy(buf.at[slot], out.at[:, x], sems.at[slot])
        copy.start()
        copies.append(copy)
    if not ends:
        whole.wait()
        for n, rows in ((0, slice(0, TILE)), (1, slice(nz - TILE, nz))):
            copies.append(pltpu.make_async_copy(heat_ends.at[n], heat_out.at[5 + n, :, rows, :], heat_sems.at[n]))
            copies[-1].start()
    for copy in copies[-2 if ends else -4 :]:
        copy.wait()


def ring(axis, by):
    count = lax.axis_size(axis)
    return [(i, (i + by) % count) for i in range(count)]


def per_device(populations, heat_pops, solid_temp, conductivity, pore_mask):
    nx, nz, ny = solid_temp.shape
    ext = nz + TILE
    field = (nx, nz, ny)
    flow, hot, tsm, km = call(
        collide_body,
        [(19, *field), (7, *field), field, field],
        [populations, heat_pops, solid_temp, conductivity, pore_mask],
    )
    new_heat, temp, bounce, zmsg = call(
        heat_body,
        [(7, *field), field, (2, nz, ny), (5 * nx + 4, TILE, ny)],
        [hot, flow, tsm, km],
    )
    if lax.axis_size("grp") == 2:
        theirs = lax.ppermute(zmsg, "grp", ring("grp", 1))
    else:
        from_below = lax.ppermute(zmsg, "grp", ring("grp", 1))
        from_above = lax.ppermute(zmsg, "grp", ring("grp", -1))
        upper = lax.broadcasted_iota(jnp.int32, zmsg.shape, 1) < DEEP
        theirs = jnp.where(upper, from_above, from_below)
    heat_ends, low, high, flow_low, flow_high = call(
        zjoin_body,
        [(2, nx, TILE, ny), (14, ext, ny), (14, ext, ny), (5, ext, ny), (5, ext, ny)],
        [zmsg, theirs, temp, hot, tsm, km, bounce, flow, new_heat],
    )
    from_low = lax.ppermute(high, "dev", ring("dev", 1))
    from_high = lax.ppermute(low, "dev", ring("dev", -1))
    flow_from_low = lax.ppermute(flow_high, "dev", ring("dev", 1))
    flow_from_high = lax.ppermute(flow_low, "dev", ring("dev", -1))
    flow_scratch = [pltpu.VMEM((2, 19, nz, ny), jnp.float32), pltpu.SemaphoreType.DMA((2,))]
    new_pops, new_heat = call(
        functools.partial(flow_body, tuple(range(1, nx - 1)), False),
        [(19, *field), (7, *field)],
        [flow, theirs, low, high, new_heat, heat_ends],
        out_specs=[ANY, ANY],
        scratch=flow_scratch + [pltpu.SemaphoreType.DMA((2,))],
        limit=6 << 20,
    )
    planes = nx + 2 * DEEP
    new_heat, new_solid = call(
        conduct_body,
        [(7, *field), field],
        [low, high, from_low, from_high, hot, solid_temp, new_heat],
        in_specs=[VM] * 6 + [ANY],
        out_specs=[ANY, VM],
        scratch=[pltpu.VMEM((planes, ext, ny), jnp.float32)] * 7
        + [pltpu.VMEM((2, nz, ny), jnp.float32), pltpu.SemaphoreType.DMA((2,))],
        aliases={6: 0},
        limit=10 << 20,
    )
    (new_pops,) = call(
        functools.partial(flow_body, (0, nx - 1), True),
        [(19, *field)],
        [flow, theirs, low, high, from_low, from_high, flow_from_low, flow_from_high, new_pops],
        in_specs=[VM] * 8 + [ANY],
        out_specs=[ANY],
        scratch=flow_scratch,
        aliases={8: 0},
        limit=6 << 20,
    )
    return new_pops, new_heat, new_solid


def solution(mesh):
    wide = P(None, "dev", "grp", None)
    flat = P("dev", "grp", None)
    return jax.shard_map(
        per_device,
        mesh=mesh,
        in_specs=(wide, wide, flat, flat, flat),
        out_specs=(wide, wide, flat),
        check_vma=False,
    )
```

time: 153 us -> 48.5 us (0.32)
  the two profiles are of different devices: /device:TPU:0 before, /device:TPU:1 now
where the time goes in v1:
time: 48.5 us; the launch traced here: 48.2 us
  waiting for transfers between devices  18.5 us (38%)
  Pallas kernels  14.4 us (30%)
  starting transfers between devices  7.83 us (16%)
  local copies, waits for them, and re-layouts  6.75 us (14%)
  between operations  0.7 us (1%)
    pallas_call x6, Pallas kernels, call(): pl.pallas_call(body, out_shape=[jax.ShapeDtypeStruct(shape, jnp.float32)...  14.4 us
    ppermute x1, waiting for transfers between devices, per_device(): theirs = lax.ppermute(zmsg, 'grp', ring('grp', 1))  8.14 us
    ppermute x1, waiting for transfers between devices, per_device(): from_low = lax.ppermute(high, 'dev', ring('dev', 1))  7.92 us
    unnamed x10, local copies, waits for them, and re-layouts  6.75 us
    ppermute x1, starting transfers between devices, per_device(): from_low = lax.ppermute(high, 'dev', ring('dev', 1))  2.65 us
    ppermute x1, waiting for transfers between devices, per_device(): from_high = lax.ppermute(low, 'dev', ring('dev', -1))  2.48 us
    ppermute x1, starting transfers between devices, per_device(): theirs = lax.ppermute(zmsg, 'grp', ring('grp', 1))  2.11 us
    ppermute x1, starting transfers between devices, per_device(): flow_from_low = lax.ppermute(flow_high, 'dev', ring('dev', 1))  1.74 us
  transfers between devices with their start and end apart: 5, of which 3 were waited for; matrix products, arithmetic and copies ran while one was open for 0% of the time, Pallas kernels for 19%

profile of v1, /device:TPU:1, one launch (start us, length us, event | category | flops | bytes accessed | tf_op | source)
XLA Modules:
  0.0 48.2 jit_solution(11803002010581855121)
XLA Ops:
  0.6 0.0 copy-start
  0.6 2.4 %copy-done = f32[19,8,32,256]{3,2,1,0:T(8,128)S(1)} copy-done((f32[19,8,32,256]{3,2,1,0:T(8,128)S(1)}, f32[19,8,32,256]{3,2,1,0:T(8,128)}, u32[]{:S(2)}) %copy-start) | copy-done | bytes 4980760
  3.0 0.0 copy-start.1
  3.0 1.5 %copy-done.1 = f32[7,8,32,256]{3,2,1,0:T(8,128)S(1)} copy-done((f32[7,8,32,256]{3,2,1,0:T(8,128)S(1)}, f32[7,8,32,256]{3,2,1,0:T(8,128)}, u32[]{:S(2)}) %copy-start.1) | copy-done | bytes 1835032
  4.5 0.0 copy-start.2
  4.5 0.9 %copy-done.2 = f32[8,32,256]{2,1,0:T(8,128)S(1)} copy-done((f32[8,32,256]{2,1,0:T(8,128)S(1)}, f32[8,32,256]{2,1,0:T(8,128)}, u32[]{:S(2)}) %copy-start.2) | copy-done | bytes 262168
  5.5 0.0 copy-start.3
  5.5 0.9 %copy-done.3 = f32[8,32,256]{2,1,0:T(8,128)S(1)} copy-done((f32[8,32,256]{2,1,0:T(8,128)S(1)}, f32[8,32,256]{2,1,0:T(8,128)}, u32[]{:S(2)}) %copy-start.3) | copy-done | bytes 262168
  6.4 0.0 copy-start.4
  6.4 0.9 %copy-done.4 = s32[8,32,256]{2,1,0:T(8,128)S(1)} copy-done((s32[8,32,256]{2,1,0:T(8,128)S(1)}, s32[8,32,256]{2,1,0:T(8,128)}, u32[]{:S(2)}) %copy-start.4) | copy-done | bytes 262168
  7.4 2.7 %shard_map.76 = (f32[19,8,32,256]{3,2,1,0:T(8,128)S(1)}, f32[7,8,32,256]{3,2,1,0:T(8,128)S(1)}, f32[8,32,256]{2,1,0:T(8,128)S(1)}, f32[8,32,256]{2,1,0:T(8,128)S(1)}) custom-call(f32[19,8,32,256]{3,2,1,0:T(8,128)S(1)} %copy-done, f32[7,8,32,256]{3,2,1,0:T(8,128)S(1)} %copy-done.1, f32[8,32,256]{2,1,0:T(8,128)S(1)} %copy-done.2, f32[8,32,256]{2,1,0:T(8,128)S(1)} %copy-done.3, ...), custom_call_target="tpu_custom_call" | custom-call | tf_op jit(solution)/shard_map/pallas_call | solution.py:55
  10.1 0.8 %shard_map.77 = (f32[7,8,32,256]{3,2,1,0:T(8,128)S(1)}, f32[8,32,256]{2,1,0:T(8,128)S(1)}, f32[2,32,256]{2,1,0:T(8,128)S(1)}, f32[44,8,256]{2,1,0:T(8,128)S(1)}) custom-call(f32[7,8,32,256]{3,2,1,0:T(8,128)S(1)} %get-tuple-element.21.hot, f32[19,8,32,256]{3,2,1,0:T(8,128)S(1)} %get-tuple-element.20.flow.refs_0_, f32[8,32,256]{2,1,0:T(8,128)S(1)} %get-tuple-element.22.tsm, ...), custom_call_target="tpu_custom_call" | custom-call | tf_op jit(solution)/shard_map/pallas_call | solution.py:55
  10.9 2.1 %collective-permute-start = (f32[44,8,256]{2,1,0:T(8,128)S(1)}, f32[44,8,256]{2,1,0:T(8,128)S(1)}, u32[]{:S(2)}, u32[]{:S(2)}) collective-permute-start(f32[44,8,256]{2,1,0:T(8,128)S(1)} %get-tuple-element.24.mine), channel_id=1, source_target_pairs={{0,16},{16,0},{1,17},{17,1},{2,18},{18,2},{3,19},{19,3},{4,20},{20... | collective-permute-start | bytes 1081352 | tf_op jit(solution)/shard_map/ppermute | solution.py:423
  13.0 8.1 %collective-permute-done.theirs.refs_1_ = f32[44,8,256]{2,1,0:T(8,128)S(1)} collective-permute-done((f32[44,8,256]{2,1,0:T(8,128)S(1)}, f32[44,8,256]{2,1,0:T(8,128)S(1)}, u32[]{:S(2)}, u32[]{:S(2)}) %collective-permute-start) | collective-permute-done | bytes 360480 | tf_op jit(solution)/shard_map/ppermute | solution.py:423
  21.1 0.1 shard_map.78
  21.3 2.7 %collective-permute-start.1 = (f32[14,40,256]{2,1,0:T(8,128)S(1)}, f32[14,40,256]{2,1,0:T(8,128)S(1)}, u32[]{:S(2)}, u32[]{:S(2)}) collective-permute-start(f32[14,40,256]{2,1,0:T(8,128)S(1)} %get-tuple-element.29.refs_3_.high), channel_id=1, source_target_pairs={{0,1},{1,2},{2,3},{3,4},{4,5},{5,6},{6,7},{7,8},{8,9},{9,10},{10,1... | collective-permute-start | bytes 1720328 | tf_op jit(solution)/shard_map/ppermute | solution.py:434
  23.9 0.0 collective-permute-start.2
  23.9 1.7 %collective-permute-start.3 = (f32[5,40,256]{2,1,0:T(8,128)S(1)}, f32[5,40,256]{2,1,0:T(8,128)S(1)}, u32[]{:S(2)}, u32[]{:S(2)}) collective-permute-start(f32[5,40,256]{2,1,0:T(8,128)S(1)} %get-tuple-element.30), channel_id=1, source_target_pairs={{0,1},{1,2},{2,3},{3,4},{4,5},{5,6},{6,7},{7,8},{8,9},{9,10},{10,1... | collective-permute-start | bytes 614408 | tf_op jit(solution)/shard_map/ppermute | solution.py:436
  25.7 1.3 %collective-permute-start.4 = (f32[5,40,256]{2,1,0:T(8,128)S(1)}, f32[5,40,256]{2,1,0:T(8,128)S(1)}, u32[]{:S(2)}, u32[]{:S(2)}) collective-permute-start(f32[5,40,256]{2,1,0:T(8,128)S(1)} %get-tuple-element.31), channel_id=1, source_target_pairs={{0,15},{1,0},{2,1},{3,2},{4,3},{5,4},{6,5},{7,6},{8,7},{9,8},{10,9... | collective-permute-start | bytes 614408 | tf_op jit(solution)/shard_map/ppermute | solution.py:437
  27.0 4.0 %shard_map.79 = (f32[19,8,32,256]{3,2,1,0:T(8,128)}, f32[7,8,32,256]{3,2,1,0:T(8,128)}) custom-call(f32[19,8,32,256]{3,2,1,0:T(8,128)S(1)} %get-tuple-element.20.flow.refs_0_, f32[44,8,256]{2,1,0:T(8,128)S(1)} %collective-permute-done.theirs.refs_1_, f32[14,40,256]{2,1,0:T(8,128)S(1)} %get-tuple-element.28.refs_2_.low, ...), custom_call_target="tpu_custom_call" | custom-call | tf_op jit(solution)/shard_map/pallas_call | solution.py:55
  31.0 7.9 %collective-permute-done.1.refs_4_.from_low = f32[14,40,256]{2,1,0:T(8,128)S(1)} collective-permute-done((f32[14,40,256]{2,1,0:T(8,128)S(1)}, f32[14,40,256]{2,1,0:T(8,128)S(1)}, u32[]{:S(2)}, u32[]{:S(2)}) %collective-permute-start.1) | collective-permute-done | bytes 573472 | tf_op jit(solution)/shard_map/ppermute | solution.py:434
  38.9 2.5 %collective-permute-done.2.refs_5_.from_high = f32[14,40,256]{2,1,0:T(8,128)S(1)} collective-permute-done((f32[14,40,256]{2,1,0:T(8,128)S(1)}, f32[14,40,256]{2,1,0:T(8,128)S(1)}, u32[]{:S(2)}, u32[]{:S(2)}) %collective-permute-start.2) | collective-permute-done | bytes 573472 | tf_op jit(solution)/shard_map/ppermute | solution.py:435
  41.4 5.4 %shard_map.81 = (f32[7,8,32,256]{3,2,1,0:T(8,128)}, f32[8,32,256]{2,1,0:T(8,128)}) custom-call(f32[14,40,256]{2,1,0:T(8,128)S(1)} %get-tuple-element.28.refs_2_.low, f32[14,40,256]{2,1,0:T(8,128)S(1)} %get-tuple-element.29.refs_3_.high, f32[14,40,256]{2,1,0:T(8,128)S(1)} %collective-permute-done.1.refs_4_.from_low, ...), custom_call_target="tpu_custom_call", output_to_operand_aliasing={{0}: (6, {})} | custom-call | tf_op jit(solution)/shard_map/pallas_call | solution.py:55
  46.8 0.0 collective-permute-done.3.refs_6_
  46.8 0.0 collective-permute-done.4.refs_7_
  46.8 1.4 %shard_map.80 = f32[19,8,32,256]{3,2,1,0:T(8,128)} custom-call(f32[19,8,32,256]{3,2,1,0:T(8,128)S(1)} %get-tuple-element.20.flow.refs_0_, f32[44,8,256]{2,1,0:T(8,128)S(1)} %collective-permute-done.theirs.refs_1_, f32[14,40,256]{2,1,0:T(8,128)S(1)} %get-tuple-element.28.refs_2_.low, ...), custom_call_target="tpu_custom_call", output_to_operand_aliasing={{}: (8, {})} | custom-call | tf_op jit(solution)/shard_map/pallas_call | solution.py:55
Async XLA Ops:
  0.6 2.4 %copy-start = (f32[19,8,32,256]{3,2,1,0:T(8,128)S(1)}, f32[19,8,32,256]{3,2,1,0:T(8,128)}, u32[]{:S(2)}) copy-start(f32[19,8,32,256]{3,2,1,0:T(8,128)} %pops.1) | copy-start | bytes 14942212
  3.0 1.5 %copy-start.1 = (f32[7,8,32,256]{3,2,1,0:T(8,128)S(1)}, f32[7,8,32,256]{3,2,1,0:T(8,128)}, u32[]{:S(2)}) copy-start(f32[7,8,32,256]{3,2,1,0:T(8,128)} %heat.1) | copy-start | bytes 5505028
  4.5 0.9 %copy-start.2 = (f32[8,32,256]{2,1,0:T(8,128)S(1)}, f32[8,32,256]{2,1,0:T(8,128)}, u32[]{:S(2)}) copy-start(f32[8,32,256]{2,1,0:T(8,128)} %ts.3) | copy-start | bytes 786436
  5.5 0.9 %copy-start.3 = (f32[8,32,256]{2,1,0:T(8,128)S(1)}, f32[8,32,256]{2,1,0:T(8,128)}, u32[]{:S(2)}) copy-start(f32[8,32,256]{2,1,0:T(8,128)} %cond.1) | copy-start | bytes 786436
  6.4 0.9 %copy-start.4 = (s32[8,32,256]{2,1,0:T(8,128)S(1)}, s32[8,32,256]{2,1,0:T(8,128)}, u32[]{:S(2)}) copy-start(s32[8,32,256]{2,1,0:T(8,128)} %pore.1) | copy-start | bytes 786436
  10.9 10.2 %collective-permute-start = (f32[44,8,256]{2,1,0:T(8,128)S(1)}, f32[44,8,256]{2,1,0:T(8,128)S(1)}, u32[]{:S(2)}, u32[]{:S(2)}) collective-permute-start(f32[44,8,256]{2,1,0:T(8,128)S(1)} %get-tuple-element.24.mine), channel_id=1, source_target_pairs={{0,16},{16,0},{1,17},{17,1},{2,18},{18,2},{3,19},{19,3},{4,20},{20... | collective-permute-start | bytes 1081352 | tf_op jit(solution)/shard_map/ppermute | solution.py:423
  21.3 17.6 %collective-permute-start.1 = (f32[14,40,256]{2,1,0:T(8,128)S(1)}, f32[14,40,256]{2,1,0:T(8,128)S(1)}, u32[]{:S(2)}, u32[]{:S(2)}) collective-permute-start(f32[14,40,256]{2,1,0:T(8,128)S(1)} %get-tuple-element.29.refs_3_.high), channel_id=1, source_target_pairs={{0,1},{1,2},{2,3},{3,4},{4,5},{5,6},{6,7},{7,8},{8,9},{9,10},{10,1... | collective-permute-start | bytes 1720328 | tf_op jit(solution)/shard_map/ppermute | solution.py:434
  23.9 17.5 %collective-permute-start.2 = (f32[14,40,256]{2,1,0:T(8,128)S(1)}, f32[14,40,256]{2,1,0:T(8,128)S(1)}, u32[]{:S(2)}, u32[]{:S(2)}) collective-permute-start(f32[14,40,256]{2,1,0:T(8,128)S(1)} %get-tuple-element.28.refs_2_.low), channel_id=1, source_target_pairs={{0,15},{1,0},{2,1},{3,2},{4,3},{5,4},{6,5},{7,6},{8,7},{9,8},{10,9... | collective-permute-start | bytes 1720328 | tf_op jit(solution)/shard_map/ppermute | solution.py:435
  23.9 22.9 %collective-permute-start.3 = (f32[5,40,256]{2,1,0:T(8,128)S(1)}, f32[5,40,256]{2,1,0:T(8,128)S(1)}, u32[]{:S(2)}, u32[]{:S(2)}) collective-permute-start(f32[5,40,256]{2,1,0:T(8,128)S(1)} %get-tuple-element.30), channel_id=1, source_target_pairs={{0,1},{1,2},{2,3},{3,4},{4,5},{5,6},{6,7},{7,8},{8,9},{9,10},{10,1... | collective-permute-start | bytes 614408 | tf_op jit(solution)/shard_map/ppermute | solution.py:436
  25.7 21.1 %collective-permute-start.4 = (f32[5,40,256]{2,1,0:T(8,128)S(1)}, f32[5,40,256]{2,1,0:T(8,128)S(1)}, u32[]{:S(2)}, u32[]{:S(2)}) collective-permute-start(f32[5,40,256]{2,1,0:T(8,128)S(1)} %get-tuple-element.31), channel_id=1, source_target_pairs={{0,15},{1,0},{2,1},{3,2},{4,3},{5,4},{6,5},{7,6},{8,7},{9,8},{10,9... | collective-permute-start | bytes 614408 | tf_op jit(solution)/shard_map/ppermute | solution.py:437

commit v2 on v1

v2 whole, which is shorter than its diff:
```python
import functools

import jax
import jax.numpy as jnp
from jax import lax
from jax.experimental import pallas as pl
from jax.experimental.pallas import tpu as pltpu
from jax.sharding import PartitionSpec as P

ITERS = 4
DIRS = (
    (0, 0, 0),
    (1, 0, 0),
    (-1, 0, 0),
    (0, 1, 0),
    (0, -1, 0),
    (0, 0, 1),
    (0, 0, -1),
    (1, 1, 0),
    (-1, -1, 0),
    (1, -1, 0),
    (-1, 1, 0),
    (1, 0, 1),
    (-1, 0, -1),
    (1, 0, -1),
    (-1, 0, 1),
    (0, 1, 1),
    (0, -1, -1),
    (0, 1, -1),
    (0, -1, 1),
)
OPP = (0, 2, 1, 4, 3, 6, 5, 8, 7, 10, 9, 12, 11, 14, 13, 16, 15, 18, 17)
PAIRS = ((1, 2), (3, 4), (5, 6), (7, 8), (9, 10), (11, 12), (13, 14), (15, 16), (17, 18))
ZPAIRS = ((5, 6), (11, 12), (14, 13), (15, 16), (18, 17))
ZSLOT = {5: (1, 2), 6: (1, 2), 11: (1, 3), 12: (1, 3), 14: (2, 0), 13: (2, 0), 15: (2, 1), 16: (2, 1), 18: (2, 2), 17: (2, 2)}
XHIGH = (1, 7, 9, 11, 13)
XLOW = (2, 8, 10, 12, 14)
W0, W1, W2 = 1.0 / 3.0, 1.0 / 18.0, 1.0 / 36.0
RELAX_FLOW = 0.8
RELAX_HEAT = 0.7
JUMP = 0.3
FILM = 0.5
THETA = 61.0
DELTA = 60.0
WALL_OWN = 0.25 * JUMP
WALL_NEAR = 0.25 * (1.0 - JUMP)
DEEP = 4
TILE = 8

VM = pl.BlockSpec(memory_space=pltpu.VMEM)
ANY = pl.BlockSpec(memory_space=pl.ANY)
HBM = pl.BlockSpec(memory_space=pltpu.HBM)


def call(body, outs, args, in_specs=None, out_specs=None, scratch=(), aliases=None, limit=4 << 20, us=0.5):
    return pl.pallas_call(
        body,
        out_shape=[jax.ShapeDtypeStruct(shape, jnp.float32) for shape in outs],
        in_specs=in_specs or [VM] * len(args),
        out_specs=out_specs or [VM] * len(outs),
        scratch_shapes=list(scratch),
        input_output_aliases=aliases or {},
        compiler_params=pltpu.CompilerParams(vmem_limit_bytes=limit),
        cost_estimate=pl.CostEstimate(flops=0, bytes_accessed=int(us * 3e6), transcendentals=0),
    )(*args)


def rows8(shape):
    return lax.broadcasted_iota(jnp.int32, shape, 0)


def collide_body(*refs):
    sources, (flow, hot, tsm, km, rows_out), held, sems = refs[:5], refs[5:10], refs[10:15], refs[15]
    pops, heat, ts, cond, pore = held
    nx, nz, ny = tsm.shape
    row = rows8((TILE, ny))

    def fetch(n, x):
        if n < 2:
            return pltpu.make_async_copy(sources[n].at[:, x], held[n].at[:, x], sems.at[3 + n * nx + x])
        return pltpu.make_async_copy(sources[n], held[n], sems.at[n - 2])

    for n in (2, 3, 4):
        fetch(n, 0).start()
    for x in range(nx):
        for n in (0, 1):
            fetch(n, x).start()
    for n in (2, 3, 4):
        fetch(n, 0).wait()

    def plane(x, carry):
        is_pore = pore[x] != 0
        for n, (src, dst) in enumerate(((ts, tsm), (cond, km))):
            v = jnp.where(is_pore, 0.0, src[x])
            dst[x] = v
            rows_out[n * nx + x] = edge_tile(v[0:TILE], v[nz - TILE : nz], row)
        for n in (0, 1):
            fetch(n, x).wait()
        return lax.fori_loop(0, nz // TILE, lambda i, c: step(x, i, c), carry)

    def step(x, i, carry):
        rows = pl.ds(pl.multiple_of(i * TILE, TILE), TILE)
        is_pore = tsm[x, rows, :] == 0.0
        p = [pops[d, x, rows, :] for d in range(19)]
        diff = [p[a] - p[b] for a, b in PAIRS]
        rho = p[0]
        for a, b in PAIRS:
            rho = rho + (p[a] + p[b])
        inv = 1.0 / rho
        ux = (diff[0] + diff[3] + diff[4] + diff[5] + diff[6]) * inv
        uy = (diff[1] + diff[3] - diff[4] + diff[7] + diff[8]) * inv
        uz = (diff[2] + diff[5] - diff[6] + diff[7] - diff[8]) * inv
        base = 1.0 - 1.5 * (ux * ux + uy * uy + uz * uz)
        keep = 1.0 - 1.0 / RELAX_FLOW
        flow[0, x, rows, :] = jnp.where(is_pore, (W0 / RELAX_FLOW) * rho * base + keep * p[0], p[0])
        speeds = (ux, uy, uz, ux + uy, ux - uy, ux + uz, ux - uz, uy + uz, uy - uz)
        scaled1 = (W1 / RELAX_FLOW) * rho
        scaled2 = (W2 / RELAX_FLOW) * rho
        for n, (a, b) in enumerate(PAIRS):
            scaled = scaled1 if n < 3 else scaled2
            cu = speeds[n]
            even = scaled * (base + 4.5 * (cu * cu))
            odd = scaled * (3.0 * cu)
            flow[a, x, rows, :] = jnp.where(is_pore, (even + odd) + keep * p[a], p[a])
            flow[b, x, rows, :] = jnp.where(is_pore, (even - odd) + keep * p[b], p[b])
        h = [heat[d, x, rows, :] for d in range(7)]
        temp = h[0] + (h[1] + h[2]) + (h[3] + h[4]) + (h[5] + h[6])
        hkeep = 1.0 - 1.0 / RELAX_HEAT
        hot[0, x, rows, :] = jnp.where(is_pore, (0.25 / RELAX_HEAT) * temp + hkeep * h[0], h[0])
        even = (0.125 / RELAX_HEAT) * temp
        for n in range(3):
            a, b = PAIRS[n]
            odd = even * (4.0 * speeds[n])
            hot[a, x, rows, :] = jnp.where(is_pore, (even + odd) + hkeep * h[a], h[a])
            hot[b, x, rows, :] = jnp.where(is_pore, (even - odd) + hkeep * h[b], h[b])
        return carry

    lax.fori_loop(0, nx, plane, 0)


def edge_tile(low, high, row):
    return jnp.where(row < DEEP, low, high)


def pack_pairs(pairs, row):
    out = None
    for j, (low, high) in enumerate(pairs):
        if j:
            low, high = pltpu.roll(low, j, 0), pltpu.roll(high, TILE - j, 0)
        both = jnp.where(row < DEEP, low, high)
        out = both if out is None else jnp.where((row == j) | (row == TILE - 1 - j), both, out)
    return out


def heat_body(hot, flow, tsm, rows_in, new_heat, temp, bounce, zmsg):
    nx, nz, ny = tsm.shape
    rowz = rows8((nz, ny))
    row = rows8((TILE, ny))
    first, last = slice(0, TILE), slice(nz - TILE, nz)
    for x in range(nx):
        t = tsm[x]
        is_pore = t == 0.0
        g = [hot[d, x] for d in range(7)]
        own = WALL_OWN * (g[0] + (g[1] + g[2]) + (g[3] + g[4]) + (g[5] + g[6]))
        new_heat[0, x] = g[0]
        total = g[0]

        def arrive(d, near, moved):
            return jnp.where(near == 0.0, moved, (own - g[OPP[d]]) + WALL_NEAR * near)

        for d in (1, 2):
            src = x - DIRS[d][0]
            if 0 <= src < nx:
                got = arrive(d, tsm[src], hot[d, src])
                total = total + got
                new_heat[d, x] = jnp.where(is_pore, got, g[d])
            else:
                new_heat[d, x] = g[d]
                bounce[0 if x == 0 else 1] = own - g[OPP[d]]
        for d in (3, 4):
            by = DIRS[d][1] % ny
            got = arrive(d, pltpu.roll(t, by, 1), pltpu.roll(g[d], by, 1))
            total = total + got
            new_heat[d, x] = jnp.where(is_pore, got, g[d])
        for d in (5, 6):
            by = DIRS[d][2] % nz
            got = arrive(d, pltpu.roll(t, by, 0), pltpu.roll(g[d], by, 0))
            inside = rowz != (0 if d == 5 else nz - 1)
            total = total + jnp.where(inside, got, 0.0)
            new_heat[d, x] = jnp.where(is_pore & inside, got, g[d])
        total = jnp.where(is_pore, total, 0.0)
        temp[x] = total
        zmsg[x] = edge_tile(total[first], total[last], row)
        pairs = [(g[6][first], g[5][last]), ((own - g[6])[first], (own - g[5])[last])]
        for up, down in ZPAIRS:
            pairs.append((flow[down, x, first, :], flow[up, x, last, :]))
        zmsg[nx + x] = pack_pairs(pairs[:4], row)
        zmsg[2 * nx + x] = pack_pairs(pairs[4:], row)
    ends = (hot[2, 0], hot[1, nx - 1], bounce[0], bounce[1])
    for n, v in enumerate(ends):
        zmsg[3 * nx + n] = edge_tile(v[first], v[last], row)
    zmsg[3 * nx + 4 :] = rows_in[...]


def put_plane(out, n, v):
    tiles = v.shape[0] // TILE
    for i in range(tiles):
        out[n + i] = v[i * TILE : (i + 1) * TILE]
    return n + tiles


def get_plane(ref, n, tiles):
    return ref[n : n + tiles].reshape(tiles * TILE, ref.shape[-1])


def early_body(tsm, km, flow, after, low, high):
    nx = tsm.shape[0]
    for side, out in ((0, low), (1, high)):
        n = 0
        for field in (tsm, km):
            for x in range(side * (nx - DEEP), side * (nx - DEEP) + DEEP):
                n = put_plane(out, n, field[x])
        for d in (XLOW, XHIGH)[side]:
            n = put_plane(out, n, flow[d, side * (nx - 1)])


def zjoin_body(mine, theirs, temp, hot, bounce, heat_in, after, heat_ends, low, high):
    nx, nz, ny = temp.shape
    row = rows8((TILE, ny))
    edge = (row == 0) | (row == TILE - 1)
    first, last = slice(0, TILE), slice(nz - TILE, nz)

    def swap(v):
        return jnp.where(row < DEEP, pltpu.roll(v, 1, 0), pltpu.roll(v, TILE - 1, 0))

    def slot1(v):
        return jnp.where(row < DEEP, pltpu.roll(v, TILE - 1, 0), pltpu.roll(v, 1, 0))

    at = [0, 0]
    for x in range(nx):
        my_t, their_t = mine[3 * nx + 4 + x], theirs[3 * nx + 4 + x]
        my_p, their_p = mine[nx + x], theirs[nx + x]
        near = swap(their_t)
        got = jnp.where(near == 0.0, swap(their_p), slot1(my_p) + WALL_NEAR * near)
        mine_in = edge & (my_t == 0.0)
        add = jnp.where(mine_in, got, 0.0)
        near = swap(my_t)
        back = jnp.where(near == 0.0, swap(my_p), slot1(their_p) + WALL_NEAR * near)
        back = jnp.where(edge & (their_t == 0.0), back, 0.0)
        heat_ends[0, x] = jnp.where(mine_in & (row == 0), got, heat_in[5, x, first, :])
        heat_ends[1, x] = jnp.where(mine_in & (row == TILE - 1), got, heat_in[6, x, last, :])
        for side, out in ((0, low), (1, high)):
            if side * (nx - DEEP) <= x < side * (nx - DEEP) + DEEP:
                n = at[side]
                out[n] = temp[x, first, :] + jnp.where(row == 0, add, 0.0)
                n = put_plane(out, n + 1, temp[x, TILE : nz - TILE, :])
                out[n] = temp[x, last, :] + jnp.where(row == TILE - 1, add, 0.0)
                out[n + 1] = theirs[x] + back
                at[side] = n + 2
    for side, out in ((0, low), (1, high)):
        x = side * (nx - 1)
        n = put_plane(out, at[side], hot[2 - side, x])
        out[n] = theirs[3 * nx + side]
        n = put_plane(out, n + 1, bounce[side])
        out[n] = theirs[3 * nx + 2 + side]
        a, b = theirs[nx + x], theirs[2 * nx + x]
        if side:
            out[n + 1] = jnp.where(row < DEEP, b, pltpu.roll(a, 3, 0))
        else:
            out[n + 1] = jnp.where(row < DEEP, pltpu.roll(a, TILE - 3, 0), b)
        for f in range(2):
            base = 3 * nx + 4 + f * nx + side * (nx - DEEP)
            out[n + 2 + f * DEEP : n + 2 + (f + 1) * DEEP] = theirs[base : base + DEEP]


def reader(nx, early, late, fields, rows):
    tiles = fields[0].shape[1] // TILE
    corner = (DEEP + 2) * (tiles + 1) + 1

    def core(f, p):
        if DEEP <= p < DEEP + nx:
            return fields[f][p - DEEP]
        side, n = (0, p) if p < DEEP else (1, p - DEEP - nx)
        return get_plane(early[side], (f * DEEP + n) * tiles, tiles)

    def halo(f, p):
        if DEEP <= p < DEEP + nx:
            return rows[3 * nx + 4 + f * nx + p - DEEP]
        side, n = (0, p) if p < DEEP else (1, p - DEEP - nx)
        return late[side][corner + f * DEEP + n]

    def whole(f, p):
        return jnp.concatenate([core(f, p), halo(f, p)], axis=0)

    return core, halo, whole


def face(a, b):
    return (2.0 * a) * b / jnp.maximum(a + b, 1.0)


def still_plane(whole, p, fx_low, fx_high):
    k, t = whole(1, p), whole(0, p)
    ext, ny = k.shape
    ky = pltpu.roll(k, 1, 1)
    kz = pltpu.roll(k, 1, 0)
    gy, gz = face(k, ky), face(k, kz)
    pore = jnp.where(k == 0.0, 1.0, 0.0)
    count = jnp.where(ky == 0.0, 1.0, 0.0) + jnp.where(kz == 0.0, 1.0, 0.0)
    count = count + pltpu.roll(pore, ny - 1, 1) + pltpu.roll(pore, ext - 1, 0)
    count = count + jnp.where(whole(1, p - 1) == 0.0, 1.0, 0.0) + jnp.where(whole(1, p + 1) == 0.0, 1.0, 0.0)
    flux_y = gy * (pltpu.roll(t, 1, 1) - t)
    flux_z = gz * (pltpu.roll(t, 1, 0) - t)
    net = fx_low * (whole(0, p - 1) - t) - fx_high * (t - whole(0, p + 1))
    net = net + (flux_y - pltpu.roll(flux_y, ny - 1, 1))
    net = net + (flux_z - pltpu.roll(flux_z, ext - 1, 0))
    return gy, gz, net - FILM * count * t


def static_body(tsm, km, theirs, fx, fy, fz, still):
    nx = tsm.shape[0]
    _, _, whole = reader(nx, None, None, (tsm, km), theirs)
    first = DEEP + 1
    for n in range(nx - 1):
        fx[n] = face(whole(1, first + n), whole(1, first + n - 1))
    for n in range(nx - 2):
        fy[n], fz[n], still[n] = still_plane(whole, first + n, fx[n], fx[n + 1])


def conduct_body(*all_refs):
    early_low, early_high, from_low, low, high, from_high, theirs = all_refs[0:7]
    in_fx, in_fy, in_fz, in_still, tsm, km, hot, ts, corners, heat_in, pops_in, new_heat, new_pops, new_solid = all_refs[7:21]
    temp, resid, step_a, step_b, fx, fy, fz, still, ends, patched, sems = all_refs[21:]
    nx, nz, ny = ts.shape
    planes, ext = temp.shape[:2]
    tiles = ext // TILE
    own = slice(0, nz)
    late = (from_low, low, high, from_high)
    core, halo, whole = reader(nx, (early_low, early_high), (from_low, from_high), (tsm, km), theirs)

    def ready(p):
        return DEEP < p < DEEP + nx - 1

    def fx_at(p):
        return in_fx[p - DEEP - 1] if DEEP < p < DEEP + nx else fx[p]

    def fy_at(p):
        return in_fy[p - DEEP - 1] if ready(p) else fy[p]

    def fz_at(p):
        return in_fz[p - DEEP - 1] if ready(p) else fz[p]

    def still_at(p):
        return in_still[p - DEEP - 1] if ready(p) else still[p]

    def ts_at(p):
        return whole(0, p)

    def temp_at(p):
        ref, n = ((from_low, p), (low, p - DEEP), (high, p - nx), (from_high, p - DEEP - nx))[p // DEEP]
        return get_plane(ref, n * tiles, tiles)

    def out_of(ref):
        return get_plane(ref, DEEP * tiles, tiles)

    def bounce_of(ref):
        return get_plane(ref, (DEEP + 1) * tiles, tiles)

    def join(below, above, p_low, p_high):
        t_low, t_high = ts_at(p_low), ts_at(p_high)
        up = jnp.where(t_low == 0.0, out_of(below), bounce_of(above) + WALL_NEAR * t_low)
        down = jnp.where(t_high == 0.0, out_of(above), bounce_of(below) + WALL_NEAR * t_high)
        temp[p_high] = jnp.where(t_high == 0.0, temp_at(p_high) + up, 0.0)
        temp[p_low] = jnp.where(t_low == 0.0, temp_at(p_low) + down, 0.0)
        return up, down

    row = rows8((TILE, ny))
    corner = (DEEP + 2) * tiles
    copies = []
    for n, (d, x, p, ref) in enumerate(
        (
            (11, 0, DEEP - 1, from_low),
            (13, 0, DEEP - 1, from_low),
            (12, nx - 1, DEEP + nx, from_high),
            (14, nx - 1, DEEP + nx, from_high),
        )
    ):
        by, at, rows = (1, 0, slice(0, TILE)) if DIRS[d][2] > 0 else (TILE - 1, TILE - 1, slice(nz - TILE, nz))
        there = pltpu.roll(halo(0, p), by, 0)
        both = (row == at) & (tsm[x, rows, :] == 0.0) & (there == 0.0)
        patched[n] = jnp.where(both, pltpu.roll(ref[corner], by, 0), corners[n])
        copies.append(pltpu.make_async_copy(patched.at[n], new_pops.at[d, x, rows, :], sems.at[n]))
        copies[-1].start()
    for p in range(1, planes - 1):
        if p not in (DEEP - 1, DEEP, DEEP + nx - 1, DEEP + nx):
            temp[p] = temp_at(p)
    temp[0] = temp_at(0)
    temp[planes - 1] = temp_at(planes - 1)
    up, _ = join(from_low, low, DEEP - 1, DEEP)
    _, down = join(high, from_high, DEEP + nx - 1, DEEP + nx)
    ends[0] = jnp.where(tsm[0] == 0.0, up[own], hot[1, 0])
    ends[1] = jnp.where(tsm[nx - 1] == 0.0, down[own], hot[2, nx - 1])
    for n, (d, x) in enumerate(((1, 0), (2, nx - 1))):
        copies.append(pltpu.make_async_copy(ends.at[n], new_heat.at[d, x], sems.at[4 + n]))
        copies[-1].start()

    for p in range(1, planes):
        if not DEEP < p < DEEP + nx:
            fx[p] = face(whole(1, p), whole(1, p - 1))
    for p in range(1, planes - 1):
        if not ready(p):
            fy[p], fz[p], still[p] = still_plane(whole, p, fx_at(p), fx_at(p + 1))
    for p in range(1, planes - 1):
        mid = temp[p]
        near = (temp[p - 1] + temp[p + 1]) + (pltpu.roll(mid, 1, 1) + pltpu.roll(mid, ny - 1, 1))
        near = near + (pltpu.roll(mid, 1, 0) + pltpu.roll(mid, ext - 1, 0))
        r = jnp.where(ts_at(p) == 0.0, 0.0, FILM * near) + still_at(p)
        resid[p] = r
        s = r * (1.0 / THETA)
        step_a[p] = s
        if DEEP <= p < DEEP + nx:
            new_solid[p - DEEP] = ts[p - DEEP] + s[own]
    sigma = THETA / DELTA
    ratio = 1.0 / sigma
    now, later = step_a, step_b
    for sweep in range(1, ITERS):
        after = 1.0 / (2.0 * sigma - ratio)
        start = 1 + sweep
        below = fx_at(start) * (now[start - 1] - now[start])
        for p in range(start, planes - start):
            v = now[p]
            flux_y = fy_at(p) * (pltpu.roll(v, 1, 1) - v)
            flux_z = fz_at(p) * (pltpu.roll(v, 1, 0) - v)
            above = fx_at(p + 1) * (v - now[p + 1])
            net = (below - above) + (flux_y - pltpu.roll(flux_y, ny - 1, 1))
            net = net + (flux_z - pltpu.roll(flux_z, ext - 1, 0))
            below = above
            r = resid[p] - (v - net)
            s = (after * ratio) * v + (2.0 * after / DELTA) * r
            if sweep + 1 < ITERS:
                resid[p] = r
                later[p] = s
            if DEEP <= p < DEEP + nx:
                new_solid[p - DEEP] = new_solid[p - DEEP] + s[own]
        ratio = after
        now, later = later, now
    for copy in copies:
        copy.wait()


FLOW_DIRS = (
    (0, 1, 2, 3, 4, 7, 8, 9, 10),
    (5, 6, 11, 12, 13, 14, 15, 16, 17, 18),
    tuple(range(19)),
)
FLOW_RUNS = (((0, 5), (7, 4)), ((5, 2), (11, 8)), ((0, 19),))


def flow_body(part, *all_refs):
    early = late = theirs = None
    if part == 0:
        flow, tsm, out, done, buf, sems = all_refs
    elif part == 1:
        flow, tsm, theirs, heat, heat_ends, held, out, heat_out, buf, sems, heat_sems = all_refs
    else:
        flow, tsm, theirs, early_low, early_high, held, out, corners, buf, sems = all_refs
        early = (early_low, early_high)
    nx, nz, ny = flow.shape[1:]
    tiles = nz // TILE
    ext = nz + TILE
    rowz = rows8((nz, ny))
    core, _, whole = reader(nx, early, None, (tsm, None), theirs)
    if part == 1:
        copy_heat = pltpu.make_async_copy(heat, heat_out, heat_sems.at[0])
        copy_heat.start()

    def source(d, q):
        if 0 <= q < nx:
            return flow[d, q]
        ref, n = (early_low, XHIGH.index(d)) if q < 0 else (early_high, XLOW.index(d))
        return get_plane(ref, (2 * DEEP + n) * tiles, tiles)

    copies = []
    for at, x in enumerate(range(1, nx - 1) if part < 2 else (0, nx - 1)):
        slot = at % 2
        if at >= 2:
            for copy in copies[at - 2]:
                copy.wait()
        is_pore = tsm[x] == 0.0
        turned = {}
        for at_d, d in enumerate(FLOW_DIRS[part]):
            if d == 0:
                buf[slot, at_d] = flow[0, x]
                continue
            cx, cy, cz = DIRS[d]
            q = x - cx
            inside = 0 <= q < nx
            tall = bool(cz) and inside
            if (cx, cy, tall) not in turned:
                t = (whole if tall else core)(0, q + DEEP)
                turned[cx, cy, tall] = pltpu.roll(t, cy % ny, 1) if cy else t
            t = turned[cx, cy, tall]
            if cz:
                t = pltpu.roll(t, cz % t.shape[0], 0)
            both = is_pore & (t[0:nz] == 0.0)
            v = source(d, q)
            if cz:
                at_end = rowz == (0 if cz > 0 else nz - 1)
                v = pltpu.roll(v, cz % nz, 0)
                if inside:
                    block, j = ZSLOT[d]
                    n = TILE - 1 - j if cz > 0 else j
                    v = jnp.where(at_end, theirs[block * nx + q, n : n + 1, :], v)
                else:
                    both = both & ~at_end
            if cy:
                v = pltpu.roll(v, cy % ny, 1)
            v = jnp.where(both, v, jnp.where(is_pore, flow[OPP[d], x], flow[d, x]))
            buf[slot, at_d] = v
            if cz and not inside:
                corners[(11, 13, 12, 14).index(d)] = v[0:TILE] if cz > 0 else v[nz - TILE : nz]
        begin = 0
        copies.append([])
        for n, (d, count) in enumerate(FLOW_RUNS[part]):
            src, dst = buf.at[slot, begin : begin + count], out.at[d : d + count, x]
            copies[-1].append(pltpu.make_async_copy(src, dst, sems.at[2 * slot + n]))
            copies[-1][-1].start()
            begin += count
    if part == 0:
        done[...] = jnp.zeros(done.shape, jnp.float32)
    if part == 1:
        copy_heat.wait()
        for n, rows in ((0, slice(0, TILE)), (1, slice(nz - TILE, nz))):
            copy = pltpu.make_async_copy(heat_ends.at[n], heat_out.at[5 + n, :, rows, :], heat_sems.at[n])
            copy.start()
            copies[-1].append(copy)
    for group in copies[-2:]:
        for copy in group:
            copy.wait()


def ring(axis, by):
    count = lax.axis_size(axis)
    return [(i, (i + by) % count) for i in range(count)]


def along_z(rows):
    if lax.axis_size("grp") == 2:
        return lax.ppermute(rows, "grp", ring("grp", 1))
    from_below = lax.ppermute(rows, "grp", ring("grp", 1))
    from_above = lax.ppermute(rows, "grp", ring("grp", -1))
    upper = lax.broadcasted_iota(jnp.int32, rows.shape, 1) < DEEP
    return jnp.where(upper, from_above, from_below)


def along_x(low, high):
    return lax.ppermute(high, "dev", ring("dev", 1)), lax.ppermute(low, "dev", ring("dev", -1))


def per_device(populations, heat_pops, solid_temp, conductivity, pore_mask):
    nx, nz, ny = solid_temp.shape
    ext = nz + TILE
    tiles = ext // TILE
    planes = nx + 2 * DEEP
    field = (nx, nz, ny)
    wide = (planes, ext, ny)
    dma = pltpu.SemaphoreType.DMA
    flow, hot, tsm, km, my_rows = call(
        collide_body,
        [(19, *field), (7, *field), field, field, (2 * nx, TILE, ny)],
        [pltpu.with_memory_space_constraint(v, pltpu.HBM) for v in (populations, heat_pops, solid_temp, conductivity, pore_mask)],
        in_specs=[HBM] * 5,
        scratch=[
            pltpu.VMEM((19, *field), jnp.float32),
            pltpu.VMEM((7, *field), jnp.float32),
            pltpu.VMEM(field, jnp.float32),
            pltpu.VMEM(field, jnp.float32),
            pltpu.VMEM(field, jnp.int32),
            dma((3 + 2 * nx,)),
        ],
        limit=12 << 20,
        us=4,
    )
    new_heat, temp, bounce, zmsg = call(
        heat_body,
        [(7, *field), field, (2, nz, ny), (5 * nx + 4, TILE, ny)],
        [hot, flow, tsm, my_rows],
    )
    theirs = along_z(zmsg)
    early_shape = ((2 * DEEP + len(XLOW)) * (tiles - 1), TILE, ny)
    early_low, early_high = call(early_body, [early_shape] * 2, [tsm, km, flow, bounce])
    early_low, early_high = along_x(early_low, early_high)

    def flow_call(part, outs, args, out_specs, in_hbm=0, extra=(), **rest):
        held = (2, len(FLOW_DIRS[part]), nz, ny)
        return call(
            functools.partial(flow_body, part),
            outs,
            args,
            in_specs=[VM] * (len(args) - in_hbm) + [ANY] * in_hbm,
            out_specs=out_specs,
            scratch=[pltpu.VMEM(held, jnp.float32), dma((4,)), *extra],
            limit=6 << 20,
            **rest,
        )

    pops_shape, heat_shape = (19, *field), (7, *field)
    new_pops, after = flow_call(0, [pops_shape, (TILE, 128)], [flow, tsm], [ANY, VM], us=20)
    late_shape = ((DEEP + 2) * tiles + 1 + 2 * DEEP, TILE, ny)
    heat_ends, low, high = call(
        zjoin_body,
        [(2, nx, TILE, ny), late_shape, late_shape],
        [zmsg, theirs, temp, hot, bounce, new_heat, after],
    )
    from_low, from_high = along_x(low, high)
    new_pops, new_heat = flow_call(
        1,
        [pops_shape, heat_shape],
        [flow, tsm, theirs, new_heat, heat_ends, new_pops],
        [ANY, ANY],
        in_hbm=1,
        extra=[dma((2,))],
        aliases={5: 0},
        us=20,
    )
    new_pops, corners = flow_call(
        2,
        [pops_shape, (4, TILE, ny)],
        [flow, tsm, theirs, early_low, early_high, new_pops],
        [ANY, VM],
        in_hbm=1,
        aliases={5: 0},
    )
    fx, fy, fz, still = call(
        static_body,
        [(nx - 1, ext, ny)] + [(nx - 2, ext, ny)] * 3,
        [tsm, km, theirs],
    )
    new_heat, new_pops, new_solid = call(
        conduct_body,
        [heat_shape, pops_shape, field],
        [early_low, early_high, from_low, low, high, from_high, theirs]
        + [fx, fy, fz, still, tsm, km, hot, solid_temp, corners, new_heat, new_pops],
        in_specs=[VM] * 16 + [ANY] * 2,
        out_specs=[ANY, ANY, VM],
        scratch=[pltpu.VMEM(wide, jnp.float32)] * 8
        + [pltpu.VMEM((2, nz, ny), jnp.float32), pltpu.VMEM((4, TILE, ny), jnp.float32), dma((6,))],
        aliases={16: 0, 17: 1},
        limit=10 << 20,
        us=4,
    )
    return new_pops, new_heat, new_solid


def solution(mesh):
    wide = P(None, "dev", "grp", None)
    flat = P("dev", "grp", None)
    return jax.shard_map(
        per_device,
        mesh=mesh,
        in_specs=(wide, wide, flat, flat, flat),
        out_specs=(wide, wide, flat),
        check_vma=False,
    )
```

time: 48.5 us -> 34 us (0.70)
  waiting for transfers between devices: 18.5 us -> 7.94 us
  local copies, waits for them, and re-layouts: 6.75 us -> 0.01 us
  Pallas kernels: 14.4 us -> 18.3 us
  starting transfers between devices: 7.83 us -> 6.9 us
    ppermute x5, waiting for transfers between devices: 18.5 us -> 7.94 us  [the longest x1 3.07 us: along_z(): return lax.ppermute(rows, 'grp', ring('grp', 1))]
    unnamed x10 -> x2, local copies, waits for them, and re-layouts: 6.75 us -> 0.01 us
    pallas_call x6 -> x9, Pallas kernels: 14.4 us -> 18.3 us  [call(): pl.pallas_call(body, out_shape=[jax.ShapeDtypeStruct(shape, jnp.float32)...]
    ppermute x5, starting transfers between devices: 7.83 us -> 6.9 us  [the longest x2 4.79 us: along_x(): lax.ppermute(high, 'dev', ring('dev', 1))]
  transfers between devices with their start and end apart: 5 -> 5, of which waited for: 3 -> 3; matrix products, arithmetic and copies ran while one was open for 0% -> 0% of each run, Pallas kernels for 19% -> 25%
where the time goes in v2:
time: 34 us; the launch traced here: 33.8 us
  Pallas kernels  18.3 us (54%)
  waiting for transfers between devices  7.94 us (23%)
  starting transfers between devices  6.9 us (20%)
  between operations  0.71 us (2%)
    pallas_call x9, Pallas kernels, call(): pl.pallas_call(body, out_shape=[jax.ShapeDtypeStruct(shape, jnp.float32)...  18.3 us
    ppermute x2, starting transfers between devices, along_x(): lax.ppermute(high, 'dev', ring('dev', 1))  4.79 us
    ppermute x1, waiting for transfers between devices, along_z(): return lax.ppermute(rows, 'grp', ring('grp', 1))  3.07 us
    ppermute x2, waiting for transfers between devices, along_x(): lax.ppermute(low, 'dev', ring('dev', -1))  2.48 us
    ppermute x2, waiting for transfers between devices, along_x(): lax.ppermute(high, 'dev', ring('dev', 1))  2.39 us
    ppermute x1, starting transfers between devices, along_z(): return lax.ppermute(rows, 'grp', ring('grp', 1))  2.11 us
  transfers between devices with their start and end apart: 5, of which 3 were waited for; matrix products, arithmetic and copies ran while one was open for 0% of the time, Pallas kernels for 25%

profile of v2, /device:TPU:1, one launch (start us, length us, event | category | flops | bytes accessed | tf_op | source)
XLA Modules:
  0.0 33.8 jit_solution(9782698559533634277)
XLA Ops:
  0.6 4.2 %shard_map.76 = (f32[19,8,32,256]{3,2,1,0:T(8,128)S(1)}, f32[7,8,32,256]{3,2,1,0:T(8,128)S(1)}, f32[8,32,256]{2,1,0:T(8,128)S(1)}, f32[8,32,256]{2,1,0:T(8,128)S(1)}, f32[16,8,256]{2,1,0:T(8,128)S(1)}) custom-call(f32[19,8,32,256]{3,2,1,0:T(8,128)} %refs_0_.1, f32[7,8,32,256]{3,2,1,0:T(8,128)} %refs_1_.1, f32[8,32,256]{2,1,0:T(8,128)} %all_refs_14_.1, ...), custom_call_target="tpu_custom_call" | custom-call | bytes 12000000 | tf_op jit(solution)/shard_map/pallas_call | solution.py:56
  4.8 0.8 %shard_map.77 = (f32[7,8,32,256]{3,2,1,0:T(8,128)S(1)}, f32[8,32,256]{2,1,0:T(8,128)S(1)}, f32[2,32,256]{2,1,0:T(8,128)S(1)}, f32[44,8,256]{2,1,0:T(8,128)S(1)}) custom-call(f32[7,8,32,256]{3,2,1,0:T(8,128)S(1)} %get-tuple-element.33.hot.all_refs_13_, f32[19,8,32,256]{3,2,1,0:T(8,128)S(1)} %get-tuple-element.32.flow.all_refs_0_, ...), custom_call_target="tpu_custom_call" | custom-call | bytes 1500000 | tf_op jit(solution)/shard_map/pallas_call | solution.py:56
  5.6 2.1 %collective-permute-start.2 = (f32[44,8,256]{2,1,0:T(8,128)S(1)}, f32[44,8,256]{2,1,0:T(8,128)S(1)}, u32[]{:S(2)}, u32[]{:S(2)}) collective-permute-start(f32[44,8,256]{2,1,0:T(8,128)S(1)} %get-tuple-element.38.mine), channel_id=1, source_target_pairs={{0,16},{16,0},{1,17},{17,1},{2,18},{18,2},{3,19},{19,3},{4,20},{20... | collective-permute-start | bytes 1081352 | tf_op jit(solution)/shard_map/ppermute | solution.py:549
  7.8 0.1 shard_map.78
  7.8 2.1 %collective-permute-start = (f32[52,8,256]{2,1,0:T(8,128)S(1)}, f32[52,8,256]{2,1,0:T(8,128)S(1)}, u32[]{:S(2)}, u32[]{:S(2)}) collective-permute-start(f32[52,8,256]{2,1,0:T(8,128)S(1)} %get-tuple-element.36), channel_id=1, source_target_pairs={{0,1},{1,2},{2,3},{3,4},{4,5},{5,6},{6,7},{7,8},{8,9},{9,10},{10,1... | collective-permute-start | bytes 1277960 | tf_op jit(solution)/shard_map/ppermute | solution.py:557
  9.9 0.0 collective-permute-start.1
  10.0 2.9 %shard_map.79 = (f32[19,8,32,256]{3,2,1,0:T(8,128)}, f32[8,128]{1,0:T(8,128)S(1)}) custom-call(f32[19,8,32,256]{3,2,1,0:T(8,128)S(1)} %get-tuple-element.32.flow.all_refs_0_, f32[8,32,256]{2,1,0:T(8,128)S(1)} %get-tuple-element.30.tsm.all_refs_1_.all_refs_11_), custom_call_target="tpu_custom_call" | custom-call | bytes 60000000 | tf_op jit(solution)/shard_map/pallas_call | solution.py:56
  12.8 3.1 %collective-permute-done.2.theirs.all_refs_2_.all_refs_6_ = f32[44,8,256]{2,1,0:T(8,128)S(1)} collective-permute-done((f32[44,8,256]{2,1,0:T(8,128)S(1)}, f32[44,8,256]{2,1,0:T(8,128)S(1)}, u32[]{:S(2)}, u32[]{:S(2)}) %collective-permute-start.2) | collective-permute-done | bytes 360480 | tf_op jit(solution)/shard_map/ppermute | solution.py:549
  15.9 0.1 shard_map.80
  16.0 2.7 %collective-permute-start.3 = (f32[39,8,256]{2,1,0:T(8,128)S(1)}, f32[39,8,256]{2,1,0:T(8,128)S(1)}, u32[]{:S(2)}, u32[]{:S(2)}) collective-permute-start(f32[39,8,256]{2,1,0:T(8,128)S(1)} %get-tuple-element.42.all_refs_4_), channel_id=1, source_target_pairs={{0,1},{1,2},{2,3},{3,4},{4,5},{5,6},{6,7},{7,8},{8,9},{9,10},{10,1... | collective-permute-start | bytes 958472 | tf_op jit(solution)/shard_map/ppermute | solution.py:557
  18.6 0.0 collective-permute-start.4
  18.7 0.6 %shard_map.81 = (f32[7,40,256]{2,1,0:T(8,128)S(1)}, f32[6,40,256]{2,1,0:T(8,128)S(1)}, f32[6,40,256]{2,1,0:T(8,128)S(1)}, f32[6,40,256]{2,1,0:T(8,128)S(1)}) custom-call(f32[8,32,256]{2,1,0:T(8,128)S(1)} %get-tuple-element.30.tsm.all_refs_1_.all_refs_11_, f32[8,32,256]{2,1,0:T(8,128)S(1)} %get-tuple-element.31.km.all_refs_12_, ...), custom_call_target="tpu_custom_call" | custom-call | bytes 1500000 | tf_op jit(solution)/shard_map/pallas_call | solution.py:56
  19.3 3.3 %shard_map.82 = (f32[19,8,32,256]{3,2,1,0:T(8,128)}, f32[7,8,32,256]{3,2,1,0:T(8,128)}) custom-call(f32[19,8,32,256]{3,2,1,0:T(8,128)S(1)} %get-tuple-element.32.flow.all_refs_0_, f32[8,32,256]{2,1,0:T(8,128)S(1)} %get-tuple-element.30.tsm.all_refs_1_.all_refs_11_, ...), custom_call_target="tpu_custom_call", output_to_operand_aliasing={{0}: (5, {})} | custom-call | bytes 60000000 | tf_op jit(solution)/shard_map/pallas_call | solution.py:56
  22.6 0.0 collective-permute-done.all_refs_3_.all_refs_0_
  22.6 0.0 collective-permute-done.1.all_refs_4_.all_refs_1_
  22.6 0.0 copy-start
  22.6 1.4 %shard_map.83 = (f32[19,8,32,256]{3,2,1,0:T(8,128)}, f32[4,8,256]{2,1,0:T(8,128)S(1)}) custom-call(f32[19,8,32,256]{3,2,1,0:T(8,128)S(1)} %get-tuple-element.32.flow.all_refs_0_, f32[8,32,256]{2,1,0:T(8,128)S(1)} %get-tuple-element.30.tsm.all_refs_1_.all_refs_11_, ...), custom_call_target="tpu_custom_call", output_to_operand_aliasing={{0}: (5, {})} | custom-call | bytes 1500000 | tf_op jit(solution)/shard_map/pallas_call | solution.py:56
  24.0 2.4 %collective-permute-done.3.all_refs_2_ = f32[39,8,256]{2,1,0:T(8,128)S(1)} collective-permute-done((f32[39,8,256]{2,1,0:T(8,128)S(1)}, f32[39,8,256]{2,1,0:T(8,128)S(1)}, u32[]{:S(2)}, u32[]{:S(2)}) %collective-permute-start.3) | collective-permute-done | bytes 319520 | tf_op jit(solution)/shard_map/ppermute | solution.py:557
  26.4 2.5 %collective-permute-done.4.all_refs_5_ = f32[39,8,256]{2,1,0:T(8,128)S(1)} collective-permute-done((f32[39,8,256]{2,1,0:T(8,128)S(1)}, f32[39,8,256]{2,1,0:T(8,128)S(1)}, u32[]{:S(2)}, u32[]{:S(2)}) %collective-permute-start.4) | collective-permute-done | bytes 319520 | tf_op jit(solution)/shard_map/ppermute | solution.py:557
  28.9 0.0 copy-done
  28.9 4.9 %shard_map.84 = (f32[7,8,32,256]{3,2,1,0:T(8,128)}, f32[19,8,32,256]{3,2,1,0:T(8,128)}, f32[8,32,256]{2,1,0:T(8,128)}) custom-call(f32[52,8,256]{2,1,0:T(8,128)S(1)} %collective-permute-done.all_refs_3_.all_refs_0_, f32[52,8,256]{2,1,0:T(8,128)S(1)} %collective-permute-done.1.all_refs_4_.all_refs_1_, ...), custom_call_target="tpu_custom_call", output_to_operand_aliasing={{0}: (16, {}), {1}: (17, {})} | custom-call | bytes 12000000 | tf_op jit(solution)/shard_map/pallas_call | solution.py:56
Async XLA Ops:
  5.6 10.2 %collective-permute-start.2 = (f32[44,8,256]{2,1,0:T(8,128)S(1)}, f32[44,8,256]{2,1,0:T(8,128)S(1)}, u32[]{:S(2)}, u32[]{:S(2)}) collective-permute-start(f32[44,8,256]{2,1,0:T(8,128)S(1)} %get-tuple-element.38.mine), channel_id=1, source_target_pairs={{0,16},{16,0},{1,17},{17,1},{2,18},{18,2},{3,19},{19,3},{4,20},{20... | collective-permute-start | bytes 1081352 | tf_op jit(solution)/shard_map/ppermute | solution.py:549
  7.8 14.7 %collective-permute-start = (f32[52,8,256]{2,1,0:T(8,128)S(1)}, f32[52,8,256]{2,1,0:T(8,128)S(1)}, u32[]{:S(2)}, u32[]{:S(2)}) collective-permute-start(f32[52,8,256]{2,1,0:T(8,128)S(1)} %get-tuple-element.36), channel_id=1, source_target_pairs={{0,1},{1,2},{2,3},{3,4},{4,5},{5,6},{6,7},{7,8},{8,9},{9,10},{10,1... | collective-permute-start | bytes 1277960 | tf_op jit(solution)/shard_map/ppermute | solution.py:557
  9.9 12.6 %collective-permute-start.1 = (f32[52,8,256]{2,1,0:T(8,128)S(1)}, f32[52,8,256]{2,1,0:T(8,128)S(1)}, u32[]{:S(2)}, u32[]{:S(2)}) collective-permute-start(f32[52,8,256]{2,1,0:T(8,128)S(1)} %get-tuple-element.37), channel_id=1, source_target_pairs={{0,15},{1,0},{2,1},{3,2},{4,3},{5,4},{6,5},{7,6},{8,7},{9,8},{10,9... | collective-permute-start | bytes 1277960 | tf_op jit(solution)/shard_map/ppermute | solution.py:557
  16.0 10.4 %collective-permute-start.3 = (f32[39,8,256]{2,1,0:T(8,128)S(1)}, f32[39,8,256]{2,1,0:T(8,128)S(1)}, u32[]{:S(2)}, u32[]{:S(2)}) collective-permute-start(f32[39,8,256]{2,1,0:T(8,128)S(1)} %get-tuple-element.42.all_refs_4_), channel_id=1, source_target_pairs={{0,1},{1,2},{2,3},{3,4},{4,5},{5,6},{6,7},{7,8},{8,9},{9,10},{10,1... | collective-permute-start | bytes 958472 | tf_op jit(solution)/shard_map/ppermute | solution.py:557
  18.6 10.3 %collective-permute-start.4 = (f32[39,8,256]{2,1,0:T(8,128)S(1)}, f32[39,8,256]{2,1,0:T(8,128)S(1)}, u32[]{:S(2)}, u32[]{:S(2)}) collective-permute-start(f32[39,8,256]{2,1,0:T(8,128)S(1)} %get-tuple-element.43.all_refs_3_), channel_id=1, source_target_pairs={{0,15},{1,0},{2,1},{3,2},{4,3},{5,4},{6,5},{7,6},{8,7},{9,8},{10,9... | collective-permute-start | bytes 958472 | tf_op jit(solution)/shard_map/ppermute | solution.py:557
  22.6 6.3 %copy-start = (f32[8,32,256]{2,1,0:T(8,128)S(1)}, f32[8,32,256]{2,1,0:T(8,128)}, u32[]{:S(2)}) copy-start(f32[8,32,256]{2,1,0:T(8,128)} %all_refs_14_.1) | copy-start | bytes 786436

commit v3 on v2

--- a/solution.py
+++ b/solution.py
@@ -31,8 +31,8 @@
 )
 OPP = (0, 2, 1, 4, 3, 6, 5, 8, 7, 10, 9, 12, 11, 14, 13, 16, 15, 18, 17)
 PAIRS = ((1, 2), (3, 4), (5, 6), (7, 8), (9, 10), (11, 12), (13, 14), (15, 16), (17, 18))
-ZPAIRS = ((5, 6), (11, 12), (14, 13), (15, 16), (18, 17))
-ZSLOT = {5: (1, 2), 6: (1, 2), 11: (1, 3), 12: (1, 3), 14: (2, 0), 13: (2, 0), 15: (2, 1), 16: (2, 1), 18: (2, 2), 17: (2, 2)}
+ZPAIRS = ((11, 12), (14, 13), (5, 6), (15, 16), (18, 17))
+ZSLOT = {11: 2, 12: 2, 14: 3, 13: 3, 5: 0, 6: 0, 15: 1, 16: 1, 18: 2, 17: 2}
 XHIGH = (1, 7, 9, 11, 13)
 XLOW = (2, 8, 10, 12, 14)
 W0, W1, W2 = 1.0 / 3.0, 1.0 / 18.0, 1.0 / 36.0
@@ -61,7 +61,7 @@
         scratch_shapes=list(scratch),
         input_output_aliases=aliases or {},
         compiler_params=pltpu.CompilerParams(vmem_limit_bytes=limit),
-        cost_estimate=pl.CostEstimate(flops=0, bytes_accessed=int(us * 3e6), transcendentals=0),
+        cost_estimate=pl.CostEstimate(flops=int(us * 1e9), bytes_accessed=int(us * 3e6), transcendentals=0),
     )(*args)
 
 
@@ -93,7 +93,8 @@
         for n, (src, dst) in enumerate(((ts, tsm), (cond, km))):
             v = jnp.where(is_pore, 0.0, src[x])
             dst[x] = v
-            rows_out[n * nx + x] = edge_tile(v[0:TILE], v[nz - TILE : nz], row)
+            if n:
+                rows_out[x] = edge_tile(v[0:TILE], v[nz - TILE : nz], row)
         for n in (0, 1):
             fetch(n, x).wait()
         return lax.fori_loop(0, nz // TILE, lambda i, c: step(x, i, c), carry)
@@ -152,7 +153,7 @@
     return out
 
 
-def heat_body(hot, flow, tsm, rows_in, new_heat, temp, bounce, zmsg):
+def heat_body(hot, flow, tsm, rows_in, new_heat, temp, bounce, zmsg, zflow):
     nx, nz, ny = tsm.shape
     rowz = rows8((nz, ny))
     row = rows8((TILE, ny))
@@ -188,18 +189,18 @@
             inside = rowz != (0 if d == 5 else nz - 1)
             total = total + jnp.where(inside, got, 0.0)
             new_heat[d, x] = jnp.where(is_pore & inside, got, g[d])
-        total = jnp.where(is_pore, total, 0.0)
+        total = jnp.where(is_pore, total, t)
         temp[x] = total
         zmsg[x] = edge_tile(total[first], total[last], row)
         pairs = [(g[6][first], g[5][last]), ((own - g[6])[first], (own - g[5])[last])]
         for up, down in ZPAIRS:
             pairs.append((flow[down, x, first, :], flow[up, x, last, :]))
         zmsg[nx + x] = pack_pairs(pairs[:4], row)
-        zmsg[2 * nx + x] = pack_pairs(pairs[4:], row)
+        zflow[x] = pack_pairs(pairs[4:], row)
     ends = (hot[2, 0], hot[1, nx - 1], bounce[0], bounce[1])
     for n, v in enumerate(ends):
-        zmsg[3 * nx + n] = edge_tile(v[first], v[last], row)
-    zmsg[3 * nx + 4 :] = rows_in[...]
+        zmsg[2 * nx + n] = edge_tile(v[first], v[last], row)
+    zmsg[2 * nx + 4 :] = rows_in[...]
 
 
 def put_plane(out, n, v):
@@ -213,18 +214,50 @@
     return ref[n : n + tiles].reshape(tiles * TILE, ref.shape[-1])
 
 
-def early_body(tsm, km, flow, after, low, high):
-    nx = tsm.shape[0]
-    for side, out in ((0, low), (1, high)):
-        n = 0
-        for field in (tsm, km):
-            for x in range(side * (nx - DEEP), side * (nx - DEEP) + DEEP):
-                n = put_plane(out, n, field[x])
-        for d in (XLOW, XHIGH)[side]:
-            n = put_plane(out, n, flow[d, side * (nx - 1)])
-
-
-def zjoin_body(mine, theirs, temp, hot, bounce, heat_in, after, heat_ends, low, high):
+def parity():
+    return lax.axis_index("dev") % 2
+
+
+def by_side(cross, intra, body):
+    odd = parity()
+    for value, (low, high) in enumerate(((cross, intra), (intra, cross))):
+
+        @pl.when(odd == value)
+        def _(low=low, high=high):
+            body(low, high)
+
+
+def picker(cross, intra):
+    odd = parity()
+
+    def pick(side, n, tiles):
+        across, within = get_plane(cross, n, tiles), get_plane(intra, n, tiles)
+        even_value, odd_value = (across, within) if side == 0 else (within, across)
+        return jnp.where(jnp.full(across.shape, odd) == 0, even_value, odd_value)
+
+    return pick
+
+
+def early_body(km, flow, hot, bounce, temp, cross, intra):
+    nx, nz = km.shape[:2]
+
+    def fill(low, high):
+        for side, out in ((0, low), (1, high)):
+            n = 0
+            deep = range(side * (nx - DEEP), side * (nx - DEEP) + DEEP)
+            for x in deep:
+                n = put_plane(out, n, km[x])
+            for d in (XLOW, XHIGH)[side]:
+                n = put_plane(out, n, flow[d, side * (nx - 1)])
+            n = put_plane(out, n, hot[2 - side, side * (nx - 1)])
+            n = put_plane(out, n, bounce[side])
+            for x in deep:
+                n = put_plane(out, n, temp[x, TILE : nz - TILE, :])
+
+    by_side(cross, intra, fill)
+
+
+def zjoin_body(mine, theirs, temp, heat_in, after, heat_ends, joined, cross, intra):
     nx, nz, ny = temp.shape
     row = rows8((TILE, ny))
     edge = (row == 0) | (row == TILE - 1)
@@ -236,9 +269,9 @@
     def slot1(v):
         return jnp.where(row < DEEP, pltpu.roll(v, TILE - 1, 0), pltpu.roll(v, 1, 0))
 
-    at = [0, 0]
     for x in range(nx):
-        my_t, their_t = mine[3 * nx + 4 + x], theirs[3 * nx + 4 + x]
+        my_k, their_k = mine[2 * nx + 4 + x], theirs[2 * nx + 4 + x]
+        my_t, their_t = jnp.where(my_k == 0.0, 0.0, mine[x]), jnp.where(their_k == 0.0, 0.0, theirs[x])
         my_p, their_p = mine[nx + x], theirs[nx + x]
         near = swap(their_t)
         got = jnp.where(near == 0.0, swap(their_p), slot1(my_p) + WALL_NEAR * near)
@@ -249,58 +282,73 @@
         back = jnp.where(edge & (their_t == 0.0), back, 0.0)
         heat_ends[0, x] = jnp.where(mine_in & (row == 0), got, heat_in[5, x, first, :])
         heat_ends[1, x] = jnp.where(mine_in & (row == TILE - 1), got, heat_in[6, x, last, :])
+        joined[x, first, :] = temp[x, first, :] + jnp.where(row == 0, add, 0.0)
+        joined[x, TILE : nz - TILE, :] = temp[x, TILE : nz - TILE, :]
+        joined[x, last, :] = temp[x, last, :] + jnp.where(row == TILE - 1, add, 0.0)
+        joined[x, nz : nz + TILE, :] = theirs[x] + back
+
+    def fill(low, high):
         for side, out in ((0, low), (1, high)):
-            if side * (nx - DEEP) <= x < side * (nx - DEEP) + DEEP:
-                n = at[side]
-                out[n] = temp[x, first, :] + jnp.where(row == 0, add, 0.0)
-                n = put_plane(out, n + 1, temp[x, TILE : nz - TILE, :])
-                out[n] = temp[x, last, :] + jnp.where(row == TILE - 1, add, 0.0)
-                out[n + 1] = theirs[x] + back
-                at[side] = n + 2
-    for side, out in ((0, low), (1, high)):
-        x = side * (nx - 1)
-        n = put_plane(out, at[side], hot[2 - side, x])
-        out[n] = theirs[3 * nx + side]
-        n = put_plane(out, n + 1, bounce[side])
-        out[n] = theirs[3 * nx + 2 + side]
-        a, b = theirs[nx + x], theirs[2 * nx + x]
-        if side:
-            out[n + 1] = jnp.where(row < DEEP, b, pltpu.roll(a, 3, 0))
+            for n in range(DEEP):
+                v = joined.at[side * (nx - DEEP) + n]
+                out[3 * n] = v[first, :]
+                out[3 * n + 1] = v[last, :]
+                out[3 * n + 2] = v[nz : nz + TILE, :]
+            n = 3 * DEEP
+            out[n] = theirs[2 * nx + side]
+            out[n + 1] = theirs[2 * nx + 2 + side]
+            v = theirs[nx + side * (nx - 1)]
+            lower, upper = (5, 2) if side else (6, 3)
+            out[n + 2] = jnp.where(row < DEEP, pltpu.roll(v, lower, 0), pltpu.roll(v, upper, 0))
+            base = 2 * nx + 4 + side * (nx - DEEP)
+            out[n + 3 : n + 3 + DEEP] = theirs[base : base + DEEP]
+
+    by_side(cross, intra, fill)
+
+
+def reader(nx, early, late, tsm, km, rows):
+    tiles = km.shape[1] // TILE
+    ahead = (DEEP + len(XLOW)) * tiles
+    corner = 3 * DEEP + 3
+
+    def away(p):
+        return (0, p) if p < DEEP else (1, p - DEEP - nx)
+
+    def km_halo(p):
+        if DEEP <= p < DEEP + nx:
+            return rows[2 * nx + 4 + p - DEEP]
+        side, n = away(p)
+        return late(side, corner + n, 1)
+
+    def km_at(p):
+        if DEEP <= p < DEEP + nx:
+            core = km[p - DEEP]
         else:
-            out[n + 1] = jnp.where(row < DEEP, pltpu.roll(a, TILE - 3, 0), b)
-        for f in range(2):
-            base = 3 * nx + 4 + f * nx + side * (nx - DEEP)
-            out[n + 2 + f * DEEP : n + 2 + (f + 1) * DEEP] = theirs[base : base + DEEP]
-
-
-def reader(nx, early, late, fields, rows):
-    tiles = fields[0].shape[1] // TILE
-    corner = (DEEP + 2) * (tiles + 1) + 1
-
-    def core(f, p):
+            side, n = away(p)
+            core = early(side, n * tiles, tiles)
+        return jnp.concatenate([core, km_halo(p)], axis=0)
+
+    def temp_far(p):
+        side, n = away(p)
+        middle = early(side, ahead + 2 * tiles + n * (tiles - 2), tiles - 2)
+        ends = late(side, 3 * n, 3)
+        return jnp.concatenate([ends[0:TILE], middle, ends[TILE:]], axis=0)
+
+    def ts_at(p):
         if DEEP <= p < DEEP + nx:
-            return fields[f][p - DEEP]
-        side, n = (0, p) if p < DEEP else (1, p - DEEP - nx)
-        return get_plane(early[side], (f * DEEP + n) * tiles, tiles)
-
-    def halo(f, p):
-        if DEEP <= p < DEEP + nx:
-            return rows[3 * nx + 4 + f * nx + p - DEEP]
-        side, n = (0, p) if p < DEEP else (1, p - DEEP - nx)
-        return late[side][corner + f * DEEP + n]
-
-    def whole(f, p):
-        return jnp.concatenate([core(f, p), halo(f, p)], axis=0)
-
-    return core, halo, whole
+            halo = jnp.where(km_halo(p) == 0.0, 0.0, rows[p - DEEP])
+            return jnp.concatenate([tsm[p - DEEP], halo], axis=0)
+        return jnp.where(km_at(p) == 0.0, 0.0, temp_far(p))
+
+    return ts_at, km_at, km_halo, temp_far, ahead
 
 
 def face(a, b):
     return (2.0 * a) * b / jnp.maximum(a + b, 1.0)
 
 
-def still_plane(whole, p, fx_low, fx_high):
-    k, t = whole(1, p), whole(0, p)
+def still_plane(ts_at, km_at, p, fx_low, fx_high):
+    k, t = km_at(p), ts_at(p)
     ext, ny = k.shape
     ky = pltpu.roll(k, 1, 1)
     kz = pltpu.roll(k, 1, 0)
@@ -308,10 +356,10 @@
     pore = jnp.where(k == 0.0, 1.0, 0.0)
     count = jnp.where(ky == 0.0, 1.0, 0.0) + jnp.where(kz == 0.0, 1.0, 0.0)
     count = count + pltpu.roll(pore, ny - 1, 1) + pltpu.roll(pore, ext - 1, 0)
-    count = count + jnp.where(whole(1, p - 1) == 0.0, 1.0, 0.0) + jnp.where(whole(1, p + 1) == 0.0, 1.0, 0.0)
+    count = count + jnp.where(km_at(p - 1) == 0.0, 1.0, 0.0) + jnp.where(km_at(p + 1) == 0.0, 1.0, 0.0)
     flux_y = gy * (pltpu.roll(t, 1, 1) - t)
     flux_z = gz * (pltpu.roll(t, 1, 0) - t)
-    net = fx_low * (whole(0, p - 1) - t) - fx_high * (t - whole(0, p + 1))
+    net = fx_low * (ts_at(p - 1) - t) - fx_high * (t - ts_at(p + 1))
     net = net + (flux_y - pltpu.roll(flux_y, ny - 1, 1))
     net = net + (flux_z - pltpu.roll(flux_z, ext - 1, 0))
     return gy, gz, net - FILM * count * t
@@ -319,24 +367,24 @@
 
 def static_body(tsm, km, theirs, fx, fy, fz, still):
     nx = tsm.shape[0]
-    _, _, whole = reader(nx, None, None, (tsm, km), theirs)
+    ts_at, km_at = reader(nx, None, None, tsm, km, theirs)[:2]
     first = DEEP + 1
     for n in range(nx - 1):
-        fx[n] = face(whole(1, first + n), whole(1, first + n - 1))
+        fx[n] = face(km_at(first + n), km_at(first + n - 1))
     for n in range(nx - 2):
-        fy[n], fz[n], still[n] = still_plane(whole, first + n, fx[n], fx[n + 1])
+        fy[n], fz[n], still[n] = still_plane(ts_at, km_at, first + n, fx[n], fx[n + 1])
 
 
 def conduct_body(*all_refs):
-    early_low, early_high, from_low, low, high, from_high, theirs = all_refs[0:7]
+    early_cross, early_intra, late_cross, late_intra, theirs, joined, bounce = all_refs[0:7]
     in_fx, in_fy, in_fz, in_still, tsm, km, hot, ts, corners, heat_in, pops_in, new_heat, new_pops, new_solid = all_refs[7:21]
     temp, resid, step_a, step_b, fx, fy, fz, still, ends, patched, sems = all_refs[21:]
     nx, nz, ny = ts.shape
     planes, ext = temp.shape[:2]
-    tiles = ext // TILE
+    tiles = nz // TILE
     own = slice(0, nz)
-    late = (from_low, low, high, from_high)
-    core, halo, whole = reader(nx, (early_low, early_high), (from_low, from_high), (tsm, km), theirs)
+    early, late = picker(early_cross, early_intra), picker(late_cross, late_intra)
+    ts_at, km_at, km_halo, temp_far, ahead = reader(nx, early, late, tsm, km, theirs)
 
     def ready(p):
         return DEEP < p < DEEP + nx - 1
@@ -353,51 +401,47 @@
     def still_at(p):
         return in_still[p - DEEP - 1] if ready(p) else still[p]
 
-    def ts_at(p):
-        return whole(0, p)
-
     def temp_at(p):
-        ref, n = ((from_low, p), (low, p - DEEP), (high, p - nx), (from_high, p - DEEP - nx))[p // DEEP]
-        return get_plane(ref, n * tiles, tiles)
-
-    def out_of(ref):
-        return get_plane(ref, DEEP * tiles, tiles)
-
-    def bounce_of(ref):
-        return get_plane(ref, (DEEP + 1) * tiles, tiles)
-
-    def join(below, above, p_low, p_high):
-        t_low, t_high = ts_at(p_low), ts_at(p_high)
-        up = jnp.where(t_low == 0.0, out_of(below), bounce_of(above) + WALL_NEAR * t_low)
-        down = jnp.where(t_high == 0.0, out_of(above), bounce_of(below) + WALL_NEAR * t_high)
-        temp[p_high] = jnp.where(t_high == 0.0, temp_at(p_high) + up, 0.0)
-        temp[p_low] = jnp.where(t_low == 0.0, temp_at(p_low) + down, 0.0)
-        return up, down
+        return joined[p - DEEP] if DEEP <= p < DEEP + nx else temp_far(p)
+
+    def sent(n, side):
+        return jnp.concatenate([early(side, ahead + n * tiles, tiles), late(side, 3 * DEEP + n, 1)], axis=0)
+
+    def mine(n, side):
+        end = (hot[2 - side, side * (nx - 1)], bounce[side])[n]
+        return jnp.concatenate([end, theirs[2 * nx + 2 * n + side]], axis=0)
+
+    def join(side):
+        p_own = DEEP + side * (nx - 1)
+        p_far = p_own - 1 + 2 * side
+        t_own, t_far = ts_at(p_own), ts_at(p_far)
+        got = jnp.where(t_far == 0.0, sent(0, side), mine(1, side) + WALL_NEAR * t_far)
+        back = jnp.where(t_own == 0.0, mine(0, side), sent(1, side) + WALL_NEAR * t_own)
+        temp[p_own] = jnp.where(t_own == 0.0, temp_at(p_own) + got, 0.0)
+        temp[p_far] = jnp.where(t_far == 0.0, temp_at(p_far) + back, 0.0)
+        return got
 
     row = rows8((TILE, ny))
-    corner = (DEEP + 2) * tiles
+    corner = 3 * DEEP + 2
     copies = []
-    for n, (d, x, p, ref) in enumerate(
+    for n, (d, x, p, side) in enumerate(
         (
-            (11, 0, DEEP - 1, from_low),
-            (13, 0, DEEP - 1, from_low),
-            (12, nx - 1, DEEP + nx, from_high),
-            (14, nx - 1, DEEP + nx, from_high),
+            (11, 0, DEEP - 1, 0),
+            (13, 0, DEEP - 1, 0),
+            (12, nx - 1, DEEP + nx, 1),
+            (14, nx - 1, DEEP + nx, 1),
         )
     ):
         by, at, rows = (1, 0, slice(0, TILE)) if DIRS[d][2] > 0 else (TILE - 1, TILE - 1, slice(nz - TILE, nz))
-        there = pltpu.roll(halo(0, p), by, 0)
+        there = pltpu.roll(km_halo(p), by, 0)
         both = (row == at) & (tsm[x, rows, :] == 0.0) & (there == 0.0)
-        patched[n] = jnp.where(both, pltpu.roll(ref[corner], by, 0), corners[n])
+        patched[n] = jnp.where(both, pltpu.roll(late(side, corner, 1), by, 0), corners[n])
         copies.append(pltpu.make_async_copy(patched.at[n], new_pops.at[d, x, rows, :], sems.at[n]))
         copies[-1].start()
-    for p in range(1, planes - 1):
+    for p in range(planes):
         if p not in (DEEP - 1, DEEP, DEEP + nx - 1, DEEP + nx):
-            temp[p] = temp_at(p)
-    temp[0] = temp_at(0)
-    temp[planes - 1] = temp_at(planes - 1)
-    up, _ = join(from_low, low, DEEP - 1, DEEP)
-    _, down = join(high, from_high, DEEP + nx - 1, DEEP + nx)
+            temp[p] = jnp.where(km_at(p) == 0.0, temp_at(p), 0.0)
+    up, down = join(0), join(1)
     ends[0] = jnp.where(tsm[0] == 0.0, up[own], hot[1, 0])
     ends[1] = jnp.where(tsm[nx - 1] == 0.0, down[own], hot[2, nx - 1])
     for n, (d, x) in enumerate(((1, 0), (2, nx - 1))):
@@ -406,15 +450,15 @@
 
     for p in range(1, planes):
         if not DEEP < p < DEEP + nx:
-            fx[p] = face(whole(1, p), whole(1, p - 1))
+            fx[p] = face(km_at(p), km_at(p - 1))
     for p in range(1, planes - 1):
         if not ready(p):
-            fy[p], fz[p], still[p] = still_plane(whole, p, fx_at(p), fx_at(p + 1))
+            fy[p], fz[p], still[p] = still_plane(ts_at, km_at, p, fx_at(p), fx_at(p + 1))
     for p in range(1, planes - 1):
         mid = temp[p]
         near = (temp[p - 1] + temp[p + 1]) + (pltpu.roll(mid, 1, 1) + pltpu.roll(mid, ny - 1, 1))
         near = near + (pltpu.roll(mid, 1, 0) + pltpu.roll(mid, ext - 1, 0))
-        r = jnp.where(ts_at(p) == 0.0, 0.0, FILM * near) + still_at(p)
+        r = jnp.where(km_at(p) == 0.0, 0.0, FILM * near) + still_at(p)
         resid[p] = r
         s = r * (1.0 / THETA)
         step_a[p] = s
@@ -457,28 +501,55 @@
 
 
 def flow_body(part, *all_refs):
-    early = late = theirs = None
+    early = theirs = None
     if part == 0:
-        flow, tsm, out, done, buf, sems = all_refs
+        flow, tsm, out, turned, buf, sems = all_refs
     elif part == 1:
-        flow, tsm, theirs, heat, heat_ends, held, out, heat_out, buf, sems, heat_sems = all_refs
+        flow, tsm, theirs, flow_rows, turned, heat, heat_ends, held, out, heat_out, buf, sems, heat_sems = all_refs
     else:
-        flow, tsm, theirs, early_low, early_high, held, out, corners, buf, sems = all_refs
-        early = (early_low, early_high)
+        flow, tsm, theirs, flow_rows, turned, early_cross, early_intra, held, out, corners, buf, sems = all_refs
+        early = picker(early_cross, early_intra)
     nx, nz, ny = flow.shape[1:]
     tiles = nz // TILE
-    ext = nz + TILE
-    rowz = rows8((nz, ny))
-    core, _, whole = reader(nx, early, None, (tsm, None), theirs)
+    row = rows8((TILE, ny))
+    if part == 0:
+        for x in range(nx):
+            for n, by in enumerate((1, ny - 1)):
+                turned[n, x] = pltpu.roll(tsm[x], by, 1)
     if part == 1:
         copy_heat = pltpu.make_async_copy(heat, heat_out, heat_sems.at[0])
         copy_heat.start()
 
-    def source(d, q):
+    def span(i):
+        return slice(i * TILE, (i + 1) * TILE)
+
+    def turn(v, cy):
+        return pltpu.roll(v, cy % ny, 1) if cy else v
+
+    def shift(tile, i, cz):
+        if not cz:
+            return tile(i)
+        far, by = (0, 1) if cz > 0 else (TILE - 1, TILE - 1)
+        return jnp.where(row == far, pltpu.roll(tile(i - cz), by, 0), pltpu.roll(tile(i), by, 0))
+
+    def mask_tile(q, cy, i):
+        if not 0 <= q < nx:
+            return turn(early(int(q > 0), (0 if q > 0 else DEEP - 1) * tiles + i % tiles, 1), cy)
+        if not 0 <= i < tiles:
+            return turn(theirs[2 * nx + 4 + q], cy)
+        if cy:
+            return turned[0 if cy > 0 else 1, q, span(i), :]
+        return tsm[q, span(i), :]
+
+    def flow_tile(d, q, i):
         if 0 <= q < nx:
-            return flow[d, q]
-        ref, n = (early_low, XHIGH.index(d)) if q < 0 else (early_high, XLOW.index(d))
-        return get_plane(ref, (2 * DEEP + n) * tiles, tiles)
+            if 0 <= i < tiles:
+                return flow[d, q, span(i), :]
+            v = theirs[nx + q] if d in (11, 12, 13, 14) else flow_rows[q]
+            by = ZSLOT[d] if DIRS[d][2] > 0 else TILE - ZSLOT[d]
+            return pltpu.roll(v, by % TILE, 0) if by % TILE else v
+        side, n = (0, XHIGH.index(d)) if q < 0 else (1, XLOW.index(d))
+        return early(side, (DEEP + n) * tiles + i % tiles, 1)
 
     copies = []
     for at, x in enumerate(range(1, nx - 1) if part < 2 else (0, nx - 1)):
@@ -486,39 +557,24 @@
         if at >= 2:
             for copy in copies[at - 2]:
                 copy.wait()
-        is_pore = tsm[x] == 0.0
-        turned = {}
-        for at_d, d in enumerate(FLOW_DIRS[part]):
-            if d == 0:
-                buf[slot, at_d] = flow[0, x]
-                continue
-            cx, cy, cz = DIRS[d]
-            q = x - cx
-            inside = 0 <= q < nx
-            tall = bool(cz) and inside
-            if (cx, cy, tall) not in turned:
-                t = (whole if tall else core)(0, q + DEEP)
-                turned[cx, cy, tall] = pltpu.roll(t, cy % ny, 1) if cy else t
-            t = turned[cx, cy, tall]
-            if cz:
-                t = pltpu.roll(t, cz % t.shape[0], 0)
-            both = is_pore & (t[0:nz] == 0.0)
-            v = source(d, q)
-            if cz:
-                at_end = rowz == (0 if cz > 0 else nz - 1)
-                v = pltpu.roll(v, cz % nz, 0)
-                if inside:
-                    block, j = ZSLOT[d]
-                    n = TILE - 1 - j if cz > 0 else j
-                    v = jnp.where(at_end, theirs[block * nx + q, n : n + 1, :], v)
-                else:
-                    both = both & ~at_end
-            if cy:
-                v = pltpu.roll(v, cy % ny, 1)
-            v = jnp.where(both, v, jnp.where(is_pore, flow[OPP[d], x], flow[d, x]))
-            buf[slot, at_d] = v
-            if cz and not inside:
-                corners[(11, 13, 12, 14).index(d)] = v[0:TILE] if cz > 0 else v[nz - TILE : nz]
+        for i in range(tiles):
+            is_pore = tsm[x, span(i), :] == 0.0
+            for at_d, d in enumerate(FLOW_DIRS[part]):
+                if d == 0:
+                    buf[slot, at_d, span(i), :] = flow[0, x, span(i), :]
+                    continue
+                cx, cy, cz = DIRS[d]
+                q = x - cx
+                t = shift(lambda n: mask_tile(q, cy, n), i, cz)
+                both = is_pore & (t == 0.0)
+                v = turn(shift(lambda n: flow_tile(d, q, n), i, cz), cy)
+                open_row = cz and not 0 <= q < nx and i == (0 if cz > 0 else tiles - 1)
+                if open_row:
+                    both = both & (row != (0 if cz > 0 else TILE - 1))
+                v = jnp.where(both, v, jnp.where(is_pore, flow[OPP[d], x, span(i), :], flow[d, x, span(i), :]))
+                buf[slot, at_d, span(i), :] = v
+                if open_row:
+                    corners[(11, 13, 12, 14).index(d)] = v
         begin = 0
         copies.append([])
         for n, (d, count) in enumerate(FLOW_RUNS[part]):
@@ -526,8 +582,6 @@
             copies[-1].append(pltpu.make_async_copy(src, dst, sems.at[2 * slot + n]))
             copies[-1][-1].start()
             begin += count
-    if part == 0:
-        done[...] = jnp.zeros(done.shape, jnp.float32)
     if part == 1:
         copy_heat.wait()
         for n, rows in ((0, slice(0, TILE)), (1, slice(nz - TILE, nz))):
@@ -553,8 +607,10 @@
     return jnp.where(upper, from_above, from_below)
 
 
-def along_x(low, high):
-    return lax.ppermute(high, "dev", ring("dev", 1)), lax.ppermute(low, "dev", ring("dev", -1))
+def along_x(cross, intra):
+    count = lax.axis_size("dev")
+    across = [(i, (i + 2 * (i % 2) - 1) % count) for i in range(count)]
+    return lax.ppermute(cross, "dev", across), lax.ppermute(intra, "dev", [(i, i ^ 1) for i in range(count)])
 
 
 def per_device(populations, heat_pops, solid_temp, conductivity, pore_mask):
@@ -567,7 +623,7 @@
     dma = pltpu.SemaphoreType.DMA
     flow, hot, tsm, km, my_rows = call(
         collide_body,
-        [(19, *field), (7, *field), field, field, (2 * nx, TILE, ny)],
+        [(19, *field), (7, *field), field, field, (nx, TILE, ny)],
         [pltpu.with_memory_space_constraint(v, pltpu.HBM) for v in (populations, heat_pops, solid_temp, conductivity, pore_mask)],
         in_specs=[HBM] * 5,
         scratch=[
@@ -581,15 +637,15 @@
         limit=12 << 20,
         us=4,
     )
-    new_heat, temp, bounce, zmsg = call(
+    new_heat, temp, bounce, zmsg, zflow = call(
         heat_body,
-        [(7, *field), field, (2, nz, ny), (5 * nx + 4, TILE, ny)],
+        [(7, *field), field, (2, nz, ny), (3 * nx + 4, TILE, ny), (nx, TILE, ny)],
         [hot, flow, tsm, my_rows],
     )
     theirs = along_z(zmsg)
-    early_shape = ((2 * DEEP + len(XLOW)) * (tiles - 1), TILE, ny)
-    early_low, early_high = call(early_body, [early_shape] * 2, [tsm, km, flow, bounce])
-    early_low, early_high = along_x(early_low, early_high)
+    flow_rows = along_z(zflow)
+    early_shape = ((DEEP + len(XLOW) + 2) * (tiles - 1) + DEEP * (tiles - 3), TILE, ny)
+    early = along_x(*call(early_body, [early_shape] * 2, [km, flow, hot, bounce, temp]))
 
     def flow_call(part, outs, args, out_specs, in_hbm=0, extra=(), **rest):
         held = (2, len(FLOW_DIRS[part]), nz, ny)
@@ -605,31 +661,32 @@
         )
 
     pops_shape, heat_shape = (19, *field), (7, *field)
-    new_pops, after = flow_call(0, [pops_shape, (TILE, 128)], [flow, tsm], [ANY, VM], us=20)
-    late_shape = ((DEEP + 2) * tiles + 1 + 2 * DEEP, TILE, ny)
-    heat_ends, low, high = call(
+    new_pops, turned = flow_call(0, [pops_shape, (2, *field)], [flow, tsm], [ANY, VM], us=20)
+    late_shape = (4 * DEEP + 3, TILE, ny)
+    heat_ends, joined, cross, intra = call(
         zjoin_body,
-        [(2, nx, TILE, ny), late_shape, late_shape],
-        [zmsg, theirs, temp, hot, bounce, new_heat, after],
+        [(2, nx, TILE, ny), (nx, ext, ny), late_shape, late_shape],
+        [zmsg, theirs, temp, new_heat, turned],
+        us=50,
     )
-    from_low, from_high = along_x(low, high)
+    late = along_x(cross, intra)
     new_pops, new_heat = flow_call(
         1,
         [pops_shape, heat_shape],
-        [flow, tsm, theirs, new_heat, heat_ends, new_pops],
+        [flow, tsm, theirs, flow_rows, turned, new_heat, heat_ends, new_pops],
         [ANY, ANY],
         in_hbm=1,
         extra=[dma((2,))],
-        aliases={5: 0},
+        aliases={7: 0},
         us=20,
     )
     new_pops, corners = flow_call(
         2,
         [pops_shape, (4, TILE, ny)],
-        [flow, tsm, theirs, early_low, early_high, new_pops],
+        [flow, tsm, theirs, flow_rows, turned, *early, new_pops],
         [ANY, VM],
         in_hbm=1,
-        aliases={5: 0},
+        aliases={7: 0},
     )
     fx, fy, fz, still = call(
         static_body,
@@ -639,7 +696,7 @@
     new_heat, new_pops, new_solid = call(
         conduct_body,
         [heat_shape, pops_shape, field],
-        [early_low, early_high, from_low, low, high, from_high, theirs]
+        [*early, *late, theirs, joined, bounce]
         + [fx, fy, fz, still, tsm, km, hot, solid_temp, corners, new_heat, new_pops],
         in_specs=[VM] * 16 + [ANY] * 2,
         out_specs=[ANY, ANY, VM],

time: 34 us -> 29.4 us (0.86)
  waiting for transfers between devices: 7.94 us -> 0.96 us
  starting transfers between devices: 6.9 us -> 9.23 us
    ppermute x4, waiting for transfers between devices: 4.87 us -> 0.96 us  [the longest x2 0.95 us: along_x(): lax.ppermute(cross, 'dev', across)]
    ppermute x1 -> x2, waiting for transfers between devices: 3.07 us -> 0.01 us  [along_z(): return lax.ppermute(rows, 'grp', ring('grp', 1))]
    ppermute x4, starting transfers between devices: 4.79 us -> 7.04 us  [the longest x2 3.61 us: along_x(): lax.ppermute(intra, 'dev', [(i, i ^ 1) for i in range(count)])]
    ppermute x1 -> x2, starting transfers between devices: 2.11 us -> 2.18 us  [along_z(): return lax.ppermute(rows, 'grp', ring('grp', 1))]
  transfers between devices with their start and end apart: 5 -> 6, of which waited for: 3 -> 1; matrix products, arithmetic and copies ran while one was open for 0% -> 0% of each run, Pallas kernels for 25% -> 28%
where the time goes in v3:
time: 29.4 us; the launch traced here: 29.2 us
  Pallas kernels  18.3 us (62%)
  starting transfers between devices  9.23 us (31%)
  waiting for transfers between devices  0.96 us (3%)
  between operations  0.72 us (2%)
    pallas_call x9, Pallas kernels, call(): pl.pallas_call(body, out_shape=[jax.ShapeDtypeStruct(shape, jnp.float32)...  18.3 us
    ppermute x2, starting transfers between devices, along_x(): lax.ppermute(intra, 'dev', [(i, i ^ 1) for i in range(count)])  3.61 us
    ppermute x2, starting transfers between devices, along_x(): lax.ppermute(cross, 'dev', across)  3.43 us
    ppermute x2, starting transfers between devices, along_z(): return lax.ppermute(rows, 'grp', ring('grp', 1))  2.18 us
    ppermute x2, waiting for transfers between devices, along_x(): lax.ppermute(cross, 'dev', across)  0.95 us
  transfers between devices with their start and end apart: 6, of which 1 were waited for; matrix products, arithmetic and copies ran while one was open for 0% of the time, Pallas kernels for 28%

profile of v3, /device:TPU:1, one launch (start us, length us, event | category | flops | bytes accessed | tf_op | source)
XLA Modules:
  0.0 29.2 jit_solution(12639943494739409654)
XLA Ops:
  0.6 4.2 %shard_map.76 = (f32[19,8,32,256]{3,2,1,0:T(8,128)S(1)}, f32[7,8,32,256]{3,2,1,0:T(8,128)S(1)}, f32[8,32,256]{2,1,0:T(8,128)S(1)}, f32[8,32,256]{2,1,0:T(8,128)S(1)}, f32[8,8,256]{2,1,0:T(8,128)S(1)}) custom-call(f32[19,8,32,256]{3,2,1,0:T(8,128)} %refs_0_.1, f32[7,8,32,256]{3,2,1,0:T(8,128)} %refs_1_.1, f32[8,32,256]{2,1,0:T(8,128)} %all_refs_14_.1, ...), custom_call_target="tpu_custom_call" | custom-call | flops 4000000000 | bytes 12000000 | tf_op jit(solution)/shard_map/pallas_call | solution.py:56
  4.8 0.8 %shard_map.77 = (f32[7,8,32,256]{3,2,1,0:T(8,128)S(1)}, f32[8,32,256]{2,1,0:T(8,128)S(1)}, f32[2,32,256]{2,1,0:T(8,128)S(1)}, f32[28,8,256]{2,1,0:T(8,128)S(1)}, f32[8,8,256]{2,1,0:T(8,128)S(1)}) custom-call(f32[7,8,32,256]{3,2,1,0:T(8,128)S(1)} %get-tuple-element.34.hot.all_refs_13_, f32[19,8,32,256]{3,2,1,0:T(8,128)S(1)} %get-tuple-element.33.flow.all_refs_0_, ...), custom_call_target="tpu_custom_call" | custom-call | flops 500000000 | bytes 1500000 | tf_op jit(solution)/shard_map/pallas_call | solution.py:56
  5.6 2.1 %collective-permute-start.2 = (f32[28,8,256]{2,1,0:T(8,128)S(1)}, f32[28,8,256]{2,1,0:T(8,128)S(1)}, u32[]{:S(2)}, u32[]{:S(2)}) collective-permute-start(f32[28,8,256]{2,1,0:T(8,128)S(1)} %get-tuple-element.41.mine), channel_id=1, source_target_pairs={{0,16},{16,0},{1,17},{17,1},{2,18},{18,2},{3,19},{19,3},{4,20},{20... | collective-permute-start | bytes 688136 | tf_op jit(solution)/shard_map/ppermute | solution.py:603
  7.7 0.1 collective-permute-start.5
  7.8 0.1 shard_map.78
  7.9 2.6 %collective-permute-start = (f32[52,8,256]{2,1,0:T(8,128)S(1)}, f32[52,8,256]{2,1,0:T(8,128)S(1)}, u32[]{:S(2)}, u32[]{:S(2)}) collective-permute-start(f32[52,8,256]{2,1,0:T(8,128)S(1)} %get-tuple-element.39), channel_id=1, source_target_pairs={{0,15},{1,2},{2,1},{3,4},{4,3},{5,6},{6,5},{7,8},{8,7},{9,10},{10,... | collective-permute-start | bytes 1277960 | tf_op jit(solution)/shard_map/ppermute | solution.py:613
  10.5 2.3 %collective-permute-start.1 = (f32[52,8,256]{2,1,0:T(8,128)S(1)}, f32[52,8,256]{2,1,0:T(8,128)S(1)}, u32[]{:S(2)}, u32[]{:S(2)}) collective-permute-start(f32[52,8,256]{2,1,0:T(8,128)S(1)} %get-tuple-element.40), channel_id=1, source_target_pairs={{0,1},{1,0},{2,3},{3,2},{4,5},{5,4},{6,7},{7,6},{8,9},{9,8},{10,11... | collective-permute-start | bytes 1277960 | tf_op jit(solution)/shard_map/ppermute | solution.py:613
  12.8 2.8 %shard_map.79 = (f32[19,8,32,256]{3,2,1,0:T(8,128)}, f32[2,8,32,256]{3,2,1,0:T(8,128)S(1)}) custom-call(f32[19,8,32,256]{3,2,1,0:T(8,128)S(1)} %get-tuple-element.33.flow.all_refs_0_, f32[8,32,256]{2,1,0:T(8,128)S(1)} %get-tuple-element.35.tsm.all_refs_1_.all_refs_11_), custom_call_target="tpu_custom_call" | custom-call | flops 20000000000 | bytes 60000000 | tf_op jit(solution)/shard_map/pallas_call | solution.py:56
  15.6 0.0 collective-permute-done.2.theirs.all_refs_2_.all_refs_4_
  15.6 0.1 shard_map.80
  15.7 0.8 %collective-permute-start.3 = (f32[19,8,256]{2,1,0:T(8,128)S(1)}, f32[19,8,256]{2,1,0:T(8,128)S(1)}, u32[]{:S(2)}, u32[]{:S(2)}) collective-permute-start(f32[19,8,256]{2,1,0:T(8,128)S(1)} %get-tuple-element.44), channel_id=1, source_target_pairs={{0,15},{1,2},{2,1},{3,4},{4,3},{5,6},{6,5},{7,8},{8,7},{9,10},{10,... | collective-permute-start | bytes 466952 | tf_op jit(solution)/shard_map/ppermute | solution.py:613
  16.5 1.3 %collective-permute-start.4 = (f32[19,8,256]{2,1,0:T(8,128)S(1)}, f32[19,8,256]{2,1,0:T(8,128)S(1)}, u32[]{:S(2)}, u32[]{:S(2)}) collective-permute-start(f32[19,8,256]{2,1,0:T(8,128)S(1)} %get-tuple-element.45), channel_id=1, source_target_pairs={{0,1},{1,0},{2,3},{3,2},{4,5},{5,4},{6,7},{7,6},{8,9},{9,8},{10,11... | collective-permute-start | bytes 466952 | tf_op jit(solution)/shard_map/ppermute | solution.py:613
  17.8 0.0 collective-permute-done.5.all_refs_3_
  17.9 3.4 %shard_map.82 = (f32[19,8,32,256]{3,2,1,0:T(8,128)}, f32[7,8,32,256]{3,2,1,0:T(8,128)}) custom-call(f32[19,8,32,256]{3,2,1,0:T(8,128)S(1)} %get-tuple-element.33.flow.all_refs_0_, f32[8,32,256]{2,1,0:T(8,128)S(1)} %get-tuple-element.35.tsm.all_refs_1_.all_refs_11_, ...), custom_call_target="tpu_custom_call", output_to_operand_aliasing={{0}: (7, {})} | custom-call | flops 20000000000 | bytes 60000000 | tf_op jit(solution)/shard_map/pallas_call | solution.py:56
  21.2 0.6 %shard_map.81 = (f32[7,40,256]{2,1,0:T(8,128)S(1)}, f32[6,40,256]{2,1,0:T(8,128)S(1)}, f32[6,40,256]{2,1,0:T(8,128)S(1)}, f32[6,40,256]{2,1,0:T(8,128)S(1)}) custom-call(f32[8,32,256]{2,1,0:T(8,128)S(1)} %get-tuple-element.35.tsm.all_refs_1_.all_refs_11_, f32[8,32,256]{2,1,0:T(8,128)S(1)} %get-tuple-element.32.km.all_refs_12_, ...), custom_call_target="tpu_custom_call" | custom-call | flops 500000000 | bytes 1500000 | tf_op jit(solution)/shard_map/pallas_call | solution.py:56
  21.8 0.0 collective-permute-done.all_refs_5_.all_refs_0_
  21.8 0.0 collective-permute-done.1.all_refs_6_.all_refs_1_
  21.8 0.0 copy-start
  21.9 1.4 %shard_map.83 = (f32[19,8,32,256]{3,2,1,0:T(8,128)}, f32[4,8,256]{2,1,0:T(8,128)S(1)}) custom-call(f32[19,8,32,256]{3,2,1,0:T(8,128)S(1)} %get-tuple-element.33.flow.all_refs_0_, f32[8,32,256]{2,1,0:T(8,128)S(1)} %get-tuple-element.35.tsm.all_refs_1_.all_refs_11_, ...), custom_call_target="tpu_custom_call", output_to_operand_aliasing={{0}: (7, {})} | custom-call | flops 500000000 | bytes 1500000 | tf_op jit(solution)/shard_map/pallas_call | solution.py:56
  23.2 0.9 %collective-permute-done.3.all_refs_2_ = f32[19,8,256]{2,1,0:T(8,128)S(1)} collective-permute-done((f32[19,8,256]{2,1,0:T(8,128)S(1)}, f32[19,8,256]{2,1,0:T(8,128)S(1)}, u32[]{:S(2)}, u32[]{:S(2)}) %collective-permute-start.3) | collective-permute-done | bytes 155680 | tf_op jit(solution)/shard_map/ppermute | solution.py:613
  24.2 0.0 collective-permute-done.4.all_refs_3_
  24.2 0.0 copy-done
  24.2 5.0 %shard_map.84 = (f32[7,8,32,256]{3,2,1,0:T(8,128)}, f32[19,8,32,256]{3,2,1,0:T(8,128)}, f32[8,32,256]{2,1,0:T(8,128)}) custom-call(f32[52,8,256]{2,1,0:T(8,128)S(1)} %collective-permute-done.all_refs_5_.all_refs_0_, f32[52,8,256]{2,1,0:T(8,128)S(1)} %collective-permute-done.1.all_refs_6_.all_refs_1_, ...), custom_call_target="tpu_custom_call", output_to_operand_aliasing={{0}: (16, {}), {1}: (17, {})} | custom-call | flops 4000000000 | bytes 12000000 | tf_op jit(solution)/shard_map/pallas_call | solution.py:56
Async XLA Ops:
  5.6 10.0 %collective-permute-start.2 = (f32[28,8,256]{2,1,0:T(8,128)S(1)}, f32[28,8,256]{2,1,0:T(8,128)S(1)}, u32[]{:S(2)}, u32[]{:S(2)}) collective-permute-start(f32[28,8,256]{2,1,0:T(8,128)S(1)} %get-tuple-element.41.mine), channel_id=1, source_target_pairs={{0,16},{16,0},{1,17},{17,1},{2,18},{18,2},{3,19},{19,3},{4,20},{20... | collective-permute-start | bytes 688136 | tf_op jit(solution)/shard_map/ppermute | solution.py:603
  7.7 10.1 %collective-permute-start.5 = (f32[8,8,256]{2,1,0:T(8,128)S(1)}, f32[8,8,256]{2,1,0:T(8,128)S(1)}, u32[]{:S(2)}, u32[]{:S(2)}) collective-permute-start(f32[8,8,256]{2,1,0:T(8,128)S(1)} %get-tuple-element.51), channel_id=1, source_target_pairs={{0,16},{16,0},{1,17},{17,1},{2,18},{18,2},{3,19},{19,3},{4,20},{20... | collective-permute-start | bytes 196616 | tf_op jit(solution)/shard_map/ppermute | solution.py:603
  7.9 14.0 %collective-permute-start = (f32[52,8,256]{2,1,0:T(8,128)S(1)}, f32[52,8,256]{2,1,0:T(8,128)S(1)}, u32[]{:S(2)}, u32[]{:S(2)}) collective-permute-start(f32[52,8,256]{2,1,0:T(8,128)S(1)} %get-tuple-element.39), channel_id=1, source_target_pairs={{0,15},{1,2},{2,1},{3,4},{4,3},{5,6},{6,5},{7,8},{8,7},{9,10},{10,... | collective-permute-start | bytes 1277960 | tf_op jit(solution)/shard_map/ppermute | solution.py:613
  10.5 11.4 %collective-permute-start.1 = (f32[52,8,256]{2,1,0:T(8,128)S(1)}, f32[52,8,256]{2,1,0:T(8,128)S(1)}, u32[]{:S(2)}, u32[]{:S(2)}) collective-permute-start(f32[52,8,256]{2,1,0:T(8,128)S(1)} %get-tuple-element.40), channel_id=1, source_target_pairs={{0,1},{1,0},{2,3},{3,2},{4,5},{5,4},{6,7},{7,6},{8,9},{9,8},{10,11... | collective-permute-start | bytes 1277960 | tf_op jit(solution)/shard_map/ppermute | solution.py:613
  15.7 8.5 %collective-permute-start.3 = (f32[19,8,256]{2,1,0:T(8,128)S(1)}, f32[19,8,256]{2,1,0:T(8,128)S(1)}, u32[]{:S(2)}, u32[]{:S(2)}) collective-permute-start(f32[19,8,256]{2,1,0:T(8,128)S(1)} %get-tuple-element.44), channel_id=1, source_target_pairs={{0,15},{1,2},{2,1},{3,4},{4,3},{5,6},{6,5},{7,8},{8,7},{9,10},{10,... | collective-permute-start | bytes 466952 | tf_op jit(solution)/shard_map/ppermute | solution.py:613
  16.5 7.6 %collective-permute-start.4 = (f32[19,8,256]{2,1,0:T(8,128)S(1)}, f32[19,8,256]{2,1,0:T(8,128)S(1)}, u32[]{:S(2)}, u32[]{:S(2)}) collective-permute-start(f32[19,8,256]{2,1,0:T(8,128)S(1)} %get-tuple-element.45), channel_id=1, source_target_pairs={{0,1},{1,0},{2,3},{3,2},{4,5},{5,4},{6,7},{7,6},{8,9},{9,8},{10,11... | collective-permute-start | bytes 466952 | tf_op jit(solution)/shard_map/ppermute | solution.py:613
  21.8 2.3 %copy-start = (f32[8,32,256]{2,1,0:T(8,128)S(1)}, f32[8,32,256]{2,1,0:T(8,128)}, u32[]{:S(2)}) copy-start(f32[8,32,256]{2,1,0:T(8,128)} %all_refs_14_.1) | copy-start | bytes 786436

commit v4 on v3

--- a/solution.py
+++ b/solution.py
@@ -350,35 +350,43 @@
 def still_plane(ts_at, km_at, p, fx_low, fx_high):
     k, t = km_at(p), ts_at(p)
     ext, ny = k.shape
-    ky = pltpu.roll(k, 1, 1)
-    kz = pltpu.roll(k, 1, 0)
-    gy, gz = face(k, ky), face(k, kz)
-    pore = jnp.where(k == 0.0, 1.0, 0.0)
-    count = jnp.where(ky == 0.0, 1.0, 0.0) + jnp.where(kz == 0.0, 1.0, 0.0)
-    count = count + pltpu.roll(pore, ny - 1, 1) + pltpu.roll(pore, ext - 1, 0)
-    count = count + jnp.where(km_at(p - 1) == 0.0, 1.0, 0.0) + jnp.where(km_at(p + 1) == 0.0, 1.0, 0.0)
-    flux_y = gy * (pltpu.roll(t, 1, 1) - t)
-    flux_z = gz * (pltpu.roll(t, 1, 0) - t)
-    net = fx_low * (ts_at(p - 1) - t) - fx_high * (t - ts_at(p + 1))
-    net = net + (flux_y - pltpu.roll(flux_y, ny - 1, 1))
-    net = net + (flux_z - pltpu.roll(flux_z, ext - 1, 0))
-    return gy, gz, net - FILM * count * t
-
-
-def static_body(tsm, km, theirs, fx, fy, fz, still):
+    k_low, k_high = pltpu.roll(k, 1, 1), pltpu.roll(k, ny - 1, 1)
+    count = jnp.where(k_low == 0.0, 1.0, 0.0) + jnp.where(k_high == 0.0, 1.0, 0.0)
+    y_low, y_high = face(k, k_low), face(k, k_high)
+    k_low, k_high = pltpu.roll(k, 1, 0), pltpu.roll(k, ext - 1, 0)
+    count = count + (jnp.where(k_low == 0.0, 1.0, 0.0) + jnp.where(k_high == 0.0, 1.0, 0.0))
+    z_low = face(k, k_low)
+    z_high = pltpu.roll(z_low, ext - 1, 0)
+    count = count + (jnp.where(km_at(p - 1) == 0.0, 1.0, 0.0) + jnp.where(km_at(p + 1) == 0.0, 1.0, 0.0))
+    total = (fx_low + fx_high) + (y_low + y_high) + (z_low + z_high)
+    near = spread(t, ts_at(p - 1), ts_at(p + 1), fx_low, fx_high, y_low, y_high, z_low, z_high)
+    return y_low, y_high, z_low, z_high, 1.0 + total, near - (FILM * count + total) * t
+
+
+def spread(v, below, above, fx_low, fx_high, y_low, y_high, z_low, z_high):
+    ext, ny = v.shape
+    in_y = y_low * pltpu.roll(v, 1, 1) + y_high * pltpu.roll(v, ny - 1, 1)
+    in_z = z_low * pltpu.roll(v, 1, 0) + z_high * pltpu.roll(v, ext - 1, 0)
+    return (fx_low * below + fx_high * above) + in_z + in_y
+
+
+def static_body(tsm, km, theirs, fx, *outs):
     nx = tsm.shape[0]
     ts_at, km_at = reader(nx, None, None, tsm, km, theirs)[:2]
     first = DEEP + 1
     for n in range(nx - 1):
         fx[n] = face(km_at(first + n), km_at(first + n - 1))
     for n in range(nx - 2):
-        fy[n], fz[n], still[n] = still_plane(ts_at, km_at, first + n, fx[n], fx[n + 1])
+        for out, v in zip(outs, still_plane(ts_at, km_at, first + n, fx[n], fx[n + 1])):
+            out[n] = v
 
 
 def conduct_body(*all_refs):
     early_cross, early_intra, late_cross, late_intra, theirs, joined, bounce = all_refs[0:7]
-    in_fx, in_fy, in_fz, in_still, tsm, km, hot, ts, corners, heat_in, pops_in, new_heat, new_pops, new_solid = all_refs[7:21]
-    temp, resid, step_a, step_b, fx, fy, fz, still, ends, patched, sems = all_refs[21:]
+    in_fx, in_still = all_refs[7], all_refs[8:14]
+    tsm, km, hot, ts, corners, heat_in, pops_in, new_heat, new_pops, new_solid = all_refs[14:24]
+    temp, resid, step_a, step_b, fx = all_refs[24:29]
+    still, (total, ends, patched, sems) = all_refs[29:35], all_refs[35:]
     nx, nz, ny = ts.shape
     planes, ext = temp.shape[:2]
     tiles = nz // TILE
@@ -392,14 +400,12 @@
     def fx_at(p):
         return in_fx[p - DEEP - 1] if DEEP < p < DEEP + nx else fx[p]
 
-    def fy_at(p):
-        return in_fy[p - DEEP - 1] if ready(p) else fy[p]
-
-    def fz_at(p):
-        return in_fz[p - DEEP - 1] if ready(p) else fz[p]
-
-    def still_at(p):
-        return in_still[p - DEEP - 1] if ready(p) else still[p]
+    def still_at(n, p):
+        return in_still[n][p - DEEP - 1] if ready(p) else still[n][p]
+
+    def apply(v, p, now):
+        near = spread(v, now[p - 1], now[p + 1], fx_at(p), fx_at(p + 1), *(still_at(n, p) for n in range(4)))
+        return near - still_at(4, p) * v
 
     def temp_at(p):
         return joined[p - DEEP] if DEEP <= p < DEEP + nx else temp_far(p)
@@ -453,39 +459,47 @@
             fx[p] = face(km_at(p), km_at(p - 1))
     for p in range(1, planes - 1):
         if not ready(p):
-            fy[p], fz[p], still[p] = still_plane(ts_at, km_at, p, fx_at(p), fx_at(p + 1))
-    for p in range(1, planes - 1):
+            for out, v in zip(still, still_plane(ts_at, km_at, p, fx_at(p), fx_at(p + 1))):
+                out[p] = v
+
+    def residual(p):
         mid = temp[p]
-        near = (temp[p - 1] + temp[p + 1]) + (pltpu.roll(mid, 1, 1) + pltpu.roll(mid, ny - 1, 1))
-        near = near + (pltpu.roll(mid, 1, 0) + pltpu.roll(mid, ext - 1, 0))
-        r = jnp.where(km_at(p) == 0.0, 0.0, FILM * near) + still_at(p)
-        resid[p] = r
-        s = r * (1.0 / THETA)
-        step_a[p] = s
-        if DEEP <= p < DEEP + nx:
-            new_solid[p - DEEP] = ts[p - DEEP] + s[own]
+        near = (temp[p - 1] + temp[p + 1]) + (pltpu.roll(mid, 1, 0) + pltpu.roll(mid, ext - 1, 0))
+        near = near + (pltpu.roll(mid, 1, 1) + pltpu.roll(mid, ny - 1, 1))
+        return jnp.where(km_at(p) == 0.0, 0.0, FILM * near) + still_at(5, p)
+
+    def pairs(start):
+        every = list(range(start, planes - start))
+        return [every[n : n + 2] for n in range(0, len(every), 2)]
+
+    for group in pairs(1):
+        for p, r in [(p, residual(p)) for p in group]:
+            resid[p] = r
+            s = r * (1.0 / THETA)
+            step_a[p] = s
+            if DEEP <= p < DEEP + nx:
+                total[p - DEEP] = ts[p - DEEP] + s[own]
     sigma = THETA / DELTA
     ratio = 1.0 / sigma
     now, later = step_a, step_b
     for sweep in range(1, ITERS):
         after = 1.0 / (2.0 * sigma - ratio)
-        start = 1 + sweep
-        below = fx_at(start) * (now[start - 1] - now[start])
-        for p in range(start, planes - start):
-            v = now[p]
-            flux_y = fy_at(p) * (pltpu.roll(v, 1, 1) - v)
-            flux_z = fz_at(p) * (pltpu.roll(v, 1, 0) - v)
-            above = fx_at(p + 1) * (v - now[p + 1])
-            net = (below - above) + (flux_y - pltpu.roll(flux_y, ny - 1, 1))
-            net = net + (flux_z - pltpu.roll(flux_z, ext - 1, 0))
-            below = above
-            r = resid[p] - (v - net)
-            s = (after * ratio) * v + (2.0 * after / DELTA) * r
-            if sweep + 1 < ITERS:
-                resid[p] = r
-                later[p] = s
-            if DEEP <= p < DEEP + nx:
-                new_solid[p - DEEP] = new_solid[p - DEEP] + s[own]
+        for group in pairs(1 + sweep):
+            done = []
+            for p in group:
+                v = now[p]
+                r = resid[p] + apply(v, p, now)
+                done.append((p, r, (after * ratio) * v + (2.0 * after / DELTA) * r))
+            for p, r, s in done:
+                if sweep + 1 < ITERS:
+                    resid[p] = r
+                    later[p] = s
+                if DEEP <= p < DEEP + nx:
+                    x = p - DEEP
+                    total[x] = total[x] + s[own]
+                    if sweep + 1 == ITERS:
+                        copies.append(pltpu.make_async_copy(total.at[x], new_solid.at[x], sems.at[6 + x]))
+                        copies[-1].start()
         ratio = after
         now, later = later, now
     for copy in copies:
@@ -553,15 +567,13 @@
 
     copies = []
     for at, x in enumerate(range(1, nx - 1) if part < 2 else (0, nx - 1)):
-        slot = at % 2
-        if at >= 2:
-            for copy in copies[at - 2]:
-                copy.wait()
+        slot = at
         for i in range(tiles):
             is_pore = tsm[x, span(i), :] == 0.0
+            done = []
             for at_d, d in enumerate(FLOW_DIRS[part]):
                 if d == 0:
-                    buf[slot, at_d, span(i), :] = flow[0, x, span(i), :]
+                    done.append(flow[0, x, span(i), :])
                     continue
                 cx, cy, cz = DIRS[d]
                 q = x - cx
@@ -572,9 +584,11 @@
                 if open_row:
                     both = both & (row != (0 if cz > 0 else TILE - 1))
                 v = jnp.where(both, v, jnp.where(is_pore, flow[OPP[d], x, span(i), :], flow[d, x, span(i), :]))
-                buf[slot, at_d, span(i), :] = v
+                done.append(v)
                 if open_row:
                     corners[(11, 13, 12, 14).index(d)] = v
+            for at_d, v in enumerate(done):
+                buf[slot, at_d, span(i), :] = v
         begin = 0
         copies.append([])
         for n, (d, count) in enumerate(FLOW_RUNS[part]):
@@ -588,7 +602,7 @@
             copy = pltpu.make_async_copy(heat_ends.at[n], heat_out.at[5 + n, :, rows, :], heat_sems.at[n])
             copy.start()
             copies[-1].append(copy)
-    for group in copies[-2:]:
+    for group in copies:
         for copy in group:
             copy.wait()
 
@@ -648,14 +662,14 @@
     early = along_x(*call(early_body, [early_shape] * 2, [km, flow, hot, bounce, temp]))
 
     def flow_call(part, outs, args, out_specs, in_hbm=0, extra=(), **rest):
-        held = (2, len(FLOW_DIRS[part]), nz, ny)
+        held = (2 if part == 2 else nx - 2, len(FLOW_DIRS[part]), nz, ny)
         return call(
             functools.partial(flow_body, part),
             outs,
             args,
             in_specs=[VM] * (len(args) - in_hbm) + [ANY] * in_hbm,
             out_specs=out_specs,
-            scratch=[pltpu.VMEM(held, jnp.float32), dma((4,)), *extra],
+            scratch=[pltpu.VMEM(held, jnp.float32), dma((2 * nx,)), *extra],
             limit=6 << 20,
             **rest,
         )
@@ -688,22 +702,22 @@
         in_hbm=1,
         aliases={7: 0},
     )
-    fx, fy, fz, still = call(
+    fixed = call(
         static_body,
-        [(nx - 1, ext, ny)] + [(nx - 2, ext, ny)] * 3,
+        [(nx - 1, ext, ny)] + [(nx - 2, ext, ny)] * 6,
         [tsm, km, theirs],
     )
     new_heat, new_pops, new_solid = call(
         conduct_body,
         [heat_shape, pops_shape, field],
-        [*early, *late, theirs, joined, bounce]
-        + [fx, fy, fz, still, tsm, km, hot, solid_temp, corners, new_heat, new_pops],
-        in_specs=[VM] * 16 + [ANY] * 2,
-        out_specs=[ANY, ANY, VM],
-        scratch=[pltpu.VMEM(wide, jnp.float32)] * 8
-        + [pltpu.VMEM((2, nz, ny), jnp.float32), pltpu.VMEM((4, TILE, ny), jnp.float32), dma((6,))],
-        aliases={16: 0, 17: 1},
-        limit=10 << 20,
+        [*early, *late, theirs, joined, bounce, *fixed, tsm, km, hot, solid_temp, corners, new_heat, new_pops],
+        in_specs=[VM] * 19 + [ANY] * 2,
+        out_specs=[ANY, ANY, ANY],
+        scratch=[pltpu.VMEM(wide, jnp.float32)] * 11
+        + [pltpu.VMEM(field, jnp.float32), pltpu.VMEM((2, nz, ny), jnp.float32), pltpu.VMEM((4, TILE, ny), jnp.float32)]
+        + [dma((6 + nx,))],
+        aliases={19: 0, 20: 1},
+        limit=12 << 20,
         us=4,
     )
     return new_pops, new_heat, new_solid

time: 29.4 us -> 27.7 us (0.942)
  Pallas kernels: 18.3 us -> 14.9 us
  starting transfers between devices: 9.23 us -> 10.4 us
  waiting for transfers between devices: 0.96 us -> 1.49 us
    pallas_call x9, Pallas kernels: 18.3 us -> 14.9 us  [call(): pl.pallas_call(body, out_shape=[jax.ShapeDtypeStruct(shape, jnp.float32)...]
    ppermute x2, starting transfers between devices: 3.43 us -> 4.64 us  [along_x(): lax.ppermute(cross, 'dev', across)]
    ppermute x2, waiting for transfers between devices: 0.95 us -> 1.48 us  [along_x(): lax.ppermute(cross, 'dev', across)]
  transfers between devices with their start and end apart: 6 -> 6, of which waited for: 1 -> 2; matrix products, arithmetic and copies ran while one was open for 0% -> 0% of each run, Pallas kernels for 28% -> 24%
where the time goes in v4:
time: 27.7 us; the launch traced here: 27.5 us
  Pallas kernels  14.9 us (54%)
  starting transfers between devices  10.4 us (38%)
  waiting for transfers between devices  1.49 us (5%)
  between operations  0.7 us (3%)
    pallas_call x9, Pallas kernels, call(): pl.pallas_call(body, out_shape=[jax.ShapeDtypeStruct(shape, jnp.float32)...  14.9 us
    ppermute x2, starting transfers between devices, along_x(): lax.ppermute(cross, 'dev', across)  4.64 us
    ppermute x2, starting transfers between devices, along_x(): lax.ppermute(intra, 'dev', [(i, i ^ 1) for i in range(count)])  3.61 us
    ppermute x2, starting transfers between devices, along_z(): return lax.ppermute(rows, 'grp', ring('grp', 1))  2.18 us
    ppermute x2, waiting for transfers between devices, along_x(): lax.ppermute(cross, 'dev', across)  1.48 us
  transfers between devices with their start and end apart: 6, of which 2 were waited for; matrix products, arithmetic and copies ran while one was open for 0% of the time, Pallas kernels for 24%

profile of v4, /device:TPU:1, one launch (start us, length us, event | category | flops | bytes accessed | tf_op | source)
XLA Modules:
  0.0 27.5 jit_solution(11556194980547070659)
XLA Ops:
  0.6 4.2 %shard_map.76 = (f32[19,8,32,256]{3,2,1,0:T(8,128)S(1)}, f32[7,8,32,256]{3,2,1,0:T(8,128)S(1)}, f32[8,32,256]{2,1,0:T(8,128)S(1)}, f32[8,32,256]{2,1,0:T(8,128)S(1)}, f32[8,8,256]{2,1,0:T(8,128)S(1)}) custom-call(f32[19,8,32,256]{3,2,1,0:T(8,128)} %refs_0_.1, f32[7,8,32,256]{3,2,1,0:T(8,128)} %refs_1_.1, f32[8,32,256]{2,1,0:T(8,128)} %all_refs_17_.1, ...), custom_call_target="tpu_custom_call" | custom-call | flops 4000000000 | bytes 12000000 | tf_op jit(solution)/shard_map/pallas_call | solution.py:56
  4.8 0.8 %shard_map.77 = (f32[7,8,32,256]{3,2,1,0:T(8,128)S(1)}, f32[8,32,256]{2,1,0:T(8,128)S(1)}, f32[2,32,256]{2,1,0:T(8,128)S(1)}, f32[28,8,256]{2,1,0:T(8,128)S(1)}, f32[8,8,256]{2,1,0:T(8,128)S(1)}) custom-call(f32[7,8,32,256]{3,2,1,0:T(8,128)S(1)} %get-tuple-element.37.hot.all_refs_16_, f32[19,8,32,256]{3,2,1,0:T(8,128)S(1)} %get-tuple-element.36.flow.all_refs_0_, ...), custom_call_target="tpu_custom_call" | custom-call | flops 500000000 | bytes 1500000 | tf_op jit(solution)/shard_map/pallas_call | solution.py:56
  5.6 2.1 %collective-permute-start.2 = (f32[28,8,256]{2,1,0:T(8,128)S(1)}, f32[28,8,256]{2,1,0:T(8,128)S(1)}, u32[]{:S(2)}, u32[]{:S(2)}) collective-permute-start(f32[28,8,256]{2,1,0:T(8,128)S(1)} %get-tuple-element.44.mine), channel_id=1, source_target_pairs={{0,16},{16,0},{1,17},{17,1},{2,18},{18,2},{3,19},{19,3},{4,20},{20... | collective-permute-start | bytes 688136 | tf_op jit(solution)/shard_map/ppermute | solution.py:617
  7.7 0.1 collective-permute-start.5
  7.8 0.1 shard_map.78
  7.8 2.6 %collective-permute-start = (f32[52,8,256]{2,1,0:T(8,128)S(1)}, f32[52,8,256]{2,1,0:T(8,128)S(1)}, u32[]{:S(2)}, u32[]{:S(2)}) collective-permute-start(f32[52,8,256]{2,1,0:T(8,128)S(1)} %get-tuple-element.42), channel_id=1, source_target_pairs={{0,15},{1,2},{2,1},{3,4},{4,3},{5,6},{6,5},{7,8},{8,7},{9,10},{10,... | collective-permute-start | bytes 1277960 | tf_op jit(solution)/shard_map/ppermute | solution.py:627
  10.4 2.3 %collective-permute-start.1 = (f32[52,8,256]{2,1,0:T(8,128)S(1)}, f32[52,8,256]{2,1,0:T(8,128)S(1)}, u32[]{:S(2)}, u32[]{:S(2)}) collective-permute-start(f32[52,8,256]{2,1,0:T(8,128)S(1)} %get-tuple-element.43), channel_id=1, source_target_pairs={{0,1},{1,0},{2,3},{3,2},{4,5},{5,4},{6,7},{7,6},{8,9},{9,8},{10,11... | collective-permute-start | bytes 1277960 | tf_op jit(solution)/shard_map/ppermute | solution.py:627
  12.7 1.6 %shard_map.79 = (f32[19,8,32,256]{3,2,1,0:T(8,128)}, f32[2,8,32,256]{3,2,1,0:T(8,128)S(1)}) custom-call(f32[19,8,32,256]{3,2,1,0:T(8,128)S(1)} %get-tuple-element.36.flow.all_refs_0_, f32[8,32,256]{2,1,0:T(8,128)S(1)} %get-tuple-element.38.tsm.all_refs_1_.all_refs_14_), custom_call_target="tpu_custom_call" | custom-call | flops 20000000000 | bytes 60000000 | tf_op jit(solution)/shard_map/pallas_call | solution.py:56
  14.3 0.0 collective-permute-done.2.theirs.all_refs_2_.all_refs_4_
  14.3 0.1 shard_map.80
  14.5 2.0 %collective-permute-start.3 = (f32[19,8,256]{2,1,0:T(8,128)S(1)}, f32[19,8,256]{2,1,0:T(8,128)S(1)}, u32[]{:S(2)}, u32[]{:S(2)}) collective-permute-start(f32[19,8,256]{2,1,0:T(8,128)S(1)} %get-tuple-element.47), channel_id=1, source_target_pairs={{0,15},{1,2},{2,1},{3,4},{4,3},{5,6},{6,5},{7,8},{8,7},{9,10},{10,... | collective-permute-start | bytes 466952 | tf_op jit(solution)/shard_map/ppermute | solution.py:627
  16.5 1.3 %collective-permute-start.4 = (f32[19,8,256]{2,1,0:T(8,128)S(1)}, f32[19,8,256]{2,1,0:T(8,128)S(1)}, u32[]{:S(2)}, u32[]{:S(2)}) collective-permute-start(f32[19,8,256]{2,1,0:T(8,128)S(1)} %get-tuple-element.48), channel_id=1, source_target_pairs={{0,1},{1,0},{2,3},{3,2},{4,5},{5,4},{6,7},{7,6},{8,9},{9,8},{10,11... | collective-permute-start | bytes 466952 | tf_op jit(solution)/shard_map/ppermute | solution.py:627
  17.8 0.0 collective-permute-done.5.all_refs_3_
  17.8 2.7 %shard_map.82 = (f32[19,8,32,256]{3,2,1,0:T(8,128)}, f32[7,8,32,256]{3,2,1,0:T(8,128)}) custom-call(f32[19,8,32,256]{3,2,1,0:T(8,128)S(1)} %get-tuple-element.36.flow.all_refs_0_, f32[8,32,256]{2,1,0:T(8,128)S(1)} %get-tuple-element.38.tsm.all_refs_1_.all_refs_14_, ...), custom_call_target="tpu_custom_call", output_to_operand_aliasing={{0}: (7, {})} | custom-call | flops 20000000000 | bytes 60000000 | tf_op jit(solution)/shard_map/pallas_call | solution.py:56
  20.5 0.7 %shard_map.81 = (f32[7,40,256]{2,1,0:T(8,128)S(1)}, f32[6,40,256]{2,1,0:T(8,128)S(1)}, f32[6,40,256]{2,1,0:T(8,128)S(1)}, f32[6,40,256]{2,1,0:T(8,128)S(1)}, f32...) custom-call(f32[8,32,256]{2,1,0:T(8,128)S(1)} %get-tuple-element.38.tsm.all_refs_1_.all_refs_14_, ...), custom_call_target="tpu_custom_call" | custom-call | flops 500000000 | bytes 1500000 | tf_op jit(solution)/shard_map/pallas_call | solution.py:56
  21.2 1.3 %collective-permute-done.all_refs_5_.all_refs_0_ = f32[52,8,256]{2,1,0:T(8,128)S(1)} collective-permute-done((f32[52,8,256]{2,1,0:T(8,128)S(1)}, f32[52,8,256]{2,1,0:T(8,128)S(1)}, u32[]{:S(2)}, u32[]{:S(2)}) %collective-permute-start) | collective-permute-done | bytes 426016 | tf_op jit(solution)/shard_map/ppermute | solution.py:627
  22.5 0.0 collective-permute-done.1.all_refs_6_.all_refs_1_
  22.5 0.0 copy-start
  22.5 1.5 %shard_map.83 = (f32[19,8,32,256]{3,2,1,0:T(8,128)}, f32[4,8,256]{2,1,0:T(8,128)S(1)}) custom-call(f32[19,8,32,256]{3,2,1,0:T(8,128)S(1)} %get-tuple-element.36.flow.all_refs_0_, f32[8,32,256]{2,1,0:T(8,128)S(1)} %get-tuple-element.38.tsm.all_refs_1_.all_refs_14_, ...), custom_call_target="tpu_custom_call", output_to_operand_aliasing={{0}: (7, {})} | custom-call | flops 500000000 | bytes 1500000 | tf_op jit(solution)/shard_map/pallas_call | solution.py:56
  24.0 0.2 collective-permute-done.3.all_refs_2_
  24.1 0.0 collective-permute-done.4.all_refs_3_
  24.2 0.0 copy-done
  24.2 3.4 %shard_map.84 = (f32[7,8,32,256]{3,2,1,0:T(8,128)}, f32[19,8,32,256]{3,2,1,0:T(8,128)}, f32[8,32,256]{2,1,0:T(8,128)}) custom-call(f32[52,8,256]{2,1,0:T(8,128)S(1)} %collective-permute-done.all_refs_5_.all_refs_0_, f32[52,8,256]{2,1,0:T(8,128)S(1)} %collective-permute-done.1.all_refs_6_.all_refs_1_, ...), custom_call_target="tpu_custom_call", output_to_operand_aliasing={{0}: (19, {}), {1}: (20, {})} | custom-call | flops 4000000000 | bytes 12000000 | tf_op jit(solution)/shard_map/pallas_call | solution.py:56
Async XLA Ops:
  5.6 8.8 %collective-permute-start.2 = (f32[28,8,256]{2,1,0:T(8,128)S(1)}, f32[28,8,256]{2,1,0:T(8,128)S(1)}, u32[]{:S(2)}, u32[]{:S(2)}) collective-permute-start(f32[28,8,256]{2,1,0:T(8,128)S(1)} %get-tuple-element.44.mine), channel_id=1, source_target_pairs={{0,16},{16,0},{1,17},{17,1},{2,18},{18,2},{3,19},{19,3},{4,20},{20... | collective-permute-start | bytes 688136 | tf_op jit(solution)/shard_map/ppermute | solution.py:617
  7.7 10.1 %collective-permute-start.5 = (f32[8,8,256]{2,1,0:T(8,128)S(1)}, f32[8,8,256]{2,1,0:T(8,128)S(1)}, u32[]{:S(2)}, u32[]{:S(2)}) collective-permute-start(f32[8,8,256]{2,1,0:T(8,128)S(1)} %get-tuple-element.57), channel_id=1, source_target_pairs={{0,16},{16,0},{1,17},{17,1},{2,18},{18,2},{3,19},{19,3},{4,20},{20... | collective-permute-start | bytes 196616 | tf_op jit(solution)/shard_map/ppermute | solution.py:617
  7.8 14.7 %collective-permute-start = (f32[52,8,256]{2,1,0:T(8,128)S(1)}, f32[52,8,256]{2,1,0:T(8,128)S(1)}, u32[]{:S(2)}, u32[]{:S(2)}) collective-permute-start(f32[52,8,256]{2,1,0:T(8,128)S(1)} %get-tuple-element.42), channel_id=1, source_target_pairs={{0,15},{1,2},{2,1},{3,4},{4,3},{5,6},{6,5},{7,8},{8,7},{9,10},{10,... | collective-permute-start | bytes 1277960 | tf_op jit(solution)/shard_map/ppermute | solution.py:627
  10.4 12.0 %collective-permute-start.1 = (f32[52,8,256]{2,1,0:T(8,128)S(1)}, f32[52,8,256]{2,1,0:T(8,128)S(1)}, u32[]{:S(2)}, u32[]{:S(2)}) collective-permute-start(f32[52,8,256]{2,1,0:T(8,128)S(1)} %get-tuple-element.43), channel_id=1, source_target_pairs={{0,1},{1,0},{2,3},{3,2},{4,5},{5,4},{6,7},{7,6},{8,9},{9,8},{10,11... | collective-permute-start | bytes 1277960 | tf_op jit(solution)/shard_map/ppermute | solution.py:627
  14.5 9.7 %collective-permute-start.3 = (f32[19,8,256]{2,1,0:T(8,128)S(1)}, f32[19,8,256]{2,1,0:T(8,128)S(1)}, u32[]{:S(2)}, u32[]{:S(2)}) collective-permute-start(f32[19,8,256]{2,1,0:T(8,128)S(1)} %get-tuple-element.47), channel_id=1, source_target_pairs={{0,15},{1,2},{2,1},{3,4},{4,3},{5,6},{6,5},{7,8},{8,7},{9,10},{10,... | collective-permute-start | bytes 466952 | tf_op jit(solution)/shard_map/ppermute | solution.py:627
  16.5 7.6 %collective-permute-start.4 = (f32[19,8,256]{2,1,0:T(8,128)S(1)}, f32[19,8,256]{2,1,0:T(8,128)S(1)}, u32[]{:S(2)}, u32[]{:S(2)}) collective-permute-start(f32[19,8,256]{2,1,0:T(8,128)S(1)} %get-tuple-element.48), channel_id=1, source_target_pairs={{0,1},{1,0},{2,3},{3,2},{4,5},{5,4},{6,7},{7,6},{8,9},{9,8},{10,11... | collective-permute-start | bytes 466952 | tf_op jit(solution)/shard_map/ppermute | solution.py:627
  22.5 1.7 %copy-start = (f32[8,32,256]{2,1,0:T(8,128)S(1)}, f32[8,32,256]{2,1,0:T(8,128)}, u32[]{:S(2)}) copy-start(f32[8,32,256]{2,1,0:T(8,128)} %all_refs_17_.1) | copy-start | bytes 786436

commit v5 on v4

--- a/solution.py
+++ b/solution.py
@@ -45,6 +45,7 @@
 WALL_OWN = 0.25 * JUMP
 WALL_NEAR = 0.25 * (1.0 - JUMP)
 DEEP = 4
+HALO = DEEP - 1
 TILE = 8
 
 VM = pl.BlockSpec(memory_space=pltpu.VMEM)
@@ -238,26 +239,38 @@
     return pick
 
 
+def face(a, b):
+    return (2.0 * a) * b / jnp.maximum(a + b, 1.0)
+
+
+def beyond(k, k_far, temp, temp_far):
+    rate = jnp.where(k_far == 0.0, FILM, face(k, k_far))
+    return jnp.where(k == 0.0, 0.0, rate * (temp_far - temp))
+
+
 def early_body(km, flow, hot, bounce, temp, cross, intra):
     nx, nz = km.shape[:2]
 
     def fill(low, high):
         for side, out in ((0, low), (1, high)):
             n = 0
-            deep = range(side * (nx - DEEP), side * (nx - DEEP) + DEEP)
+            deep = range(side * (nx - HALO), side * (nx - HALO) + HALO)
             for x in deep:
                 n = put_plane(out, n, km[x])
             for d in (XLOW, XHIGH)[side]:
                 n = put_plane(out, n, flow[d, side * (nx - 1)])
             n = put_plane(out, n, hot[2 - side, side * (nx - 1)])
             n = put_plane(out, n, bounce[side])
+            middle = slice(TILE, nz - TILE)
             for x in deep:
-                n = put_plane(out, n, temp[x, TILE : nz - TILE, :])
+                n = put_plane(out, n, temp[x, middle, :])
+            x, far = (HALO - 1, HALO) if side == 0 else (nx - HALO, nx - DEEP)
+            put_plane(out, n, beyond(km[x, middle, :], km[far, middle, :], temp[x, middle, :], temp[far, middle, :]))
 
     by_side(cross, intra, fill)
 
 
-def zjoin_body(mine, theirs, temp, heat_in, after, heat_ends, joined, cross, intra):
+def zjoin_body(mine, theirs, temp, km, heat_in, after, heat_ends, joined, cross, intra):
     nx, nz, ny = temp.shape
     row = rows8((TILE, ny))
     edge = (row == 0) | (row == TILE - 1)
@@ -289,30 +302,34 @@
 
     def fill(low, high):
         for side, out in ((0, low), (1, high)):
-            for n in range(DEEP):
-                v = joined.at[side * (nx - DEEP) + n]
+            for n in range(HALO):
+                v = joined.at[side * (nx - HALO) + n]
                 out[3 * n] = v[first, :]
                 out[3 * n + 1] = v[last, :]
                 out[3 * n + 2] = v[nz : nz + TILE, :]
-            n = 3 * DEEP
+            x, far = (HALO - 1, HALO) if side == 0 else (nx - HALO, nx - DEEP)
+            n = 3 * HALO
+            for rows in (first, last):
+                out[n] = beyond(km[x, rows, :], km[far, rows, :], joined[x, rows, :], joined[far, rows, :])
+                n += 1
             out[n] = theirs[2 * nx + side]
             out[n + 1] = theirs[2 * nx + 2 + side]
             v = theirs[nx + side * (nx - 1)]
             lower, upper = (5, 2) if side else (6, 3)
             out[n + 2] = jnp.where(row < DEEP, pltpu.roll(v, lower, 0), pltpu.roll(v, upper, 0))
-            base = 2 * nx + 4 + side * (nx - DEEP)
-            out[n + 3 : n + 3 + DEEP] = theirs[base : base + DEEP]
+            base = 2 * nx + 4 + side * (nx - HALO)
+            out[n + 3 : n + 3 + HALO] = theirs[base : base + HALO]
 
     by_side(cross, intra, fill)
 
 
 def reader(nx, early, late, tsm, km, rows):
     tiles = km.shape[1] // TILE
-    ahead = (DEEP + len(XLOW)) * tiles
-    corner = 3 * DEEP + 3
+    ahead = (HALO + len(XLOW)) * tiles
+    corner = 3 * HALO + 5
 
     def away(p):
-        return (0, p) if p < DEEP else (1, p - DEEP - nx)
+        return (0, p - 1) if p < DEEP else (1, p - DEEP - nx)
 
     def km_halo(p):
         if DEEP <= p < DEEP + nx:
@@ -341,10 +358,6 @@
         return jnp.where(km_at(p) == 0.0, 0.0, temp_far(p))
 
     return ts_at, km_at, km_halo, temp_far, ahead
-
-
-def face(a, b):
-    return (2.0 * a) * b / jnp.maximum(a + b, 1.0)
 
 
 def still_plane(ts_at, km_at, p, fx_low, fx_high):
@@ -357,17 +370,25 @@
     count = count + (jnp.where(k_low == 0.0, 1.0, 0.0) + jnp.where(k_high == 0.0, 1.0, 0.0))
     z_low = face(k, k_low)
     z_high = pltpu.roll(z_low, ext - 1, 0)
-    count = count + (jnp.where(km_at(p - 1) == 0.0, 1.0, 0.0) + jnp.where(km_at(p + 1) == 0.0, 1.0, 0.0))
-    total = (fx_low + fx_high) + (y_low + y_high) + (z_low + z_high)
-    near = spread(t, ts_at(p - 1), ts_at(p + 1), fx_low, fx_high, y_low, y_high, z_low, z_high)
+    total = (y_low + y_high) + (z_low + z_high)
+    near = spread_in_plane(t, y_low, y_high, z_low, z_high)
+    for fx, q in ((fx_low, p - 1), (fx_high, p + 1)):
+        if fx is not None:
+            count = count + jnp.where(km_at(q) == 0.0, 1.0, 0.0)
+            total = total + fx
+            near = near + fx * ts_at(q)
     return y_low, y_high, z_low, z_high, 1.0 + total, near - (FILM * count + total) * t
 
 
-def spread(v, below, above, fx_low, fx_high, y_low, y_high, z_low, z_high):
+def spread_in_plane(v, y_low, y_high, z_low, z_high):
     ext, ny = v.shape
     in_y = y_low * pltpu.roll(v, 1, 1) + y_high * pltpu.roll(v, ny - 1, 1)
     in_z = z_low * pltpu.roll(v, 1, 0) + z_high * pltpu.roll(v, ext - 1, 0)
-    return (fx_low * below + fx_high * above) + in_z + in_y
+    return in_z + in_y
+
+
+def spread(v, below, above, fx_low, fx_high, *faces):
+    return (fx_low * below + fx_high * above) + spread_in_plane(v, *faces)
 
 
 def static_body(tsm, km, theirs, fx, *outs):
@@ -398,6 +419,8 @@
         return DEEP < p < DEEP + nx - 1
 
     def fx_at(p):
+        if p in (1, planes - 1):
+            return None
         return in_fx[p - DEEP - 1] if DEEP < p < DEEP + nx else fx[p]
 
     def still_at(n, p):
@@ -411,7 +434,7 @@
         return joined[p - DEEP] if DEEP <= p < DEEP + nx else temp_far(p)
 
     def sent(n, side):
-        return jnp.concatenate([early(side, ahead + n * tiles, tiles), late(side, 3 * DEEP + n, 1)], axis=0)
+        return jnp.concatenate([early(side, ahead + n * tiles, tiles), late(side, 3 * HALO + 2 + n, 1)], axis=0)
 
     def mine(n, side):
         end = (hot[2 - side, side * (nx - 1)], bounce[side])[n]
@@ -428,7 +451,7 @@
         return got
 
     row = rows8((TILE, ny))
-    corner = 3 * DEEP + 2
+    corner = 3 * HALO + 4
     copies = []
     for n, (d, x, p, side) in enumerate(
         (
@@ -444,7 +467,7 @@
         patched[n] = jnp.where(both, pltpu.roll(late(side, corner, 1), by, 0), corners[n])
         copies.append(pltpu.make_async_copy(patched.at[n], new_pops.at[d, x, rows, :], sems.at[n]))
         copies[-1].start()
-    for p in range(planes):
+    for p in range(1, planes - 1):
         if p not in (DEEP - 1, DEEP, DEEP + nx - 1, DEEP + nx):
             temp[p] = jnp.where(km_at(p) == 0.0, temp_at(p), 0.0)
     up, down = join(0), join(1)
@@ -454,7 +477,7 @@
         copies.append(pltpu.make_async_copy(ends.at[n], new_heat.at[d, x], sems.at[4 + n]))
         copies[-1].start()
 
-    for p in range(1, planes):
+    for p in range(2, planes - 1):
         if not DEEP < p < DEEP + nx:
             fx[p] = face(km_at(p), km_at(p - 1))
     for p in range(1, planes - 1):
@@ -464,9 +487,19 @@
 
     def residual(p):
         mid = temp[p]
-        near = (temp[p - 1] + temp[p + 1]) + (pltpu.roll(mid, 1, 0) + pltpu.roll(mid, ext - 1, 0))
+        near = pltpu.roll(mid, 1, 0) + pltpu.roll(mid, ext - 1, 0)
+        for q in (p - 1, p + 1):
+            if 0 < q < planes - 1:
+                near = near + temp[q]
         near = near + (pltpu.roll(mid, 1, 1) + pltpu.roll(mid, ny - 1, 1))
-        return jnp.where(km_at(p) == 0.0, 0.0, FILM * near) + still_at(5, p)
+        r = jnp.where(km_at(p) == 0.0, 0.0, FILM * near) + still_at(5, p)
+        if p in (1, planes - 2):
+            side = int(p > 1)
+            middle = early(side, ahead + (2 * tiles) + HALO * (tiles - 2), tiles - 2)
+            ends_of = late(side, 3 * HALO, 2)
+            open_rows = jnp.zeros((TILE, ny), jnp.float32)
+            r = r + jnp.concatenate([ends_of[0:TILE], middle, ends_of[TILE:], open_rows], axis=0)
+        return r
 
     def pairs(start):
         every = list(range(start, planes - start))
@@ -548,7 +581,7 @@
 
     def mask_tile(q, cy, i):
         if not 0 <= q < nx:
-            return turn(early(int(q > 0), (0 if q > 0 else DEEP - 1) * tiles + i % tiles, 1), cy)
+            return turn(early(int(q > 0), (0 if q > 0 else HALO - 1) * tiles + i % tiles, 1), cy)
         if not 0 <= i < tiles:
             return turn(theirs[2 * nx + 4 + q], cy)
         if cy:
@@ -563,7 +596,7 @@
             by = ZSLOT[d] if DIRS[d][2] > 0 else TILE - ZSLOT[d]
             return pltpu.roll(v, by % TILE, 0) if by % TILE else v
         side, n = (0, XHIGH.index(d)) if q < 0 else (1, XLOW.index(d))
-        return early(side, (DEEP + n) * tiles + i % tiles, 1)
+        return early(side, (HALO + n) * tiles + i % tiles, 1)
 
     copies = []
     for at, x in enumerate(range(1, nx - 1) if part < 2 else (0, nx - 1)):
@@ -658,7 +691,7 @@
     )
     theirs = along_z(zmsg)
     flow_rows = along_z(zflow)
-    early_shape = ((DEEP + len(XLOW) + 2) * (tiles - 1) + DEEP * (tiles - 3), TILE, ny)
+    early_shape = ((HALO + len(XLOW) + 2) * (tiles - 1) + DEEP * (tiles - 3), TILE, ny)
     early = along_x(*call(early_body, [early_shape] * 2, [km, flow, hot, bounce, temp]))
 
     def flow_call(part, outs, args, out_specs, in_hbm=0, extra=(), **rest):
@@ -676,11 +709,11 @@
 
     pops_shape, heat_shape = (19, *field), (7, *field)
     new_pops, turned = flow_call(0, [pops_shape, (2, *field)], [flow, tsm], [ANY, VM], us=20)
-    late_shape = (4 * DEEP + 3, TILE, ny)
+    late_shape = (4 * HALO + 5, TILE, ny)
     heat_ends, joined, cross, intra = call(
         zjoin_body,
         [(2, nx, TILE, ny), (nx, ext, ny), late_shape, late_shape],
-        [zmsg, theirs, temp, new_heat, turned],
+        [zmsg, theirs, temp, km, new_heat, turned],
         us=50,
     )
     late = along_x(cross, intra)

time: 27.7 us -> 26.6 us (0.960)
  waiting for transfers between devices: 1.49 us -> 0.4 us
    ppermute x2, waiting for transfers between devices: 1.48 us -> 0.39 us  [along_x(): lax.ppermute(cross, 'dev', across)]
  transfers between devices with their start and end apart: 6 -> 6, of which waited for: 2 -> 1; matrix products, arithmetic and copies ran while one was open for 0% -> 0% of each run, Pallas kernels for 24% -> 25%
where the time goes in v5:
time: 26.6 us; the launch traced here: 26.4 us
  Pallas kernels  14.9 us (56%)
  starting transfers between devices  10.4 us (39%)
  between operations  0.72 us (3%)
  waiting for transfers between devices  0.4 us (2%)
    pallas_call x9, Pallas kernels, call(): pl.pallas_call(body, out_shape=[jax.ShapeDtypeStruct(shape, jnp.float32)...  14.9 us
    ppermute x2, starting transfers between devices, along_x(): lax.ppermute(cross, 'dev', across)  4.64 us
    ppermute x2, starting transfers between devices, along_x(): lax.ppermute(intra, 'dev', [(i, i ^ 1) for i in range(count)])  3.61 us
    ppermute x2, starting transfers between devices, along_z(): return lax.ppermute(rows, 'grp', ring('grp', 1))  2.18 us
  transfers between devices with their start and end apart: 6, of which 1 were waited for; matrix products, arithmetic and copies ran while one was open for 0% of the time, Pallas kernels for 25%

profile of v5, /device:TPU:1, one launch (start us, length us, event | category | flops | bytes accessed | tf_op | source)
XLA Modules:
  0.0 26.4 jit_solution(2852911510804910759)
XLA Ops:
  0.6 4.2 %shard_map.76 = (f32[19,8,32,256]{3,2,1,0:T(8,128)S(1)}, f32[7,8,32,256]{3,2,1,0:T(8,128)S(1)}, f32[8,32,256]{2,1,0:T(8,128)S(1)}, f32[8,32,256]{2,1,0:T(8,128)S(1)}, f32[8,8,256]{2,1,0:T(8,128)S(1)}) custom-call(f32[19,8,32,256]{3,2,1,0:T(8,128)} %refs_0_.1, f32[7,8,32,256]{3,2,1,0:T(8,128)} %refs_1_.1, f32[8,32,256]{2,1,0:T(8,128)} %all_refs_17_.1, ...), custom_call_target="tpu_custom_call" | custom-call | flops 4000000000 | bytes 12000000 | tf_op jit(solution)/shard_map/pallas_call | solution.py:57
  4.8 0.8 %shard_map.77 = (f32[7,8,32,256]{3,2,1,0:T(8,128)S(1)}, f32[8,32,256]{2,1,0:T(8,128)S(1)}, f32[2,32,256]{2,1,0:T(8,128)S(1)}, f32[28,8,256]{2,1,0:T(8,128)S(1)}, f32[8,8,256]{2,1,0:T(8,128)S(1)}) custom-call(f32[7,8,32,256]{3,2,1,0:T(8,128)S(1)} %get-tuple-element.37.hot.all_refs_16_, f32[19,8,32,256]{3,2,1,0:T(8,128)S(1)} %get-tuple-element.36.flow.all_refs_0_, ...), custom_call_target="tpu_custom_call" | custom-call | flops 500000000 | bytes 1500000 | tf_op jit(solution)/shard_map/pallas_call | solution.py:57
  5.6 2.1 %collective-permute-start.2 = (f32[28,8,256]{2,1,0:T(8,128)S(1)}, f32[28,8,256]{2,1,0:T(8,128)S(1)}, u32[]{:S(2)}, u32[]{:S(2)}) collective-permute-start(f32[28,8,256]{2,1,0:T(8,128)S(1)} %get-tuple-element.44.mine), channel_id=1, source_target_pairs={{0,16},{16,0},{1,17},{17,1},{2,18},{18,2},{3,19},{19,3},{4,20},{20... | collective-permute-start | bytes 688136 | tf_op jit(solution)/shard_map/ppermute | solution.py:650
  7.7 0.1 collective-permute-start.5
  7.8 0.1 shard_map.78
  7.8 2.6 %collective-permute-start = (f32[48,8,256]{2,1,0:T(8,128)S(1)}, f32[48,8,256]{2,1,0:T(8,128)S(1)}, u32[]{:S(2)}, u32[]{:S(2)}) collective-permute-start(f32[48,8,256]{2,1,0:T(8,128)S(1)} %get-tuple-element.42), channel_id=1, source_target_pairs={{0,15},{1,2},{2,1},{3,4},{4,3},{5,6},{6,5},{7,8},{8,7},{9,10},{10,... | collective-permute-start | bytes 1179656 | tf_op jit(solution)/shard_map/ppermute | solution.py:660
  10.4 2.3 %collective-permute-start.1 = (f32[48,8,256]{2,1,0:T(8,128)S(1)}, f32[48,8,256]{2,1,0:T(8,128)S(1)}, u32[]{:S(2)}, u32[]{:S(2)}) collective-permute-start(f32[48,8,256]{2,1,0:T(8,128)S(1)} %get-tuple-element.43), channel_id=1, source_target_pairs={{0,1},{1,0},{2,3},{3,2},{4,5},{5,4},{6,7},{7,6},{8,9},{9,8},{10,11... | collective-permute-start | bytes 1179656 | tf_op jit(solution)/shard_map/ppermute | solution.py:660
  12.7 1.6 %shard_map.79 = (f32[19,8,32,256]{3,2,1,0:T(8,128)}, f32[2,8,32,256]{3,2,1,0:T(8,128)S(1)}) custom-call(f32[19,8,32,256]{3,2,1,0:T(8,128)S(1)} %get-tuple-element.36.flow.all_refs_0_, f32[8,32,256]{2,1,0:T(8,128)S(1)} %get-tuple-element.38.tsm.all_refs_1_.all_refs_14_), custom_call_target="tpu_custom_call" | custom-call | flops 20000000000 | bytes 60000000 | tf_op jit(solution)/shard_map/pallas_call | solution.py:57
  14.3 0.0 collective-permute-done.2.theirs.all_refs_2_.all_refs_4_
  14.4 0.1 shard_map.80
  14.5 2.0 %collective-permute-start.3 = (f32[17,8,256]{2,1,0:T(8,128)S(1)}, f32[17,8,256]{2,1,0:T(8,128)S(1)}, u32[]{:S(2)}, u32[]{:S(2)}) collective-permute-start(f32[17,8,256]{2,1,0:T(8,128)S(1)} %get-tuple-element.47), channel_id=1, source_target_pairs={{0,15},{1,2},{2,1},{3,4},{4,3},{5,6},{6,5},{7,8},{8,7},{9,10},{10,... | collective-permute-start | bytes 417800 | tf_op jit(solution)/shard_map/ppermute | solution.py:660
  16.5 1.3 %collective-permute-start.4 = (f32[17,8,256]{2,1,0:T(8,128)S(1)}, f32[17,8,256]{2,1,0:T(8,128)S(1)}, u32[]{:S(2)}, u32[]{:S(2)}) collective-permute-start(f32[17,8,256]{2,1,0:T(8,128)S(1)} %get-tuple-element.48), channel_id=1, source_target_pairs={{0,1},{1,0},{2,3},{3,2},{4,5},{5,4},{6,7},{7,6},{8,9},{9,8},{10,11... | collective-permute-start | bytes 417800 | tf_op jit(solution)/shard_map/ppermute | solution.py:660
  17.8 0.0 collective-permute-done.5.all_refs_3_
  17.8 2.7 %shard_map.82 = (f32[19,8,32,256]{3,2,1,0:T(8,128)}, f32[7,8,32,256]{3,2,1,0:T(8,128)}) custom-call(f32[19,8,32,256]{3,2,1,0:T(8,128)S(1)} %get-tuple-element.36.flow.all_refs_0_, f32[8,32,256]{2,1,0:T(8,128)S(1)} %get-tuple-element.38.tsm.all_refs_1_.all_refs_14_, ...), custom_call_target="tpu_custom_call", output_to_operand_aliasing={{0}: (7, {})} | custom-call | flops 20000000000 | bytes 60000000 | tf_op jit(solution)/shard_map/pallas_call | solution.py:57
  20.5 0.7 %shard_map.81 = (f32[7,40,256]{2,1,0:T(8,128)S(1)}, f32[6,40,256]{2,1,0:T(8,128)S(1)}, f32[6,40,256]{2,1,0:T(8,128)S(1)}, f32[6,40,256]{2,1,0:T(8,128)S(1)}, f32...) custom-call(f32[8,32,256]{2,1,0:T(8,128)S(1)} %get-tuple-element.38.tsm.all_refs_1_.all_refs_14_, ...), custom_call_target="tpu_custom_call" | custom-call | flops 500000000 | bytes 1500000 | tf_op jit(solution)/shard_map/pallas_call | solution.py:57
  21.2 0.0 collective-permute-done.all_refs_5_.all_refs_0_
  21.2 0.0 collective-permute-done.1.all_refs_6_.all_refs_1_
  21.2 0.0 copy-start
  21.2 1.5 %shard_map.83 = (f32[19,8,32,256]{3,2,1,0:T(8,128)}, f32[4,8,256]{2,1,0:T(8,128)S(1)}) custom-call(f32[19,8,32,256]{3,2,1,0:T(8,128)S(1)} %get-tuple-element.36.flow.all_refs_0_, f32[8,32,256]{2,1,0:T(8,128)S(1)} %get-tuple-element.38.tsm.all_refs_1_.all_refs_14_, ...), custom_call_target="tpu_custom_call", output_to_operand_aliasing={{0}: (7, {})} | custom-call | flops 500000000 | bytes 1500000 | tf_op jit(solution)/shard_map/pallas_call | solution.py:57
  22.7 0.4 %collective-permute-done.3.all_refs_2_ = f32[17,8,256]{2,1,0:T(8,128)S(1)} collective-permute-done((f32[17,8,256]{2,1,0:T(8,128)S(1)}, f32[17,8,256]{2,1,0:T(8,128)S(1)}, u32[]{:S(2)}, u32[]{:S(2)}) %collective-permute-start.3) | collective-permute-done | bytes 139296 | tf_op jit(solution)/shard_map/ppermute | solution.py:660
  23.1 0.0 collective-permute-done.4.all_refs_3_
  23.1 0.0 copy-done
  23.1 3.3 %shard_map.84 = (f32[7,8,32,256]{3,2,1,0:T(8,128)}, f32[19,8,32,256]{3,2,1,0:T(8,128)}, f32[8,32,256]{2,1,0:T(8,128)}) custom-call(f32[48,8,256]{2,1,0:T(8,128)S(1)} %collective-permute-done.all_refs_5_.all_refs_0_, f32[48,8,256]{2,1,0:T(8,128)S(1)} %collective-permute-done.1.all_refs_6_.all_refs_1_, ...), custom_call_target="tpu_custom_call", output_to_operand_aliasing={{0}: (19, {}), {1}: (20, {})} | custom-call | flops 4000000000 | bytes 12000000 | tf_op jit(solution)/shard_map/pallas_call | solution.py:57
Async XLA Ops:
  5.6 8.8 %collective-permute-start.2 = (f32[28,8,256]{2,1,0:T(8,128)S(1)}, f32[28,8,256]{2,1,0:T(8,128)S(1)}, u32[]{:S(2)}, u32[]{:S(2)}) collective-permute-start(f32[28,8,256]{2,1,0:T(8,128)S(1)} %get-tuple-element.44.mine), channel_id=1, source_target_pairs={{0,16},{16,0},{1,17},{17,1},{2,18},{18,2},{3,19},{19,3},{4,20},{20... | collective-permute-start | bytes 688136 | tf_op jit(solution)/shard_map/ppermute | solution.py:650
  7.7 10.1 %collective-permute-start.5 = (f32[8,8,256]{2,1,0:T(8,128)S(1)}, f32[8,8,256]{2,1,0:T(8,128)S(1)}, u32[]{:S(2)}, u32[]{:S(2)}) collective-permute-start(f32[8,8,256]{2,1,0:T(8,128)S(1)} %get-tuple-element.57), channel_id=1, source_target_pairs={{0,16},{16,0},{1,17},{17,1},{2,18},{18,2},{3,19},{19,3},{4,20},{20... | collective-permute-start | bytes 196616 | tf_op jit(solution)/shard_map/ppermute | solution.py:650
  7.8 13.4 %collective-permute-start = (f32[48,8,256]{2,1,0:T(8,128)S(1)}, f32[48,8,256]{2,1,0:T(8,128)S(1)}, u32[]{:S(2)}, u32[]{:S(2)}) collective-permute-start(f32[48,8,256]{2,1,0:T(8,128)S(1)} %get-tuple-element.42), channel_id=1, source_target_pairs={{0,15},{1,2},{2,1},{3,4},{4,3},{5,6},{6,5},{7,8},{8,7},{9,10},{10,... | collective-permute-start | bytes 1179656 | tf_op jit(solution)/shard_map/ppermute | solution.py:660
  10.4 10.8 %collective-permute-start.1 = (f32[48,8,256]{2,1,0:T(8,128)S(1)}, f32[48,8,256]{2,1,0:T(8,128)S(1)}, u32[]{:S(2)}, u32[]{:S(2)}) collective-permute-start(f32[48,8,256]{2,1,0:T(8,128)S(1)} %get-tuple-element.43), channel_id=1, source_target_pairs={{0,1},{1,0},{2,3},{3,2},{4,5},{5,4},{6,7},{7,6},{8,9},{9,8},{10,11... | collective-permute-start | bytes 1179656 | tf_op jit(solution)/shard_map/ppermute | solution.py:660
  14.5 8.6 %collective-permute-start.3 = (f32[17,8,256]{2,1,0:T(8,128)S(1)}, f32[17,8,256]{2,1,0:T(8,128)S(1)}, u32[]{:S(2)}, u32[]{:S(2)}) collective-permute-start(f32[17,8,256]{2,1,0:T(8,128)S(1)} %get-tuple-element.47), channel_id=1, source_target_pairs={{0,15},{1,2},{2,1},{3,4},{4,3},{5,6},{6,5},{7,8},{8,7},{9,10},{10,... | collective-permute-start | bytes 417800 | tf_op jit(solution)/shard_map/ppermute | solution.py:660
  16.5 6.6 %collective-permute-start.4 = (f32[17,8,256]{2,1,0:T(8,128)S(1)}, f32[17,8,256]{2,1,0:T(8,128)S(1)}, u32[]{:S(2)}, u32[]{:S(2)}) collective-permute-start(f32[17,8,256]{2,1,0:T(8,128)S(1)} %get-tuple-element.48), channel_id=1, source_target_pairs={{0,1},{1,0},{2,3},{3,2},{4,5},{5,4},{6,7},{7,6},{8,9},{9,8},{10,11... | collective-permute-start | bytes 417800 | tf_op jit(solution)/shard_map/ppermute | solution.py:660
  21.2 1.9 %copy-start = (f32[8,32,256]{2,1,0:T(8,128)S(1)}, f32[8,32,256]{2,1,0:T(8,128)}, u32[]{:S(2)}) copy-start(f32[8,32,256]{2,1,0:T(8,128)} %all_refs_17_.1) | copy-start | bytes 786436
